TPU v7x, 512 devices: a whole 4x4x16 slice. The times are simulated.
512 devices in a mesh: stn: 64 (over z, x_hi, core), tm: 8 (over x_lo, y).
Axes of the slice: x: 4 (x_hi: 2, x_lo: 2; x = x_hi * 2 + x_lo), y: 4, z: 16, core: 2. Of those that a mesh axis runs over, the one named last changes fastest.
Arguments:
- samples: bfloat16 [2, 512, 491520], P(None, 'stn', 'tm'), may hold values from -6 to 6
- taps: bfloat16 [16, 4096], replicated, may hold values from -1.5 to 1.5
- scales: int32 [512, 2048], P('stn'), may hold values from 1 to 8
Outputs:
- visibilities: bfloat16 [2048, 512, 512], P(('stn', 'tm'))
Inputs may be any that keep to these rules, and one draw needn't show every extreme that they name: scales are whole numbers.
All inputs are finite; a program needn't handle non-finite values.
Results may differ from a plain program's by a relative error of at most 0.0041.
Values may be sent and summed in bfloat16 or wider, within the bound.
No kernel may reach another device: no remote copies, remote signals or barrier semaphores. Data moves between devices by JAX's collectives and lax.ppermute only.
A program may use at most 128 MiB of HBM per device.

v0:
```python
import math

import jax
import jax.numpy as jnp
from jax import lax
from jax.sharding import PartitionSpec as P


def from_behind(block, axis, distance):
    devices = range(lax.axis_size(axis))
    route = [(i - distance, i) for i in devices if i - distance in devices]
    return lax.ppermute(block, axis, route)


def cos_sin(row_index, col_index, modulus):
    product = row_index[:, None] * col_index[None, :] % modulus
    angles = product.astype(jnp.float32) * (2.0 * math.pi / modulus)
    return (jnp.cos(angles), jnp.sin(angles))


def factor_length(length):
    outer_size = 1
    for divisor in range(1, math.isqrt(length) + 1):
        if length % divisor == 0:
            outer_size = divisor
    return outer_size


def rotation_table(cosine, sine):
    return jnp.stack([jnp.stack([cosine, -sine]), jnp.stack([sine, cosine])])


def band_transform(filtered, band_size):
    length = filtered.shape[2]
    outer_size = factor_length(length)
    inner_size = length // outer_size
    highest = lax.Precision.HIGHEST
    first = filtered.reshape(2, -1, outer_size, inner_size)
    outer_index = jnp.arange(outer_size, dtype=jnp.int32)
    inner_index = jnp.arange(inner_size, dtype=jnp.int32)
    cos_outer, sin_outer = cos_sin(outer_index, outer_index, outer_size)
    mixed = jnp.einsum(
        "crnq,cdnk->drkq",
        first,
        rotation_table(cos_outer, sin_outer),
        precision=highest,
        preferred_element_type=jnp.float32,
    )
    cos_twist, sin_twist = cos_sin(outer_index, inner_index, length)
    twisted_real = mixed[0] * cos_twist + mixed[1] * sin_twist
    twisted_imag = mixed[1] * cos_twist - mixed[0] * sin_twist
    twisted = jnp.stack([twisted_real, twisted_imag])
    offset = (length - band_size) // 2
    low_col = offset // outer_size
    high_col = -(-(offset + band_size) // outer_size)
    kept = high_col - low_col
    cos_inner, sin_inner = cos_sin(inner_index, inner_index, inner_size)
    table = rotation_table(cos_inner[:, low_col:high_col], sin_inner[:, low_col:high_col])
    final = jnp.einsum(
        "crkq,cdqm->drmk", twisted, table, precision=highest, preferred_element_type=jnp.float32
    )
    start = offset - low_col * outer_size
    rescale = 1.0 / math.sqrt(length)
    return final.reshape(2, -1, kept * outer_size)[:, :, start : start + band_size] * rescale


def filter_frames(padded, taps, frame_count):
    components, inputs, spans, length = padded.shape
    flat = padded.reshape(components * inputs, spans, length)
    kernel = taps[:, None, :]
    filtered = lax.conv_general_dilated(
        flat,
        kernel,
        (1,),
        "VALID",
        dimension_numbers=("NWC", "WIO", "NWC"),
        feature_group_count=length,
        precision=lax.Precision.HIGHEST,
        preferred_element_type=jnp.float32,
    )
    return filtered.reshape(components, inputs * frame_count, length)


def body(samples, taps, scales):
    tap_count, length = taps.shape
    history = tap_count - 1
    inputs = samples.shape[1]
    frames = samples.shape[2] // length
    band_size = scales.shape[1]
    station_count = lax.axis_size("stn")
    time_count = lax.axis_size("tm")
    per_device = band_size // (station_count * time_count)
    voltages = samples.reshape(2, inputs, frames, length)
    earlier = from_behind(voltages, "tm", 1)
    padded = jnp.concatenate([earlier, voltages], axis=2)
    spectrum = band_transform(filter_frames(padded, taps, frames), band_size)
    spectrum = spectrum.reshape(2, inputs, frames, band_size)
    factor = (scales.astype(jnp.float32) * 16.0)[None, :, None, :]
    quantized = jnp.clip(spectrum * factor, -127.0, 127.0).astype(jnp.bfloat16)
    arranged = quantized.reshape(2, inputs, frames, station_count, time_count, per_device)
    arranged = jnp.transpose(arranged, (0, 3, 4, 5, 1, 2))
    step_one = lax.all_to_all(arranged, "tm", split_axis=2, concat_axis=5, tiled=True)
    turned = lax.all_to_all(step_one, "stn", split_axis=1, concat_axis=4, tiled=True)
    all_inputs = turned.shape[4]
    all_frames = turned.shape[5]
    turned = turned.reshape(2, per_device, all_inputs, all_frames)
    normalizer = 1.0 / (2.0 * all_frames * length)
    joined = jnp.concatenate([turned[0], turned[1]], axis=2)
    swapped = jnp.concatenate([turned[1], -turned[0]], axis=2)
    both_left = jnp.stack([joined, swapped])
    products = jnp.einsum("scak,cbk->scab", both_left, joined, preferred_element_type=jnp.float32)
    positions = jnp.arange(all_inputs, dtype=jnp.int32)
    lower_mask = positions[:, None] >= positions[None, :]
    return (jnp.where(lower_mask[None], products[0], products[1]) * normalizer).astype(jnp.bfloat16)


def solution(mesh):
    placed = (P(None, "stn", "tm"), P(), P("stn", None))
    return jax.shard_map(
        body, mesh=mesh, in_specs=placed, out_specs=P(("stn", "tm"), None, None), check_vma=False
    )
```

profile of v0, /device:TPU:1, one launch (start us, length us, event | category | flops | bytes accessed | tf_op | source)
XLA Modules:
  0.0 228.2 jit_solution(4993729798927846625)
XLA Ops:
  0.0 3.1 %copy.50 = bf16[2,8,15,4096]{3,1,0,2:T(8,128)(2,1)} copy(bf16[2,8,15,4096]{3,1,2,0:T(8,128)(2,1)} %bitcast.102) | data formatting | bytes 3932160 | tf_op jit(solution)/shard_map/reshape | solution.py:93
  3.1 5.3 %collective-permute-start = (bf16[2,8,15,4096]{3,1,0,2:T(8,128)(2,1)}, bf16[2,8,15,4096]{3,1,0,2:T(8,128)(2,1)}, u32[]{:S(2)}, u32[]{:S(2)}) collective-permute-start(bf16[2,8,15,4096]{3,1,0,2:T(8,128)(2,1)} %copy.50), channel_id=1, source_target_pairs={{0,1},{1,2},{2,3},{3,4},{4,5},{5,6},{6,7},{8,9},{9,10},{10,11},{11... | collective-permute-start | bytes 5898248 | tf_op jit(solution)/shard_map/ppermute | solution.py:12
  8.4 3.1 %concatenate.15 = bf16[16,15,4096]{2,1,0:T(8,128)(2,1)S(1)} reshape(bf16[2,8,61440]{2,1,0:T(8,128)(2,1)} %param.3) | data formatting | bytes 3932160 | tf_op jit(solution)/shard_map/concatenate | solution.py:95
  11.5 2.4 %copy.51 = bf16[16,15,4096]{2,0,1:T(8,128)(2,1)} copy(bf16[16,15,4096]{2,1,0:T(8,128)(2,1)S(1)} %concatenate.15) | data formatting | bytes 3932160 | tf_op jit(solution)/shard_map/concatenate | solution.py:95
  13.9 0.3 copy.57
  14.9 30.8 %collective-permute-done = bf16[2,8,15,4096]{3,1,0,2:T(8,128)(2,1)} collective-permute-done((bf16[2,8,15,4096]{3,1,0,2:T(8,128)(2,1)}, bf16[2,8,15,4096]{3,1,0,2:T(8,128)(2,1)}, u32[]{:S(2)}, u32[]{:S(2)}) %collective-permute-start) | collective-permute-done | bytes 1966112 | tf_op jit(solution)/shard_map/ppermute | solution.py:12
  45.7 7.6 %fusion.9 = f32[16,15,4096]{2,0,1:T(8,128)S(1)} fusion(bf16[16,15,4096]{2,0,1:T(8,128)(2,1)} %copy.51, bf16[16,15,4096]{2,0,1:T(8,128)(2,1)} %bitcast.14, bf16[16,1,4096]{2,0,1:T(8,128)(2,1)S(1)} %bitcast.100), kind=kOutput, calls=%fused_computation.13 | convolution fusion | flops 33423360 | bytes 7995392 | tf_op jit(solution)/shard_map/conv_general_dilated | solution.py:71
  53.3 4.3 %copy.53 = f32[16,15,4096]{2,1,0:T(8,128)} copy(f32[16,15,4096]{2,0,1:T(8,128)S(1)} %fusion.9) | data formatting | bytes 7864320 | tf_op jit(solution)/shard_map/conv_general_dilated | solution.py:71
  57.6 7.6 %reshape_reshape.3 = f32[2,120,64,64]{3,2,1,0:T(8,128)} reshape(f32[16,15,4096]{2,1,0:T(8,128)} %copy.53) | data formatting | bytes 7864320 | tf_op jit(solution)/shard_map/reshape;reshape | solution.py:38
  65.2 8.6 %copy.54 = f32[2,120,64,64]{1,2,0,3:T(8,128)} copy(f32[2,120,64,64]{3,2,1,0:T(8,128)} %reshape_reshape.3) | data formatting | bytes 7864320 | tf_op jit(solution)/shard_map/reshape;reshape | solution.py:38
  73.8 5.5 %fusion.13 = f32[2,120,64,64]{1,2,3,0:T(8,128)S(1)} fusion(f32[2,120,64,64]{1,2,0,3:T(8,128)} %copy.54, f32[1,2,64,64]{2,3,0,1:T(8,128)S(1)} %get-tuple-element.15, f32[1,2,64,64]{2,3,0,1:T(8,128)S(1)} %get-tuple-element.14), kind=kOutput, calls=%fused_computation.18 | convolution fusion | flops 1509965824 | bytes 7929856 | tf_op jit(solution)/shard_map/crnq,cdnk->drkq/dot_general | solution.py:42
  79.3 1.6 multiply_add_fusion
  80.9 0.8 pad_maximum_fusion
  81.7 4.8 %fusion.19 = f32[2,120,32,64]{1,2,3,0:T(8,128)S(1)} fusion(f32[2,120,64,64]{1,2,3,0:T(8,128)S(1)} %pad_maximum_fusion, f32[1,2,64,32]{2,3,0,1:T(8,128)S(1)} %get-tuple-element.17, f32[1,2,64,32]{2,3,0,1:T(8,128)S(1)} %get-tuple-element.16), kind=kOutput, calls=%fused_computation.24 | convolution fusion | flops 754982912 | bytes 5931008 | tf_op jit(solution)/shard_map/crkq,cdqm->drmk/dot_general | solution.py:59
  86.5 1.2 copy.56
  87.7 8.3 %reshape.149 = f32[2,8,15,64,8,4]{2,1,5,4,3,0:T(8,128)} reshape(f32[2,120,32,64]{1,3,2,0:T(8,128)S(1)} %copy.56) | data formatting | bytes 3932160 | tf_op jit(solution)/shard_map/reshape | solution.py:64
  96.1 9.9 %fusion = bf16[2,64,8,4,8,15]{5,4,3,2,1,0:T(8,128)(2,1)} fusion(f32[2,8,15,64,8,4]{2,1,5,4,3,0:T(8,128)} %reshape.149, f32[8,64,8,4]{0,3,2,1:T(4,128)S(1)} %bitcast.104), kind=kLoop, calls=%fused_computation.1 | loop fusion | flops 1474560 | bytes 3014656 | tf_op jit(solution)/shard_map/transpose | solution.py:101
  106.0 11.1 %copy.58 = bf16[2,64,8,4,8,15]{1,4,5,3,0,2:T(8,128)(2,1)S(1)} copy(bf16[2,64,8,4,8,15]{5,4,3,2,1,0:T(8,128)(2,1)} %fusion) | data formatting | bytes 1966080 | tf_op jit(solution)/shard_map/transpose | solution.py:101
  117.1 1.4 reshape.157
  118.5 21.8 %all_to_all.33 = bf16[8,2,30720]{2,1,0:T(2,128)(2,1)} all-to-all(bf16[8,2,30720]{2,1,0:T(2,128)(2,1)S(1)} %reshape.157), channel_id=1, replica_groups=mesh['stn'=64,'tm'=8] {'tm'}, dimensions={0} | all-to-all | bytes 1966080 | tf_op jit(solution)/shard_map/all_to_all | solution.py:102
  140.2 3.5 %reshape.158 = bf16[8,2,4,15,8,64]{5,4,3,2,1,0:T(8,128)(2,1)S(1)} reshape(bf16[8,2,30720]{2,1,0:T(2,128)(2,1)} %all_to_all.33) | data formatting | bytes 1966080
  143.7 0.2 bitcast_bitcast_fusion
  143.9 0.3 copy.59
  144.1 3.0 %copy.60 = bf16[2,64,1,4,8,120]{5,4,3,2,0,1:T(8,128)(2,1)} copy(bf16[2,64,1,4,8,120]{1,4,5,3,0,2:T(8,128)(2,1)S(1)} %bitcast.103) | data formatting | bytes 1966080 | tf_op jit(solution)/shard_map/all_to_all | solution.py:102
  147.1 21.2 %all-to-all-start.1 = ((bf16[2,64,1,4,8,120]{5,4,3,2,0,1:T(8,128)(2,1)}), bf16[2,64,1,4,8,120]{5,4,3,2,0,1:T(8,128)(2,1)S(1)}, u32[]{:S(2)}, u32[]{:S(2)}) async-start(bf16[2,64,1,4,8,120]{5,4,3,2,0,1:T(8,128)(2,1)} %copy.60), calls=%async_computation.1 | async-start | bytes 2097152 | tf_op jit(solution)/shard_map/all_to_all | solution.py:103
  168.4 54.0 %all-to-all-done.1 = bf16[2,64,1,4,8,120]{5,4,3,2,0,1:T(8,128)(2,1)S(1)} async-done(((bf16[2,64,1,4,8,120]{5,4,3,2,0,1:T(8,128)(2,1)}), bf16[2,64,1,4,8,120]{5,4,3,2,0,1:T(8,128)(2,1)S(1)}, u32[]{:S(2)}, u32[]{:S(2)}) %all-to-all-start.1) | async-done | bytes 983072 | tf_op jit(solution)/shard_map/all_to_all | solution.py:103
  222.5 0.2 copy.63
  222.9 0.2 copy.64
  223.2 0.2 fusion.23
  223.3 1.3 convolution_bitcast_fusion
  224.7 1.2 fusion.3
  225.9 2.4 %copy.68 = bf16[4,512,512]{2,1,0:T(8,128)(2,1)} copy(bf16[4,512,512]{1,2,0:T(8,128)(2,1)S(1)} %fusion.3) | data formatting | bytes 4194304 | tf_op jit(solution)/shard_map/convert_element_type | solution.py:114
  (19 shorter events, 1.0 us)
Async XLA Ops:
  0.0 45.7 %copy-start = (bf16[16,4096]{1,0:T(8,128)(2,1)S(1)}, bf16[16,4096]{1,0:T(8,128)(2,1)}, u32[]{:S(2)}) copy-start(bf16[16,4096]{1,0:T(8,128)(2,1)} %param.4) | copy-start | bytes 393220
  3.1 42.6 %collective-permute-start = (bf16[2,8,15,4096]{3,1,0,2:T(8,128)(2,1)}, bf16[2,8,15,4096]{3,1,0,2:T(8,128)(2,1)}, u32[]{:S(2)}, u32[]{:S(2)}) collective-permute-start(bf16[2,8,15,4096]{3,1,0,2:T(8,128)(2,1)} %copy.50), channel_id=1, source_target_pairs={{0,1},{1,2},{2,3},{3,4},{4,5},{5,6},{6,7},{8,9},{9,10},{10,11},{11... | collective-permute-start | bytes 5898248 | tf_op jit(solution)/shard_map/ppermute | solution.py:12
  11.5 2.4 %copy-start.2 = (s32[8,2048]{1,0:T(8,128)S(1)}, s32[8,2048]{1,0:T(8,128)}, u32[]{:S(2)}) copy-start(s32[8,2048]{1,0:T(8,128)} %param.5) | copy-start | bytes 196612
  147.1 75.2 %all-to-all-start.1 = ((bf16[2,64,1,4,8,120]{5,4,3,2,0,1:T(8,128)(2,1)}), bf16[2,64,1,4,8,120]{5,4,3,2,0,1:T(8,128)(2,1)S(1)}, u32[]{:S(2)}, u32[]{:S(2)}) async-start(bf16[2,64,1,4,8,120]{5,4,3,2,0,1:T(8,128)(2,1)} %copy.60), calls=%async_computation.1 | async-start | bytes 2097152 | tf_op jit(solution)/shard_map/all_to_all | solution.py:103
  224.7 3.6 %copy-start.1 = (bf16[16,4096]{1,0:T(8,128)(2,1)S(1)}, bf16[16,4096]{1,0:T(8,128)(2,1)}, u32[]{:S(2)}) copy-start(bf16[16,4096]{1,0:T(8,128)(2,1)} %param.4) | copy-start | bytes 393220
where the time goes:
time: 230 us; the launch traced here: 228 us
  waiting for transfers between devices  84.8 us (37%)
  local copies, waits for them, and re-layouts  61.4 us (27%)
  starting transfers between devices  26.5 us (12%)
  blocking collectives  21.8 us (9%)
  matrix products  19.2 us (8%)
  other arithmetic  14.4 us (6%)
    all_to_all x1, waiting for transfers between devices, body(): lax.all_to_all(step_one, 'stn', split_axis=1, concat_axis=4, tiled=True)  54 us
    ppermute x1, waiting for transfers between devices, from_behind(): return lax.ppermute(block, axis, route)  30.8 us
    all_to_all x1, blocking collectives, body(): lax.all_to_all(arranged, 'tm', split_axis=2, concat_axis=5, tiled=True)  21.8 us
    all_to_all x1, starting transfers between devices, body(): lax.all_to_all(step_one, 'stn', split_axis=1, concat_axis=4, tiled=True)  21.2 us
    another operation x2, local copies, waits for them, and re-layouts, band_transform(): first = filtered.reshape(2, -1, outer_size, inner_size)  16.2 us
    transpose x1, local copies, waits for them, and re-layouts, body(): arranged = jnp.transpose(arranged, (0, 3, 4, 5, 1, 2))  11.1 us
    transpose x1, other arithmetic, body(): arranged = jnp.transpose(arranged, (0, 3, 4, 5, 1, 2))  9.9 us
    reshape x1, local copies, waits for them, and re-layouts, band_transform(): final.reshape(2, -1, kept * outer_size)[:, :, start:start + band_size]  8.35 us
  transfers between devices with their start and end apart: 2, of which 2 were waited for; matrix products, arithmetic and copies ran while one was open for 3% of the time, Pallas kernels for 0%

commit v1 on v0

v1 whole, which is shorter than its diff:
```python
import functools
import math

import jax
import jax.numpy as jnp
import numpy as np
from jax import lax
from jax.experimental import pallas as pl
from jax.experimental.pallas import tpu as pltpu
from jax.sharding import PartitionSpec as P

LANES = 128
RADIX = 16
FINE = 256
KEPT = 128
SLOT = 16
VMEM_LIMIT = 56 * 2**20


def second_table():
    fine = np.arange(FINE)
    outputs = np.arange(KEPT) + (FINE - KEPT) // 2
    angle = 2.0 * np.pi * ((outputs[:, None] * fine[None, :]) % FINE) / FINE
    cosine, sine = np.cos(angle), np.sin(angle)
    return np.block([[cosine, sine], [-sine, cosine]])


def twist_table():
    angle = 2.0 * np.pi * (np.arange(RADIX)[:, None] * np.arange(FINE)[None, :]) / (RADIX * FINE)
    return np.stack([np.cos(angle), -np.sin(angle)]).astype(np.float32)


def add(a, b):
    return (a[0] + b[0], a[1] + b[1])


def sub(a, b):
    return (a[0] - b[0], a[1] - b[1])


def turn(a):
    return (a[1], -a[0])


def four(a, b, c, d):
    even, odd = add(a, c), sub(a, c)
    both, rest = add(b, d), turn(sub(b, d))
    return (add(even, both), add(odd, rest), sub(even, both), sub(odd, rest))


def times_root(a, power):
    if power == 0:
        return a
    if power == 4:
        return turn(a)
    half = math.sqrt(0.5)
    if power == 2:
        return ((a[0] + a[1]) * half, (a[1] - a[0]) * half)
    if power == 6:
        return ((a[1] - a[0]) * half, -(a[0] + a[1]) * half)
    cosine, sine = math.cos(2 * math.pi * power / 16), math.sin(2 * math.pi * power / 16)
    return (a[0] * cosine + a[1] * sine, a[1] * cosine - a[0] * sine)


def sixteen(points):
    columns = [four(points[b], points[4 + b], points[8 + b], points[12 + b]) for b in range(4)]
    out = [None] * 16
    for low in range(4):
        mixed = four(*[times_root(columns[b][low], b * low) for b in range(4)])
        for high in range(4):
            out[low + 4 * high] = mixed[high]
    return out


def channelize_kernel(
    frames, own_ref, halo_ref, taps_ref, twist_ref, table_ref, factor_ref, out_ref, filt, rows, words
):
    length = RADIX * FINE
    tap_count = taps_ref.shape[0]
    history = tap_count - 1

    def filter_chunk(chunk, _):
        taps = [
            jnp.broadcast_to(taps_ref[pl.ds(p, 1), pl.ds(pl.multiple_of(chunk * LANES, LANES), LANES)], (8, LANES))
            for p in range(tap_count)
        ]
        for comp in range(2):
            sums = [None] * frames
            for v in range(history + frames):
                ref, u = (halo_ref, v) if v < history else (own_ref, v - history)
                at = pl.multiple_of(u * length + chunk * LANES, LANES)
                block = ref[comp, :, pl.ds(at, LANES)].astype(jnp.float32)
                for f in range(max(0, v - history), min(frames, v + 1)):
                    term = taps[v - f] * block
                    sums[f] = term if sums[f] is None else sums[f] + term
            for f in range(frames):
                filt[comp, chunk, f] = sums[f]
        return 0

    lax.fori_loop(0, length // LANES, filter_chunk, 0)

    rows[...] = jnp.zeros_like(rows)

    def first_transform(f, _):
        for half in range(2):
            points = [(filt[0, 2 * n + half, f], filt[1, 2 * n + half, f]) for n in range(RADIX)]
            mixed = sixteen(points)
            for k1 in range(RADIX):
                real, imag = mixed[k1]
                if k1:
                    cosine = twist_ref[0, pl.ds(k1, 1), pl.ds(half * LANES, LANES)]
                    sine = twist_ref[1, pl.ds(k1, 1), pl.ds(half * LANES, LANES)]
                    real, imag = real * cosine - imag * sine, imag * cosine + real * sine
                start = (k1 // 4) * (8 * 4 * SLOT) + (k1 % 4) * SLOT + f
                rows[half, pl.ds(start, 8, stride=4 * SLOT), :] = real
                rows[2 + half, pl.ds(start, 8, stride=4 * SLOT), :] = imag
        return 0

    lax.fori_loop(0, frames, first_transform, 0)

    low_lanes = lax.broadcasted_iota(jnp.int32, (KEPT, LANES), 1) < LANES // 2

    def second_transform(group, _):
        span = pl.ds(pl.multiple_of(group * 256, 256), 256)
        block = jnp.concatenate([rows[q, span, :] for q in range(4)], axis=1)
        high = block.astype(jnp.bfloat16)
        low = (block - high.astype(jnp.float32)).astype(jnp.bfloat16)
        contract = (((1,), (1,)), ((), ()))
        both = lax.dot_general(table_ref[...], high, contract, preferred_element_type=jnp.float32)
        rest = lax.dot_general(table_ref[: 2 * KEPT], low, contract, preferred_element_type=jnp.float32)
        total = both[: 2 * KEPT] + both[2 * KEPT :] + rest
        for pair in range(2):
            real = total[:KEPT, pair * LANES : (pair + 1) * LANES]
            imag = total[KEPT:, pair * LANES : (pair + 1) * LANES]
            first = jnp.where(low_lanes, real, pltpu.roll(imag, LANES // 2, 1))
            second = jnp.where(low_lanes, pltpu.roll(real, LANES // 2, 1), imag)
            at = group * 4 + pair * 2
            words[pl.ds(at, KEPT, stride=32), :] = first
            words[pl.ds(at + 1, KEPT, stride=32), :] = second
        return 0

    lax.fori_loop(0, rows.shape[1] // 256, second_transform, 0)

    def requantize(step, _):
        span = pl.ds(pl.multiple_of(step * 256, 256), 256)
        values = words[span, :] * factor_ref[span, :].astype(jnp.float32)
        out_ref[span, :] = jnp.clip(values, -127.0, 127.0).astype(jnp.bfloat16)
        return 0

    lax.fori_loop(0, words.shape[0] // 256, requantize, 0)


def channelize(own, halo, taps, factor):
    inputs, frames = own.shape[1], own.shape[2] // taps.shape[1]
    table = second_table()
    high = table.astype(jnp.bfloat16)
    low = (table - high.astype(np.float64)).astype(jnp.bfloat16)
    vmem = pl.BlockSpec(memory_space=pltpu.VMEM)
    messages = KEPT * 4 * inputs
    return pl.pallas_call(
        functools.partial(channelize_kernel, frames),
        out_shape=jax.ShapeDtypeStruct((messages, LANES), jnp.bfloat16),
        in_specs=[vmem] * 6,
        out_specs=vmem,
        scratch_shapes=[
            pltpu.VMEM((2, RADIX * FINE // LANES, frames, inputs, LANES), jnp.float32),
            pltpu.VMEM((4, 4 * inputs * 4 * SLOT, LANES), jnp.float32),
            pltpu.VMEM((messages, LANES), jnp.float32),
        ],
        compiler_params=pltpu.CompilerParams(vmem_limit_bytes=VMEM_LIMIT),
        name="channelize",
    )(own, halo, taps.astype(jnp.float32), twist_table(), jnp.concatenate([high, low]), factor)


def correlate_kernel(normalizer, words_ref, out_ref, joined, swapped):
    channel = pl.program_id(0)
    size = joined.shape[0]
    lane = lax.broadcasted_iota(jnp.int32, (size, LANES), 1)

    @pl.when(channel == 0)
    def _():
        sign = jnp.where(lane < LANES // 2, 1.0, -1.0)
        for t in range(8):
            block = words_ref[:, t].astype(jnp.float32).reshape(size, LANES)
            joined[:, t * LANES : (t + 1) * LANES] = block.astype(jnp.bfloat16)
            other = pltpu.roll(block, LANES // 2, 1) * sign
            swapped[:, t * LANES : (t + 1) * LANES] = other.astype(jnp.bfloat16)

    ours = (lane // SLOT) % 4 == channel
    chosen = jnp.concatenate([ours] * 8, axis=1)
    zero = jnp.zeros((), jnp.bfloat16)
    real_left = jnp.where(chosen, joined[...], zero)
    imag_left = jnp.where(chosen, swapped[...], zero)
    half = size // 2

    def product(left, right):
        return lax.dot_general(
            left, right, (((1,), (1,)), ((), ())), preferred_element_type=jnp.float32
        )

    first, second = joined[:half], joined[half:]
    lower = lax.broadcasted_iota(jnp.int32, (half, half), 0) >= lax.broadcasted_iota(
        jnp.int32, (half, half), 1
    )

    def finish(values):
        return (values * normalizer).astype(jnp.bfloat16)

    out_ref[0, :half, :half] = finish(
        jnp.where(lower, product(real_left[:half], first), product(imag_left[:half], first))
    )
    out_ref[0, half:, :half] = finish(product(real_left[half:], first))
    out_ref[0, :half, half:] = finish(product(imag_left[:half], second))
    out_ref[0, half:, half:] = finish(
        jnp.where(lower, product(real_left[half:], second), product(imag_left[half:], second))
    )


def correlate(words, normalizer):
    stations, _, inputs, _ = words.shape
    size = stations * inputs
    return pl.pallas_call(
        functools.partial(correlate_kernel, normalizer),
        grid=(4,),
        out_shape=jax.ShapeDtypeStruct((4, size, size), jnp.bfloat16),
        in_specs=[pl.BlockSpec(words.shape, lambda c: (0, 0, 0, 0))],
        out_specs=pl.BlockSpec((1, size, size), lambda c: (c, 0, 0)),
        scratch_shapes=[
            pltpu.VMEM((size, 8 * LANES), jnp.bfloat16),
            pltpu.VMEM((size, 8 * LANES), jnp.bfloat16),
        ],
        compiler_params=pltpu.CompilerParams(vmem_limit_bytes=VMEM_LIMIT),
        name="correlate",
    )(words)


def message_factor(scales, rescale):
    inputs, band = scales.shape
    factor = (scales.astype(jnp.float32) * rescale).astype(jnp.bfloat16)
    factor = jnp.transpose(factor.reshape(inputs, band // 4, 4), (1, 0, 2))
    factor = jnp.broadcast_to(factor[:, :, None, :, None], (band // 4, inputs, 2, 4, SLOT))
    return factor.reshape(band // 4 * inputs, 8 * SLOT)


def body(samples, taps, scales):
    length = taps.shape[1]
    inputs = samples.shape[1]
    frames = samples.shape[2] // length
    stations, times = lax.axis_size("stn"), lax.axis_size("tm")
    halo = lax.ppermute(samples, "tm", [(i, i + 1) for i in range(times - 1)])
    factor = message_factor(scales, 16.0 / math.sqrt(length))
    words = channelize(samples, halo, taps, factor)
    words = words.reshape(stations * times, inputs, LANES)
    words = lax.all_to_all(words, ("stn", "tm"), split_axis=0, concat_axis=0, tiled=True)
    words = words.reshape(stations, times, inputs, LANES)
    return correlate(words, 1.0 / (2.0 * frames * times * length))


def solution(mesh):
    placed = (P(None, "stn", "tm"), P(), P("stn", None))
    return jax.shard_map(
        body, mesh=mesh, in_specs=placed, out_specs=P(("stn", "tm"), None, None), check_vma=False
    )
```

time: 230 us -> 155 us (0.67)
  waiting for transfers between devices: 84.8 us -> 15.4 us
  blocking collectives: 21.8 us -> 86.9 us
  local copies, waits for them, and re-layouts: 61.4 us -> 22.7 us
  Pallas kernels: 0 us -> 24.2 us
  starting transfers between devices: 26.5 us -> 4.15 us
  matrix products: 19.2 us -> 0 us
  other arithmetic: 14.4 us -> 1.57 us
    all_to_all x1, blocking collectives: 21.8 us -> 86.9 us  [body(): lax.all_to_all(words, ('stn', 'tm'), split_axis=0, concat_axis=0, tiled=T...]
    all_to_all x1 -> x0, waiting for transfers between devices: 54 us -> none  [body(): lax.all_to_all(step_one, 'stn', split_axis=1, concat_axis=4, tiled=True)]
    pallas_call x0 -> x2, Pallas kernels: none -> 24.2 us  [the longest x1 17.5 us: channelize(): pl.pallas_call(functools.partial(channelize_kernel, frames), out_shape=ja...]
    all_to_all x1 -> x0, starting transfers between devices: 21.2 us -> none  [body(): lax.all_to_all(step_one, 'stn', split_axis=1, concat_axis=4, tiled=True)]
    another operation x2 -> x0, local copies, waits for them, and re-layouts: 16.2 us -> none  [band_transform(): first = filtered.reshape(2, -1, outer_size, inner_size)]
    ppermute x1, waiting for transfers between devices: 30.8 us -> 15.4 us  [body(): halo = lax.ppermute(samples, 'tm', [(i, i + 1) for i in range(times - 1)])]
    dot_general x3 -> x0, matrix products: 11.6 us -> none  [the longest x1 5.51 us: band_transform(): jnp.einsum('crnq,cdnk->drkq', first, rotation_table(cos_outer, sin_outer)...]
    transpose x1 -> x0, other arithmetic: 9.9 us -> none  [body(): arranged = jnp.transpose(arranged, (0, 3, 4, 5, 1, 2))]
  transfers between devices with their start and end apart: 2 -> 1, of which waited for: 2 -> 1; matrix products, arithmetic and copies ran while one was open for 3% -> 15% of each run, Pallas kernels for 0% -> 0%
where the time goes in v1:
time: 155 us
  blocking collectives  86.9 us (56%)
  Pallas kernels  24.2 us (16%)
  local copies, waits for them, and re-layouts  22.7 us (15%)
  waiting for transfers between devices  15.4 us (10%)
  starting transfers between devices  4.15 us (3%)
  other arithmetic  1.57 us (1%)
    all_to_all x1, blocking collectives, body(): lax.all_to_all(words, ('stn', 'tm'), split_axis=0, concat_axis=0, tiled=T...  86.9 us
    pallas_call x1, Pallas kernels, channelize(): pl.pallas_call(functools.partial(channelize_kernel, frames), out_shape=ja...  17.5 us
    ppermute x1, waiting for transfers between devices, body(): halo = lax.ppermute(samples, 'tm', [(i, i + 1) for i in range(times - 1)])  15.4 us
    reshape x1, local copies, waits for them, and re-layouts, message_factor(): return factor.reshape(band // 4 * inputs, 8 * SLOT)  12 us
    pallas_call x1, Pallas kernels, correlate(): pl.pallas_call(functools.partial(correlate_kernel, normalizer), grid=(4,)...  6.65 us
    broadcast_in_dim x1, local copies, waits for them, and re-layouts, message_factor(): jnp.broadcast_to(factor[:, :, None, :, None], (band // 4, inputs, 2, 4, S...  5.97 us
    ppermute x1, starting transfers between devices, body(): halo = lax.ppermute(samples, 'tm', [(i, i + 1) for i in range(times - 1)])  4.15 us
    transpose x1, local copies, waits for them, and re-layouts, message_factor(): factor = jnp.transpose(factor.reshape(inputs, band // 4, 4), (1, 0, 2))  3.21 us
  transfers between devices with their start and end apart: 1, of which 1 were waited for; matrix products, arithmetic and copies ran while one was open for 15% of the time, Pallas kernels for 0%

profile of v1, /device:TPU:1, one launch (start us, length us, event | category | flops | bytes accessed | tf_op | source)
XLA Modules:
  0.0 154.9 jit_solution(17260625326301172246)
XLA Ops:
  0.0 4.1 %collective-permute-start = (bf16[2,8,61440]{2,1,0:T(8,128)(2,1)}, bf16[2,8,61440]{2,1,0:T(8,128)(2,1)S(1)}, u32[]{:S(2)}, u32[]{:S(2)}) collective-permute-start(bf16[2,8,61440]{2,1,0:T(8,128)(2,1)} %own_ref.1), channel_id=1, source_target_pairs={{0,1},{1,2},{2,3},{3,4},{4,5},{5,6},{6,7},{8,9},{9,10},{10,11},{11... | collective-permute-start | bytes 5898248 | tf_op jit(solution)/shard_map/ppermute | solution.py:250
  4.2 0.8 multiply_convert_fusion
  5.0 0.3 copy.8
  5.3 3.2 %copy.9 = bf16[512,8,4]{2,1,0:T(8,128)(2,1)S(1)} copy(bf16[512,8,4]{1,2,0:T(4,128)(2,1)S(1)} %bitcast.7) | data formatting | bytes 65536 | tf_op jit(solution)/shard_map/transpose | solution.py:240
  8.5 6.0 %broadcast_in_dim.2 = bf16[512,8,2,4,16]{4,3,2,1,0:T(4,128)(2,1)} broadcast(bf16[512,8,4]{2,1,0:T(8,128)(2,1)S(1)} %copy.9), dimensions={0,1,3} | broadcast | bytes 1081344 | tf_op jit(solution)/shard_map/broadcast_in_dim | solution.py:241
  14.5 0.0 copy-start.1
  14.5 12.0 %reshape.14.factor_ref = bf16[4096,128]{1,0:T(8,128)(2,1)} reshape(bf16[512,8,2,4,16]{4,3,2,1,0:T(4,128)(2,1)} %broadcast_in_dim.2) | data formatting | bytes 2097152 | tf_op jit(solution)/shard_map/reshape | solution.py:242
  26.5 0.0 copy-done.1
  26.5 0.7 convert_element_type.9.taps_ref
  27.2 15.4 %collective-permute-done.halo_ref = bf16[2,8,61440]{2,1,0:T(8,128)(2,1)S(1)} collective-permute-done((bf16[2,8,61440]{2,1,0:T(8,128)(2,1)}, bf16[2,8,61440]{2,1,0:T(8,128)(2,1)S(1)}, u32[]{:S(2)}, u32[]{:S(2)}) %collective-permute-start) | collective-permute-done | bytes 1966112 | tf_op jit(solution)/shard_map/ppermute | solution.py:250
  42.6 0.0 copy-start
  42.6 1.3 copy-done
  43.9 17.5 %channelize.1 = bf16[4096,128]{1,0:T(8,128)(2,1)} custom-call(bf16[2,8,61440]{2,1,0:T(8,128)(2,1)} %own_ref.1, bf16[2,8,61440]{2,1,0:T(8,128)(2,1)} %copy-done, f32[16,4096]{1,0:T(8,128)} %convert_element_type.9.taps_ref, f32[2,16,256]{2,1,0:T(8,128)} %constant.10.clone.twist_ref, bf16[512,512]{1,0:T(8,128)(2,1)} %constant.13.table_ref, ...), custom_call_target="tpu_custom_call" | custom-call | tf_op jit(solution)/shard_map/channelize/pallas_call | solution.py:160
  61.4 86.9 %all_to_all.5 = bf16[512,8,128]{2,1,0:T(8,128)(2,1)} all-to-all(bf16[512,8,128]{2,1,0:T(8,128)(2,1)} %bitcast.6), channel_id=1, replica_groups=mesh['stn'=64,'tm'=8] {'stn','tm'}, dimensions={0} | all-to-all | bytes 2097152 | tf_op jit(solution)/shard_map/all_to_all | solution.py:254
  148.3 6.6 %correlate.1 = bf16[4,512,512]{2,1,0:T(8,128)(2,1)} custom-call(bf16[64,8,8,128]{3,2,1,0:T(8,128)(2,1)} %bitcast.5), custom_call_target="tpu_custom_call" | custom-call | tf_op jit(solution)/shard_map/correlate/pallas_call | solution.py:222
Async XLA Ops:
  0.0 42.6 %collective-permute-start = (bf16[2,8,61440]{2,1,0:T(8,128)(2,1)}, bf16[2,8,61440]{2,1,0:T(8,128)(2,1)S(1)}, u32[]{:S(2)}, u32[]{:S(2)}) collective-permute-start(bf16[2,8,61440]{2,1,0:T(8,128)(2,1)} %own_ref.1), channel_id=1, source_target_pairs={{0,1},{1,2},{2,3},{3,4},{4,5},{5,6},{6,7},{8,9},{9,10},{10,11},{11... | collective-permute-start | bytes 5898248 | tf_op jit(solution)/shard_map/ppermute | solution.py:250
  14.5 12.0 %copy-start.1 = (bf16[16,4096]{1,0:T(8,128)(2,1)S(1)}, bf16[16,4096]{1,0:T(8,128)(2,1)}, u32[]{:S(2)}) copy-start(bf16[16,4096]{1,0:T(8,128)(2,1)} %param.7) | copy-start | bytes 393220
  42.6 1.3 copy-start

commit v2 on v1

v2 whole, which is shorter than its diff:
```python
import functools
import math

import jax
import jax.numpy as jnp
import numpy as np
from jax import lax
from jax.experimental import pallas as pl
from jax.experimental.pallas import tpu as pltpu
from jax.sharding import PartitionSpec as P

LANES = 128
RADIX = 16
FINE = 256
KEPT = 128
SLOT = 16
PAD = 1
VMEM_LIMIT = 56 * 2**20


def second_table():
    fine = np.arange(FINE)
    outputs = np.arange(KEPT) + (FINE - KEPT) // 2
    angle = 2.0 * np.pi * ((outputs[:, None] * fine[None, :]) % FINE) / FINE
    cosine, sine = np.cos(angle), np.sin(angle)
    return np.block([[cosine, sine], [-sine, cosine]]).T


def twist_table():
    angle = 2.0 * np.pi * (np.arange(RADIX)[:, None] * np.arange(FINE)[None, :]) / (RADIX * FINE)
    return np.stack([np.cos(angle), -np.sin(angle)]).astype(np.float32)


def add(a, b):
    return (a[0] + b[0], a[1] + b[1])


def sub(a, b):
    return (a[0] - b[0], a[1] - b[1])


def turn(a):
    return (a[1], -a[0])


def four(a, b, c, d):
    even, odd = add(a, c), sub(a, c)
    both, rest = add(b, d), turn(sub(b, d))
    return (add(even, both), add(odd, rest), sub(even, both), sub(odd, rest))


def times_root(a, power):
    if power == 0:
        return a
    if power == 4:
        return turn(a)
    half = math.sqrt(0.5)
    if power == 2:
        return ((a[0] + a[1]) * half, (a[1] - a[0]) * half)
    if power == 6:
        return ((a[1] - a[0]) * half, -(a[0] + a[1]) * half)
    cosine, sine = math.cos(2 * math.pi * power / 16), math.sin(2 * math.pi * power / 16)
    return (a[0] * cosine + a[1] * sine, a[1] * cosine - a[0] * sine)


def sixteen(points):
    columns = [four(points[b], points[4 + b], points[8 + b], points[12 + b]) for b in range(4)]
    out = [None] * 16
    for low in range(4):
        mixed = four(*[times_root(columns[b][low], b * low) for b in range(4)])
        for high in range(4):
            out[low + 4 * high] = mixed[high]
    return out


def deal_kernel(in_ref, out_ref, rows):
    inputs, count = out_ref.shape[0], out_ref.shape[1]
    stride = rows.shape[0] // inputs
    for j in range(count):
        block = in_ref[0, :, j * LANES : (j + 1) * LANES].astype(jnp.float32)
        rows[pl.ds(j, inputs, stride=stride), :] = block
    for i in range(inputs):
        out_ref[i] = rows[i * stride : i * stride + count, :].astype(jnp.bfloat16)


def deal(samples):
    components, inputs, length = samples.shape
    count = 480
    steps = length // LANES // count
    return pl.pallas_call(
        deal_kernel,
        grid=(components, steps),
        out_shape=jax.ShapeDtypeStruct((inputs, components * length // LANES, LANES), samples.dtype),
        in_specs=[pl.BlockSpec((1, inputs, count * LANES), lambda c, j: (c, 0, j))],
        out_specs=pl.BlockSpec((inputs, count, LANES), lambda c, j: (0, c * steps + j, 0)),
        scratch_shapes=[pltpu.VMEM((inputs * (count + 8), LANES), jnp.float32)],
        compiler_params=pltpu.CompilerParams(vmem_limit_bytes=VMEM_LIMIT),
        name="deal",
    )(samples)


def channelize_kernel(
    frames, in_ref, taps_ref, twist_ref, table_ref, factor_ref, out_ref, wide, filt, rows, words
):
    chunks = RADIX * FINE // LANES
    tap_count = taps_ref.shape[0]
    history = tap_count - 1
    times, block_rows = in_ref.shape[0], in_ref.shape[1]
    stride = wide.shape[0] // (times + 1)

    wide[:block_rows] = jnp.zeros((block_rows, LANES), jnp.float32)
    for t in range(times):
        wide[(t + 1) * stride : (t + 1) * stride + block_rows] = in_ref[t].astype(jnp.float32)

    def filter_chunk(chunk, _):
        lanes = pl.ds(pl.multiple_of(chunk * LANES, LANES), LANES)
        weights = taps_ref[:, lanes].astype(jnp.float32)
        taps = [jnp.broadcast_to(weights[p : p + 1], (times, LANES)) for p in range(tap_count)]
        for comp in range(2):
            sums = [None] * frames
            for v in range(history + frames):
                before, u = (0, v) if v < history else (1, v - history)
                start = before * stride + (comp * frames + u) * chunks + chunk
                block = wide[pl.ds(start, times, stride=stride), :]
                for f in range(max(0, v - history), min(frames, v + 1)):
                    term = taps[v - f] * block
                    sums[f] = term if sums[f] is None else sums[f] + term
            for f in range(frames):
                filt[comp, chunk, f] = sums[f]
        return 0

    lax.fori_loop(0, chunks, filter_chunk, 0)

    for q in range(4):
        rows[q, pl.ds(frames, RADIX * times, stride=SLOT), :] = jnp.zeros((RADIX * times, LANES), jnp.float32)

    def first_transform(f, _):
        for half in range(2):
            points = [(filt[0, 2 * n + half, f], filt[1, 2 * n + half, f]) for n in range(RADIX)]
            mixed = sixteen(points)
            for k1 in range(RADIX):
                real, imag = mixed[k1]
                if k1:
                    cosine = twist_ref[0, pl.ds(k1, 1), pl.ds(half * LANES, LANES)]
                    sine = twist_ref[1, pl.ds(k1, 1), pl.ds(half * LANES, LANES)]
                    real, imag = real * cosine - imag * sine, imag * cosine + real * sine
                start = k1 * times * SLOT + f
                rows[half, pl.ds(start, times, stride=SLOT), :] = real
                rows[2 + half, pl.ds(start, times, stride=SLOT), :] = imag
        return 0

    lax.fori_loop(0, frames, first_transform, 0)

    def second_transform(group, _):
        span = pl.ds(pl.multiple_of(group * 512, 512), 512)
        block = jnp.concatenate([rows[q, span, :] for q in range(4)], axis=1)
        high = block.astype(jnp.bfloat16)
        low = (block - high.astype(jnp.float32)).astype(jnp.bfloat16)
        both = jnp.dot(high, table_ref[...], preferred_element_type=jnp.float32)
        rest = jnp.dot(low, table_ref[:, : 2 * KEPT], preferred_element_type=jnp.float32)
        total = both[:, : 2 * KEPT] + both[:, 2 * KEPT :] + rest
        for channel in range(4):
            scale = factor_ref[pl.ds(group * 4 + channel, 1), :]
            part = total[channel * LANES : (channel + 1) * LANES]
            real = jnp.clip(part[:, :KEPT] * scale, -127.0, 127.0)
            imag = jnp.clip(part[:, KEPT:] * scale, -127.0, 127.0)
            for side in range(2):
                cut = slice(side * 64, side * 64 + 64)
                word = jnp.concatenate([real[cut], imag[cut]], axis=0).T
                words[pl.ds(group * 8 + channel * 2 + side, KEPT, stride=32), :] = word
        return 0

    lax.fori_loop(0, rows.shape[1] // 512, second_transform, 0)

    def narrow(step, _):
        span = pl.ds(pl.multiple_of(step * 1024, 1024), 1024)
        out_ref[span, :] = words[span, :].astype(jnp.bfloat16)
        return 0

    lax.fori_loop(0, words.shape[0] // 1024, narrow, 0)


def channelize(dealt, taps, factor):
    times, block_rows, _ = dealt.shape
    chunks = RADIX * FINE // LANES
    frames = block_rows // (2 * chunks)
    table = second_table()
    high = table.astype(jnp.bfloat16)
    low = (table - high.astype(np.float64)).astype(jnp.bfloat16)
    vmem = pl.BlockSpec(memory_space=pltpu.VMEM)
    messages = KEPT * RADIX * 2
    return pl.pallas_call(
        functools.partial(channelize_kernel, frames),
        out_shape=jax.ShapeDtypeStruct((messages, LANES), jnp.bfloat16),
        in_specs=[vmem] * 5,
        out_specs=vmem,
        scratch_shapes=[
            pltpu.VMEM(((times + 1) * (block_rows + PAD), LANES), jnp.float32),
            pltpu.VMEM((2, chunks, frames, times, LANES), jnp.float32),
            pltpu.VMEM((4, RADIX * times * SLOT, LANES), jnp.float32),
            pltpu.VMEM((messages, LANES), jnp.float32),
        ],
        compiler_params=pltpu.CompilerParams(vmem_limit_bytes=VMEM_LIMIT),
        name="channelize",
    )(dealt, taps, twist_table(), jnp.concatenate([high, low], axis=1), factor)


def correlate_kernel(normalizer, words_ref, out_ref, wide):
    channel = pl.program_id(0)
    size = words_ref.shape[0] // 8
    half = size // 2

    @pl.when(channel == 0)
    def _():
        wide[...] = words_ref[...].astype(jnp.float32)

    sign = jnp.where(lax.broadcasted_iota(jnp.int32, (size, LANES), 1) < LANES // 2, 1.0, -1.0)
    blocks = [wide[pl.ds(2 * channel + q, size, stride=8), :] for q in range(2)]
    joined = jnp.concatenate(blocks, axis=1).astype(jnp.bfloat16)
    swapped = [pltpu.roll(block, LANES // 2, 1) * sign for block in blocks]
    swapped = jnp.concatenate(swapped, axis=1).astype(jnp.bfloat16)

    def product(left, right):
        return lax.dot_general(
            left, right, (((1,), (1,)), ((), ())), preferred_element_type=jnp.float32
        )

    first, second = joined[:half], joined[half:]
    lower = lax.broadcasted_iota(jnp.int32, (half, half), 0) >= lax.broadcasted_iota(
        jnp.int32, (half, half), 1
    )

    def finish(values):
        return (values * normalizer).astype(jnp.bfloat16)

    out_ref[0, :half, :half] = finish(
        jnp.where(lower, product(first, first), product(swapped[:half], first))
    )
    out_ref[0, half:, :half] = finish(product(second, first))
    out_ref[0, :half, half:] = finish(product(swapped[:half], second))
    out_ref[0, half:, half:] = finish(
        jnp.where(lower, product(second, second), product(swapped[half:], second))
    )


def correlate(words, normalizer):
    rows, _ = words.shape
    size = rows // 8
    return pl.pallas_call(
        functools.partial(correlate_kernel, normalizer),
        grid=(4,),
        out_shape=jax.ShapeDtypeStruct((4, size, size), jnp.bfloat16),
        in_specs=[pl.BlockSpec(words.shape, lambda c: (0, 0))],
        out_specs=pl.BlockSpec((1, size, size), lambda c: (c, 0, 0)),
        scratch_shapes=[pltpu.VMEM((rows, LANES), jnp.float32)],
        compiler_params=pltpu.CompilerParams(vmem_limit_bytes=VMEM_LIMIT),
        name="correlate",
    )(words)


def band_factor(scales, rescale):
    return (scales.astype(jnp.float32) * rescale).reshape(KEPT, RADIX).T


def body(samples, taps, scales):
    length = taps.shape[1]
    inputs = samples.shape[1]
    frames = samples.shape[2] // length
    stations, times = lax.axis_size("stn"), lax.axis_size("tm")
    mine = lax.dynamic_index_in_dim(scales, lax.axis_index("tm"), 0, keepdims=False)
    factor = band_factor(mine, 16.0 / math.sqrt(length))
    dealt = lax.all_to_all(deal(samples), "tm", split_axis=0, concat_axis=0, tiled=True)
    words = channelize(dealt, taps, factor)
    words = words.reshape(stations * times, 8, LANES)
    words = lax.all_to_all(words, ("stn", "tm"), split_axis=0, concat_axis=0, tiled=True)
    words = words.reshape(stations * times * 8, LANES)
    return correlate(words, 1.0 / (2.0 * frames * times * length))


def solution(mesh):
    placed = (P(None, "stn", "tm"), P(), P("stn", None))
    return jax.shard_map(
        body, mesh=mesh, in_specs=placed, out_specs=P(("stn", "tm"), None, None), check_vma=False
    )
```

time: 155 us -> 134 us (0.86)
  local copies, waits for them, and re-layouts: 22.7 us -> 2.02 us
  waiting for transfers between devices: 15.4 us -> 22.1 us
  blocking collectives: 86.9 us -> 81.6 us
  Pallas kernels: 24.2 us -> 20.8 us
  starting transfers between devices: 4.15 us -> 5.95 us
    all_to_all x0 -> x1, waiting for transfers between devices: none -> 22.1 us  [body(): lax.all_to_all(deal(samples), 'tm', split_axis=0, concat_axis=0, tiled=True)]
    ppermute x1 -> x0, waiting for transfers between devices: 15.4 us -> none  [body(): halo = lax.ppermute(samples, 'tm', [(i, i + 1) for i in range(times - 1)])]
    reshape x1 -> x0, local copies, waits for them, and re-layouts: 12 us -> none  [message_factor(): return factor.reshape(band // 4 * inputs, 8 * SLOT)]
    broadcast_in_dim x1 -> x0, local copies, waits for them, and re-layouts: 5.97 us -> none  [message_factor(): jnp.broadcast_to(factor[:, :, None, :, None], (band // 4, inputs, 2, 4, S...]
    all_to_all x0 -> x1, starting transfers between devices: none -> 5.95 us  [body(): lax.all_to_all(deal(samples), 'tm', split_axis=0, concat_axis=0, tiled=True)]
    all_to_all x1, blocking collectives: 86.9 us -> 81.6 us  [body(): lax.all_to_all(words, ('stn', 'tm'), split_axis=0, concat_axis=0, tiled=T...]
    ppermute x1 -> x0, starting transfers between devices: 4.15 us -> none  [body(): halo = lax.ppermute(samples, 'tm', [(i, i + 1) for i in range(times - 1)])]
    pallas_call x1, Pallas kernels: 17.5 us -> 13.7 us  [channelize(): pl.pallas_call(functools.partial(channelize_kernel, frames), out_shape=ja...]
  transfers between devices with their start and end apart: 1 -> 1, of which waited for: 1 -> 1; matrix products, arithmetic and copies ran while one was open for 15% -> 1% of each run, Pallas kernels for 0% -> 0%
where the time goes in v2:
time: 134 us; the launch traced here: 133 us
  blocking collectives  81.6 us (61%)
  waiting for transfers between devices  22.1 us (16%)
  Pallas kernels  20.8 us (16%)
  starting transfers between devices  5.95 us (4%)
  local copies, waits for them, and re-layouts  2.02 us (2%)
    all_to_all x1, blocking collectives, body(): lax.all_to_all(words, ('stn', 'tm'), split_axis=0, concat_axis=0, tiled=T...  81.6 us
    all_to_all x1, waiting for transfers between devices, body(): lax.all_to_all(deal(samples), 'tm', split_axis=0, concat_axis=0, tiled=True)  22.1 us
    pallas_call x1, Pallas kernels, channelize(): pl.pallas_call(functools.partial(channelize_kernel, frames), out_shape=ja...  13.7 us
    all_to_all x1, starting transfers between devices, body(): lax.all_to_all(deal(samples), 'tm', split_axis=0, concat_axis=0, tiled=True)  5.95 us
    pallas_call x1, Pallas kernels, correlate(): pl.pallas_call(functools.partial(correlate_kernel, normalizer), grid=(4,)...  4.22 us
    pallas_call x1, Pallas kernels, deal(): pl.pallas_call(deal_kernel, grid=(components, steps), out_shape=jax.Shape...  2.91 us
  transfers between devices with their start and end apart: 1, of which 1 were waited for; matrix products, arithmetic and copies ran while one was open for 1% of the time, Pallas kernels for 0%

profile of v2, /device:TPU:1, one launch (start us, length us, event | category | flops | bytes accessed | tf_op | source)
XLA Modules:
  0.0 133.3 jit_solution(12834536606494821356)
XLA Ops:
  0.0 2.9 %deal.1 = bf16[8,960,128]{2,1,0:T(8,128)(2,1)} custom-call(bf16[2,8,61440]{2,1,0:T(8,128)(2,1)} %in_ref.1), custom_call_target="tpu_custom_call" | custom-call | tf_op jit(solution)/shard_map/deal/pallas_call | solution.py:90
  2.9 5.9 %all-to-all-start = ((bf16[8,960,128]{2,1,0:T(8,128)(2,1)}), bf16[8,960,128]{2,1,0:T(8,128)(2,1)S(1)}, u32[]{:S(2)}, u32[]{:S(2)}) async-start(bf16[8,960,128]{2,1,0:T(8,128)(2,1)} %deal.1), calls=%async_computation | async-start | bytes 3932160 | tf_op jit(solution)/shard_map/all_to_all | solution.py:272
  8.9 0.9 multiply_reduce_fusion
  9.7 0.1 mul.12
  9.8 0.7 copy.7
  10.5 22.1 %all-to-all-done.in_ref = bf16[8,960,128]{2,1,0:T(8,128)(2,1)S(1)} async-done(((bf16[8,960,128]{2,1,0:T(8,128)(2,1)}), bf16[8,960,128]{2,1,0:T(8,128)(2,1)S(1)}, u32[]{:S(2)}, u32[]{:S(2)}) %all-to-all-start) | async-done | bytes 1966112 | tf_op jit(solution)/shard_map/all_to_all | solution.py:272
  32.6 0.0 copy-start
  32.6 1.3 copy-done
  33.9 13.7 %channelize.1 = bf16[4096,128]{1,0:T(8,128)(2,1)} custom-call(bf16[8,960,128]{2,1,0:T(8,128)(2,1)} %copy-done, bf16[16,4096]{1,0:T(8,128)(2,1)} %taps_ref.1, f32[2,16,256]{2,1,0:T(8,128)} %constant.20.clone.twist_ref, bf16[512,512]{1,0:T(8,128)(2,1)} %constant.23.table_ref, f32[16,128]{1,0:T(8,128)} %bitcast.5), custom_call_target="tpu_custom_call" | custom-call | tf_op jit(solution)/shard_map/channelize/pallas_call | solution.py:192
  47.5 81.6 %all_to_all.10 = bf16[512,8,128]{2,1,0:T(8,128)(2,1)} all-to-all(bf16[512,8,128]{2,1,0:T(8,128)(2,1)} %bitcast.3), channel_id=1, replica_groups=mesh['stn'=64,'tm'=8] {'stn','tm'}, dimensions={0} | all-to-all | bytes 2097152 | tf_op jit(solution)/shard_map/all_to_all | solution.py:275
  129.1 4.2 %correlate.1 = bf16[4,512,512]{2,1,0:T(8,128)(2,1)} custom-call(bf16[4096,128]{1,0:T(8,128)(2,1)} %bitcast.4), custom_call_target="tpu_custom_call" | custom-call | tf_op jit(solution)/shard_map/correlate/pallas_call | solution.py:249
Async XLA Ops:
  2.9 29.7 %all-to-all-start = ((bf16[8,960,128]{2,1,0:T(8,128)(2,1)}), bf16[8,960,128]{2,1,0:T(8,128)(2,1)S(1)}, u32[]{:S(2)}, u32[]{:S(2)}) async-start(bf16[8,960,128]{2,1,0:T(8,128)(2,1)} %deal.1), calls=%async_computation | async-start | bytes 3932160 | tf_op jit(solution)/shard_map/all_to_all | solution.py:272
  32.6 1.3 copy-start

commit v3 on v1

v3 whole, which is shorter than its diff:
```python
import functools
import math

import jax
import jax.numpy as jnp
import numpy as np
from jax import lax
from jax.experimental import pallas as pl
from jax.experimental.pallas import tpu as pltpu
from jax.sharding import PartitionSpec as P

LANES = 128
RADIX = 16
FINE = 256
KEPT = 128
SLOT = 16
VMEM_LIMIT = 28 * 2**20


def second_table():
    fine = np.arange(FINE)
    outputs = np.arange(KEPT) + (FINE - KEPT) // 2
    angle = 2.0 * np.pi * ((outputs[:, None] * fine[None, :]) % FINE) / FINE
    cosine, sine = np.cos(angle), np.sin(angle)
    return np.block([[cosine, sine], [-sine, cosine]]).T


def twist_table():
    angle = 2.0 * np.pi * (np.arange(RADIX)[:, None] * np.arange(FINE)[None, :]) / (RADIX * FINE)
    return np.stack([np.cos(angle), -np.sin(angle)]).astype(np.float32)


def add(a, b):
    return (a[0] + b[0], a[1] + b[1])


def sub(a, b):
    return (a[0] - b[0], a[1] - b[1])


def turn(a):
    return (a[1], -a[0])


def four(a, b, c, d):
    even, odd = add(a, c), sub(a, c)
    both, rest = add(b, d), turn(sub(b, d))
    return (add(even, both), add(odd, rest), sub(even, both), sub(odd, rest))


def times_root(a, power):
    if power == 0:
        return a
    if power == 4:
        return turn(a)
    half = math.sqrt(0.5)
    if power == 2:
        return ((a[0] + a[1]) * half, (a[1] - a[0]) * half)
    if power == 6:
        return ((a[1] - a[0]) * half, -(a[0] + a[1]) * half)
    cosine, sine = math.cos(2 * math.pi * power / 16), math.sin(2 * math.pi * power / 16)
    return (a[0] * cosine + a[1] * sine, a[1] * cosine - a[0] * sine)


def sixteen(points):
    columns = [four(points[b], points[4 + b], points[8 + b], points[12 + b]) for b in range(4)]
    out = [None] * 16
    for low in range(4):
        mixed = four(*[times_root(columns[b][low], b * low) for b in range(4)])
        for high in range(4):
            out[low + 4 * high] = mixed[high]
    return out


def analyze(plan, sources, taps_ref, keep_ref, twist_ref, table_ref, factor_ref, filt, rows, store):
    tap_count, length = taps_ref.shape
    chunks = length // LANES
    inputs = factor_ref.shape[1]
    slots = 8

    def filter_chunk(chunk, _):
        lanes = pl.ds(pl.multiple_of(chunk * LANES, LANES), LANES)
        weights = taps_ref[:, lanes].astype(jnp.float32)
        taps = [jnp.broadcast_to(weights[p : p + 1], (inputs, LANES)) for p in range(tap_count)]
        keep = keep_ref[...]
        window, first_later = sources
        for comp in range(2):
            sums = {f: [None, None] for f in plan}
            for v in range(min(plan), max(plan) + tap_count):
                users = [f for f in plan if f <= v < f + tap_count]
                if not users:
                    continue
                ref, u = window[v]
                at = pl.multiple_of(u * length + chunk * LANES, LANES)
                block = ref[comp, :, pl.ds(at, LANES)].astype(jnp.float32)
                later = int(v >= first_later)
                for f in users:
                    term = taps[v - f] * block
                    held = sums[f][later]
                    sums[f][later] = term if held is None else held + term
            for slot, f in enumerate(plan):
                early, late = sums[f]
                filt[comp, chunk, slot] = early if late is None else early * keep + late
        return 0

    lax.fori_loop(0, chunks, filter_chunk, 0)

    def first_transform(slot, _):
        for half in range(2):
            points = [(filt[0, 2 * n + half, slot], filt[1, 2 * n + half, slot]) for n in range(RADIX)]
            mixed = sixteen(points)
            for k1 in range(RADIX):
                real, imag = mixed[k1]
                if k1:
                    cosine = twist_ref[0, pl.ds(k1, 1), pl.ds(half * LANES, LANES)]
                    sine = twist_ref[1, pl.ds(k1, 1), pl.ds(half * LANES, LANES)]
                    real, imag = real * cosine - imag * sine, imag * cosine + real * sine
                at = pl.ds(pl.multiple_of((k1 * slots + slot) * inputs, inputs), inputs)
                rows[half, at, :] = real
                rows[2 + half, at, :] = imag
        return 0

    lax.fori_loop(0, len(plan), first_transform, 0)
    for slot in range(len(plan), slots):
        for q in range(4):
            for k1 in range(RADIX):
                at = (k1 * slots + slot) * inputs
                rows[q, at : at + inputs, :] = jnp.zeros((inputs, LANES), jnp.float32)

    many = 4
    count = many * slots * inputs

    def second_transform(group, _):
        span = pl.ds(pl.multiple_of(group * count, count), count)
        block = jnp.concatenate([rows[q, span, :] for q in range(4)], axis=1)
        high = block.astype(jnp.bfloat16)
        low = (block - high.astype(jnp.float32)).astype(jnp.bfloat16)
        both = jnp.dot(high, table_ref[...], preferred_element_type=jnp.float32)
        rest = jnp.dot(low, table_ref[:, : 2 * KEPT], preferred_element_type=jnp.float32)
        total = both[:, : 2 * KEPT] + both[:, 2 * KEPT :] + rest
        scale = factor_ref[pl.ds(group * many, many)][:, None]
        for comp in range(2):
            part = total[:, comp * KEPT : (comp + 1) * KEPT].reshape(many, slots, inputs, KEPT)
            part = jnp.clip(part * scale, -127.0, 127.0)
            store[comp, span, :] = part.reshape(count, KEPT)
        return 0

    lax.fori_loop(0, RADIX // many, second_transform, 0)


def window_of(own_ref, before, after, frames):
    window = [(ref, u) for ref, count in before for u in range(count)]
    window += [(own_ref, u) for u in range(frames)]
    first_later = len(window)
    window += [(ref, u) for ref, count in after for u in range(count)]
    return window, first_later


def middle_kernel(
    frames, near, far, own_ref, before_ref, after_ref, taps_ref, keep_ref, twist_ref, table_ref, factor_ref,
    out_ref, filt, rows,
):
    window, first_later = window_of(own_ref, [(None, far[0]), (before_ref, near[0])], [(after_ref, near[1])], frames)
    plan = middle_frames(near, far)
    analyze(plan, (window, first_later), taps_ref, keep_ref, twist_ref, table_ref, factor_ref, filt, rows, out_ref)


def middle_frames(near, far):
    return list(range(far[0], far[0] + near[0] + near[1]))


def outer_kernel(
    frames, near, far, own_ref, before_ref, after_ref, farther_before_ref, farther_after_ref, taps_ref, keep_ref,
    twist_ref, table_ref, factor_ref, middle_ref, out_ref, filt, rows, edge, words,
):
    window, first_later = window_of(
        own_ref,
        [(farther_before_ref, far[0]), (before_ref, near[0])],
        [(after_ref, near[1]), (farther_after_ref, far[1])],
        frames,
    )
    middle = middle_frames(near, far)
    plan = [f for f in range(frames) if f not in middle]
    analyze(plan, (window, first_later), taps_ref, keep_ref, twist_ref, table_ref, factor_ref, filt, rows, edge)
    inputs = factor_ref.shape[1]

    def arrange(high, _):
        for i in range(inputs):
            parts = []
            for comp in range(2):
                for channel in range(4):
                    at = pl.ds((high * 4 + channel) * 8 * inputs + i, 8, stride=inputs)
                    parts += [middle_ref[comp, at, :], edge[comp, at, :]]
            words[pl.ds(high * inputs + i, KEPT, stride=4 * inputs), :] = jnp.concatenate(parts, axis=0).T
        return 0

    lax.fori_loop(0, RADIX // 4, arrange, 0)

    def narrow(step, _):
        span = pl.ds(pl.multiple_of(step * 1024, 1024), 1024)
        out_ref[span, :] = words[span, :].astype(jnp.bfloat16)
        return 0

    lax.fori_loop(0, words.shape[0] // 1024, narrow, 0)


def tables():
    table = second_table()
    high = table.astype(jnp.bfloat16)
    low = (table - high.astype(np.float64)).astype(jnp.bfloat16)
    return twist_table(), jnp.concatenate([high, low], axis=1)


def scratch(inputs):
    return [
        pltpu.VMEM((2, RADIX * FINE // LANES, 8, inputs, LANES), jnp.float32),
        pltpu.VMEM((4, RADIX * 8 * inputs, LANES), jnp.float32),
    ]


def middle_frames_call(own, before, after, taps, keep, factor, frames, near, far):
    inputs = own.shape[1]
    vmem = pl.BlockSpec(memory_space=pltpu.VMEM)
    return pl.pallas_call(
        functools.partial(middle_kernel, frames, near, far),
        out_shape=jax.ShapeDtypeStruct((2, RADIX * 8 * inputs, KEPT), jnp.float32),
        in_specs=[vmem] * 8,
        out_specs=vmem,
        scratch_shapes=scratch(inputs),
        compiler_params=pltpu.CompilerParams(vmem_limit_bytes=VMEM_LIMIT),
        cost_estimate=pl.CostEstimate(flops=4 * 10**9, bytes_accessed=5 * 2**20, transcendentals=0),
        name="middle_frames",
    )(own, before, after, taps, keep, *tables(), factor)


def outer_frames_call(own, near_blocks, far_blocks, taps, keep, factor, middle, frames, near, far):
    inputs = own.shape[1]
    vmem = pl.BlockSpec(memory_space=pltpu.VMEM)
    messages = KEPT * 4 * inputs
    return pl.pallas_call(
        functools.partial(outer_kernel, frames, near, far),
        out_shape=jax.ShapeDtypeStruct((messages, LANES), jnp.bfloat16),
        in_specs=[vmem] * 11,
        out_specs=vmem,
        scratch_shapes=scratch(inputs)
        + [pltpu.VMEM((2, RADIX * 8 * inputs, KEPT), jnp.float32), pltpu.VMEM((messages, LANES), jnp.float32)],
        compiler_params=pltpu.CompilerParams(vmem_limit_bytes=VMEM_LIMIT),
        name="outer_frames",
    )(own, *near_blocks, *far_blocks, taps, keep, *tables(), factor, middle)


def correlate_kernel(normalizer, words_ref, out_ref, joined, swapped):
    channel = pl.program_id(0)
    stations, times, inputs, _ = words_ref.shape
    size = stations * inputs
    half = size // 2

    @pl.when(channel == 0)
    def _():
        some = 8
        lane = lax.broadcasted_iota(jnp.int32, (some * inputs, LANES), 1)
        sign = jnp.where(lane < LANES // 2, 1.0, -1.0)

        def trade(block, _):
            span = pl.ds(pl.multiple_of(block * some * inputs, some * inputs), some * inputs)
            for q in range(times // 4):
                held = [
                    words_ref[pl.ds(block * some, some), 4 * q + r].astype(jnp.float32).reshape(some * inputs, LANES)
                    for r in range(4)
                ]
                for bit in (1, 2):
                    shift = bit * SLOT
                    left = (lane // shift) % 2 == 0
                    for r in range(4):
                        if not r & bit:
                            x, y = held[r], held[r | bit]
                            held[r] = jnp.where(left, x, pltpu.roll(y, shift, 1))
                            held[r | bit] = jnp.where(left, pltpu.roll(x, LANES - shift, 1), y)
                for c in range(4):
                    lanes = pl.ds(q * LANES, LANES)
                    joined[c, span, lanes] = held[c].astype(jnp.bfloat16)
                    other = pltpu.roll(held[c], LANES // 2, 1) * sign
                    swapped[c, span, lanes] = other.astype(jnp.bfloat16)
            return 0

        lax.fori_loop(0, stations // some, trade, 0)

    def product(left, right):
        return lax.dot_general(
            left, right, (((1,), (1,)), ((), ())), preferred_element_type=jnp.float32
        )

    first, second = joined[channel, :half], joined[channel, half:]
    first_other, second_other = swapped[channel, :half], swapped[channel, half:]
    lower = lax.broadcasted_iota(jnp.int32, (half, half), 0) >= lax.broadcasted_iota(
        jnp.int32, (half, half), 1
    )

    def finish(values):
        return (values * normalizer).astype(jnp.bfloat16)

    out_ref[0, :half, :half] = finish(jnp.where(lower, product(first, first), product(first_other, first)))
    out_ref[0, half:, :half] = finish(product(second, first))
    out_ref[0, :half, half:] = finish(product(first_other, second))
    out_ref[0, half:, half:] = finish(
        jnp.where(lower, product(second, second), product(second_other, second))
    )


def correlate(words, normalizer):
    stations, times, inputs, _ = words.shape
    size = stations * inputs
    return pl.pallas_call(
        functools.partial(correlate_kernel, normalizer),
        grid=(4,),
        out_shape=jax.ShapeDtypeStruct((4, size, size), jnp.bfloat16),
        in_specs=[pl.BlockSpec(words.shape, lambda c: (0, 0, 0, 0))],
        out_specs=pl.BlockSpec((1, size, size), lambda c: (c, 0, 0)),
        scratch_shapes=[pltpu.VMEM((4, size, times * 2 * SLOT), jnp.bfloat16)] * 2,
        compiler_params=pltpu.CompilerParams(vmem_limit_bytes=VMEM_LIMIT),
        name="correlate",
    )(words)


def band_factor(scales, rescale):
    factor = (scales.astype(jnp.float32) * rescale).reshape(-1, KEPT, RADIX)
    return jnp.transpose(factor, (2, 0, 1))


def body(samples, taps, scales):
    length = taps.shape[1]
    inputs = samples.shape[1]
    frames = samples.shape[2] // length
    stations, times = lax.axis_size("stn"), lax.axis_size("tm")
    near, far = (4, 4), (4, 3)
    cut = frames - near[0]
    onward = [(i, i + 1) for i in range(times - 1)]
    backward = [(i, (i - 1) % times) for i in range(times)]

    def blocks(start, stop):
        return samples[:, :, start * length : stop * length]

    near_blocks = (
        lax.ppermute(blocks(cut, frames), "tm", onward),
        lax.ppermute(blocks(0, near[1]), "tm", backward),
    )
    far_blocks = (
        lax.ppermute(blocks(cut - far[0], cut), "tm", onward),
        lax.ppermute(blocks(near[1], near[1] + far[1]), "tm", backward),
    )
    keep = jnp.where(lax.axis_index("tm") == times - 1, 0.0, 1.0)
    keep = jnp.broadcast_to(keep.astype(jnp.float32), (inputs, LANES))
    factor = band_factor(scales, 16.0 / math.sqrt(length))
    middle = middle_frames_call(samples, *near_blocks, taps, keep, factor, frames, near, far)
    words = outer_frames_call(samples, near_blocks, far_blocks, taps, keep, factor, middle, frames, near, far)
    words = words.reshape(stations * times, inputs, LANES)
    words = lax.all_to_all(words, ("stn", "tm"), split_axis=0, concat_axis=0, tiled=True)
    words = words.reshape(stations, times, inputs, LANES)
    return correlate(words, 1.0 / (2.0 * frames * times * length))


def solution(mesh):
    placed = (P(None, "stn", "tm"), P(), P("stn", None))
    return jax.shard_map(
        body, mesh=mesh, in_specs=placed, out_specs=P(("stn", "tm"), None, None), check_vma=False
    )
```

time: 155 us -> 130 us (0.84)
  waiting for transfers between devices: 15.4 us -> 0.01 us
  local copies, waits for them, and re-layouts: 22.7 us -> 9.69 us
  starting transfers between devices: 4.15 us -> 13.8 us
  Pallas kernels: 24.2 us -> 17.6 us
    ppermute x1 -> x4, waiting for transfers between devices: 15.4 us -> 0.01 us  [the longest x1 0.01 us: body(): lax.ppermute(blocks(0, near[1]), 'tm', backward)]
    ppermute x1 -> x4, starting transfers between devices: 4.15 us -> 13.8 us  [the longest x1 6.39 us: body(): lax.ppermute(blocks(0, near[1]), 'tm', backward)]
    reshape x1 -> x2, local copies, waits for them, and re-layouts: 12 us -> 3.68 us  [band_factor(): factor = (scales.astype(jnp.float32) * rescale).reshape(-1, KEPT, RADIX)]
    broadcast_in_dim x1, local copies, waits for them, and re-layouts: 5.97 us -> 0.01 us  [body(): keep = jnp.broadcast_to(keep.astype(jnp.float32), (inputs, LANES))]
    pallas_call x1 -> x2, Pallas kernels: 17.5 us -> 12.7 us  [the longest x1 7.76 us: outer_frames_call(): pl.pallas_call(functools.partial(outer_kernel, frames, near, far), out_sh...]
    slice x0 -> x2, local copies, waits for them, and re-layouts: none -> 3.5 us  [blocks(): return samples[:, :, start * length:stop * length]]
    transpose x1 -> x0, local copies, waits for them, and re-layouts: 3.21 us -> none  [message_factor(): factor = jnp.transpose(factor.reshape(inputs, band // 4, 4), (1, 0, 2))]
    pallas_call x1, Pallas kernels: 6.65 us -> 4.92 us  [correlate(): pl.pallas_call(functools.partial(correlate_kernel, normalizer), grid=(4,)...]
  transfers between devices with their start and end apart: 1 -> 4, of which waited for: 1 -> 0; matrix products, arithmetic and copies ran while one was open for 15% -> 4% of each run, Pallas kernels for 0% -> 4%
where the time goes in v3:
time: 130 us; the launch traced here: 129 us
  blocking collectives  87.3 us (67%)
  Pallas kernels  17.6 us (14%)
  starting transfers between devices  13.8 us (11%)
  local copies, waits for them, and re-layouts  9.69 us (7%)
    all_to_all x1, blocking collectives, body(): lax.all_to_all(words, ('stn', 'tm'), split_axis=0, concat_axis=0, tiled=T...  87.3 us
    pallas_call x1, Pallas kernels, outer_frames_call(): pl.pallas_call(functools.partial(outer_kernel, frames, near, far), out_sh...  7.76 us
    ppermute x1, starting transfers between devices, body(): lax.ppermute(blocks(0, near[1]), 'tm', backward)  6.39 us
    pallas_call x1, Pallas kernels, middle_frames_call(): pl.pallas_call(functools.partial(middle_kernel, frames, near, far), out_s...  4.97 us
    pallas_call x1, Pallas kernels, correlate(): pl.pallas_call(functools.partial(correlate_kernel, normalizer), grid=(4,)...  4.92 us
    ppermute x1, starting transfers between devices, body(): lax.ppermute(blocks(cut - far[0], cut), 'tm', onward)  3.74 us
    reshape x2, local copies, waits for them, and re-layouts, band_factor(): factor = (scales.astype(jnp.float32) * rescale).reshape(-1, KEPT, RADIX)  3.68 us
    slice x2, local copies, waits for them, and re-layouts, blocks(): return samples[:, :, start * length:stop * length]  3.5 us
  transfers between devices with their start and end apart: 4, of which 0 were waited for; matrix products, arithmetic and copies ran while one was open for 4% of the time, Pallas kernels for 4%

profile of v3, /device:TPU:1, one launch (start us, length us, event | category | flops | bytes accessed | tf_op | source)
XLA Modules:
  0.0 129.2 jit_solution(8192148045445061773)
XLA Ops:
  0.0 0.0 copy-start.1
  0.0 0.0 copy-start
  0.0 0.0 copy-start.5
  0.0 2.7 %fusion = (bf16[2,8,16384]{2,1,0:T(8,128)(2,1)}, bf16[2,8,16384]{2,1,0:T(8,128)(2,1)}, bf16[2,8,16384]{2,1,0:T(8,128)(2,1)}) fusion(bf16[2,8,61440]{2,1,0:T(8,128)(2,1)} %own_ref.3), kind=kLoop, calls=%fused_computation.1 | loop fusion | bytes 3145728 | tf_op jit(solution)/shard_map/slice | solution.py:341
  2.7 6.4 %collective-permute-start.1 = (bf16[2,8,16384]{2,1,0:T(8,128)(2,1)}, bf16[2,8,16384]{2,1,0:T(8,128)(2,1)S(1)}, u32[]{:S(2)}, u32[]{:S(2)}) collective-permute-start(bf16[2,8,16384]{2,1,0:T(8,128)(2,1)} %get-tuple-element.6), channel_id=1, source_target_pairs={{0,7},{1,0},{2,1},{3,2},{4,3},{5,4},{6,5},{7,6},{8,15},{9,8},{10,9... | collective-permute-start | bytes 1572872 | tf_op jit(solution)/shard_map/ppermute | solution.py:345
  9.1 1.3 %collective-permute-start = (bf16[2,8,16384]{2,1,0:T(8,128)(2,1)}, bf16[2,8,16384]{2,1,0:T(8,128)(2,1)S(1)}, u32[]{:S(2)}, u32[]{:S(2)}) collective-permute-start(bf16[2,8,16384]{2,1,0:T(8,128)(2,1)} %get-tuple-element.7), channel_id=1, source_target_pairs={{0,1},{1,2},{2,3},{3,4},{4,5},{5,6},{6,7},{8,9},{9,10},{10,11},{11... | collective-permute-start | bytes 1572872 | tf_op jit(solution)/shard_map/ppermute | solution.py:344
  10.5 0.0 copy-done
  10.5 0.8 slice.15
  11.2 2.3 %collective-permute-start.3 = (bf16[2,8,12288]{2,1,0:T(8,128)(2,1)}, bf16[2,8,12288]{2,1,0:T(8,128)(2,1)}, u32[]{:S(2)}, u32[]{:S(2)}) collective-permute-start(bf16[2,8,12288]{2,1,0:T(8,128)(2,1)} %slice.15), channel_id=1, source_target_pairs={{0,7},{1,0},{2,1},{3,2},{4,3},{5,4},{6,5},{7,6},{8,15},{9,8},{10,9... | collective-permute-start | bytes 1179656 | tf_op jit(solution)/shard_map/ppermute | solution.py:349
  13.6 3.7 %collective-permute-start.2 = (bf16[2,8,16384]{2,1,0:T(8,128)(2,1)}, bf16[2,8,16384]{2,1,0:T(8,128)(2,1)}, u32[]{:S(2)}, u32[]{:S(2)}) collective-permute-start(bf16[2,8,16384]{2,1,0:T(8,128)(2,1)} %get-tuple-element.5), channel_id=1, source_target_pairs={{0,1},{1,2},{2,3},{3,4},{4,5},{5,6},{6,7},{8,9},{9,10},{10,11},{11... | collective-permute-start | bytes 1572872 | tf_op jit(solution)/shard_map/ppermute | solution.py:348
  17.3 0.0 copy-done.5
  17.3 0.6 convert_multiply_fusion
  18.0 1.8 %reshape.9 = f32[8,128,16]{2,1,0:T(8,128)} reshape(f32[8,2048]{1,0:T(8,128)} %convert_multiply_fusion) | data formatting | bytes 131072 | tf_op jit(solution)/shard_map/reshape | solution.py:326
  19.8 1.8 %copy.10 = f32[8,128,16]{1,0,2:T(8,128)} copy(f32[8,128,16]{2,1,0:T(8,128)} %reshape.9) | data formatting | bytes 131072 | tf_op jit(solution)/shard_map/reshape | solution.py:326
  21.6 0.0 collective-permute-done.1.after_ref
  21.6 0.0 collective-permute-done.before_ref
  21.7 0.0 copy-done.1
  21.7 0.0 copy-start.2
  21.7 0.8 copy-done.2
  22.5 0.0 copy-start.3
  22.5 0.9 copy-done.3
  23.4 0.0 copy-start.4
  23.4 0.8 copy-done.4
  24.2 5.0 %middle_frames.1.middle_ref = f32[2,1024,128]{2,1,0:T(8,128)S(1)} custom-call(bf16[2,8,61440]{2,1,0:T(8,128)(2,1)S(1)} %copy-done, bf16[2,8,16384]{2,1,0:T(8,128)(2,1)S(1)} %collective-permute-done.before_ref, bf16[2,8,16384]{2,1,0:T(8,128)(2,1)S(1)} %collective-permute-done.1.after_ref, bf16[16,4096]{1,0:T(8,128)(2,1)S(1)} %copy-done.3, ...), custom_call_target="tpu_custom_call" | custom-call | flops 4000000000 | bytes 5242880 | tf_op jit(solution)/shard_map/middle_frames/pallas_call | solution.py:224
  29.1 0.0 collective-permute-done.3.farther_after_ref
  29.2 0.0 collective-permute-done.2.farther_before_ref
  29.2 7.8 %outer_frames.1 = bf16[4096,128]{1,0:T(8,128)(2,1)S(1)} custom-call(bf16[2,8,61440]{2,1,0:T(8,128)(2,1)S(1)} %copy-done, bf16[2,8,16384]{2,1,0:T(8,128)(2,1)S(1)} %collective-permute-done.before_ref, bf16[2,8,16384]{2,1,0:T(8,128)(2,1)S(1)} %collective-permute-done.1.after_ref, bf16[2,8,16384]{2,1,0:T(8,128)(2,1)} %collective-permute-done.2.farther_before_ref, ...), custom_call_target="tpu_custom_call" | custom-call | tf_op jit(solution)/shard_map/outer_frames/pallas_call | solution.py:240
  36.9 87.3 %all_to_all.5 = bf16[512,8,128]{2,1,0:T(8,128)(2,1)S(1)} all-to-all(bf16[512,8,128]{2,1,0:T(8,128)(2,1)S(1)} %bitcast.4), channel_id=1, replica_groups=mesh['stn'=64,'tm'=8] {'stn','tm'}, dimensions={0} | all-to-all | bytes 2097152 | tf_op jit(solution)/shard_map/all_to_all | solution.py:357
  124.2 4.9 %correlate.1 = bf16[4,512,512]{2,1,0:T(8,128)(2,1)} custom-call(bf16[64,8,8,128]{3,2,1,0:T(8,128)(2,1)S(1)} %bitcast.3), custom_call_target="tpu_custom_call" | custom-call | tf_op jit(solution)/shard_map/correlate/pallas_call | solution.py:313
  (1 shorter events, 0.0 us)
Async XLA Ops:
  0.0 21.7 %copy-start.1 = (bf16[512,512]{1,0:T(8,128)(2,1)S(1)}, bf16[512,512]{1,0:T(8,128)(2,1)}, u32[]{:S(2)}) copy-start(bf16[512,512]{1,0:T(8,128)(2,1)} %constant.23.table_ref) | copy-start | bytes 1572868
  0.0 10.5 %copy-start = (bf16[2,8,61440]{2,1,0:T(8,128)(2,1)S(1)}, bf16[2,8,61440]{2,1,0:T(8,128)(2,1)}, u32[]{:S(2)}) copy-start(bf16[2,8,61440]{2,1,0:T(8,128)(2,1)} %own_ref.3) | copy-start | bytes 5898244
  0.0 17.3 %copy-start.5 = (s32[8,2048]{1,0:T(8,128)S(1)}, s32[8,2048]{1,0:T(8,128)}, u32[]{:S(2)}) copy-start(s32[8,2048]{1,0:T(8,128)} %param.11) | copy-start | bytes 196612
  2.7 18.9 %collective-permute-start.1 = (bf16[2,8,16384]{2,1,0:T(8,128)(2,1)}, bf16[2,8,16384]{2,1,0:T(8,128)(2,1)S(1)}, u32[]{:S(2)}, u32[]{:S(2)}) collective-permute-start(bf16[2,8,16384]{2,1,0:T(8,128)(2,1)} %get-tuple-element.6), channel_id=1, source_target_pairs={{0,7},{1,0},{2,1},{3,2},{4,3},{5,4},{6,5},{7,6},{8,15},{9,8},{10,9... | collective-permute-start | bytes 1572872 | tf_op jit(solution)/shard_map/ppermute | solution.py:345
  9.1 12.5 %collective-permute-start = (bf16[2,8,16384]{2,1,0:T(8,128)(2,1)}, bf16[2,8,16384]{2,1,0:T(8,128)(2,1)S(1)}, u32[]{:S(2)}, u32[]{:S(2)}) collective-permute-start(bf16[2,8,16384]{2,1,0:T(8,128)(2,1)} %get-tuple-element.7), channel_id=1, source_target_pairs={{0,1},{1,2},{2,3},{3,4},{4,5},{5,6},{6,7},{8,9},{9,10},{10,11},{11... | collective-permute-start | bytes 1572872 | tf_op jit(solution)/shard_map/ppermute | solution.py:344
  11.2 17.9 %collective-permute-start.3 = (bf16[2,8,12288]{2,1,0:T(8,128)(2,1)}, bf16[2,8,12288]{2,1,0:T(8,128)(2,1)}, u32[]{:S(2)}, u32[]{:S(2)}) collective-permute-start(bf16[2,8,12288]{2,1,0:T(8,128)(2,1)} %slice.15), channel_id=1, source_target_pairs={{0,7},{1,0},{2,1},{3,2},{4,3},{5,4},{6,5},{7,6},{8,15},{9,8},{10,9... | collective-permute-start | bytes 1179656 | tf_op jit(solution)/shard_map/ppermute | solution.py:349
  13.6 15.6 %collective-permute-start.2 = (bf16[2,8,16384]{2,1,0:T(8,128)(2,1)}, bf16[2,8,16384]{2,1,0:T(8,128)(2,1)}, u32[]{:S(2)}, u32[]{:S(2)}) collective-permute-start(bf16[2,8,16384]{2,1,0:T(8,128)(2,1)} %get-tuple-element.5), channel_id=1, source_target_pairs={{0,1},{1,2},{2,3},{3,4},{4,5},{5,6},{6,7},{8,9},{9,10},{10,11},{11... | collective-permute-start | bytes 1572872 | tf_op jit(solution)/shard_map/ppermute | solution.py:348
  21.7 0.8 copy-start.2
  22.5 0.9 copy-start.3
  23.4 0.8 copy-start.4

commit v4 on v3

--- a/solution.py
+++ b/solution.py
@@ -72,38 +72,46 @@
     return out
 
 
-def analyze(plan, sources, taps_ref, keep_ref, twist_ref, table_ref, factor_ref, filt, rows, store):
+def filter_blocks(plan, fresh, sources, taps_ref, keep_ref, out_ref, begun_ref=None):
     tap_count, length = taps_ref.shape
-    chunks = length // LANES
-    inputs = factor_ref.shape[1]
-    slots = 8
+    inputs = keep_ref.shape[0]
+    window, first_later = sources
 
     def filter_chunk(chunk, _):
         lanes = pl.ds(pl.multiple_of(chunk * LANES, LANES), LANES)
-        weights = taps_ref[:, lanes].astype(jnp.float32)
+        weights = taps_ref[:, lanes]
         taps = [jnp.broadcast_to(weights[p : p + 1], (inputs, LANES)) for p in range(tap_count)]
         keep = keep_ref[...]
-        window, first_later = sources
         for comp in range(2):
             sums = {f: [None, None] for f in plan}
-            for v in range(min(plan), max(plan) + tap_count):
+            if begun_ref is not None:
+                sums = {f: [None, begun_ref[comp, chunk, slot]] for slot, f in enumerate(plan)}
+            for v in fresh:
                 users = [f for f in plan if f <= v < f + tap_count]
                 if not users:
                     continue
                 ref, u = window[v]
                 at = pl.multiple_of(u * length + chunk * LANES, LANES)
                 block = ref[comp, :, pl.ds(at, LANES)].astype(jnp.float32)
-                later = int(v >= first_later)
                 for f in users:
+                    later = int(begun_ref is not None or v >= first_later or f < first_later - tap_count + 1)
                     term = taps[v - f] * block
                     held = sums[f][later]
                     sums[f][later] = term if held is None else held + term
             for slot, f in enumerate(plan):
                 early, late = sums[f]
-                filt[comp, chunk, slot] = early if late is None else early * keep + late
+                if early is not None:
+                    early = early * keep
+                    late = early if late is None else late + early
+                out_ref[comp, chunk, slot] = late
         return 0
 
-    lax.fori_loop(0, chunks, filter_chunk, 0)
+    lax.fori_loop(0, length // LANES, filter_chunk, 0)
+
+
+def transform(count_used, twist_ref, table_ref, factor_ref, filt, rows, store):
+    inputs = factor_ref.shape[1]
+    slots = 8
 
     def first_transform(slot, _):
         for half in range(2):
@@ -120,68 +128,93 @@
                 rows[2 + half, at, :] = imag
         return 0
 
-    lax.fori_loop(0, len(plan), first_transform, 0)
-    for slot in range(len(plan), slots):
+    lax.fori_loop(0, count_used, first_transform, 0, unroll=True)
+    for slot in range(count_used, slots):
         for q in range(4):
             for k1 in range(RADIX):
                 at = (k1 * slots + slot) * inputs
                 rows[q, at : at + inputs, :] = jnp.zeros((inputs, LANES), jnp.float32)
 
-    many = 4
-    count = many * slots * inputs
-
-    def second_transform(group, _):
-        span = pl.ds(pl.multiple_of(group * count, count), count)
-        block = jnp.concatenate([rows[q, span, :] for q in range(4)], axis=1)
-        high = block.astype(jnp.bfloat16)
-        low = (block - high.astype(jnp.float32)).astype(jnp.bfloat16)
-        both = jnp.dot(high, table_ref[...], preferred_element_type=jnp.float32)
-        rest = jnp.dot(low, table_ref[:, : 2 * KEPT], preferred_element_type=jnp.float32)
-        total = both[:, : 2 * KEPT] + both[:, 2 * KEPT :] + rest
-        scale = factor_ref[pl.ds(group * many, many)][:, None]
-        for comp in range(2):
-            part = total[:, comp * KEPT : (comp + 1) * KEPT].reshape(many, slots, inputs, KEPT)
-            part = jnp.clip(part * scale, -127.0, 127.0)
-            store[comp, span, :] = part.reshape(count, KEPT)
-        return 0
-
-    lax.fori_loop(0, RADIX // many, second_transform, 0)
-
-
-def window_of(own_ref, before, after, frames):
-    window = [(ref, u) for ref, count in before for u in range(count)]
-    window += [(own_ref, u) for u in range(frames)]
-    first_later = len(window)
-    window += [(ref, u) for ref, count in after for u in range(count)]
-    return window, first_later
+    block = jnp.concatenate([rows[q] for q in range(4)], axis=1)
+    high = block.astype(jnp.bfloat16)
+    low = (block - high.astype(jnp.float32)).astype(jnp.bfloat16)
+    both = jnp.dot(high, table_ref[...], preferred_element_type=jnp.float32)
+    rest = jnp.dot(low, table_ref[:, : 2 * KEPT], preferred_element_type=jnp.float32)
+    total = both[:, : 2 * KEPT] + both[:, 2 * KEPT :] + rest
+    scale = factor_ref[...][:, None]
+    for comp in range(2):
+        part = total[:, comp * KEPT : (comp + 1) * KEPT].reshape(RADIX, slots, inputs, KEPT)
+        store[comp] = jnp.clip(part * scale, -127.0, 127.0).reshape(-1, KEPT)
+
+
+def split_frames(frames, near, far):
+    middle = range(far[0], far[0] + near[0] + near[1])
+    return list(middle), [f for f in range(frames) if f not in middle]
+
+
+def window_of(frames, near, far, refs):
+    far_before, before, own, after, far_after = refs
+    counts = (far[0], near[0], frames, near[1], far[1])
+    window = [(ref, u) for ref, count in zip(refs, counts) for u in range(count)]
+    return window, far[0] + near[0] + frames
+
+
+def given(window):
+    return [v for v, (ref, _) in enumerate(window) if ref is not None]
+
+
+def own_kernel(
+    frames, near, far, rescale, own_ref, taps_ref, keep_ref, scales_ref, order_ref, twist_ref,
+    middle_ref, outer_ref, factor_ref, wide_taps_ref, same_twist_ref,
+):
+    inputs = scales_ref.shape[0]
+    blocks = scales_ref.shape[1] // LANES
+    part = LANES // blocks
+    values = scales_ref[...].astype(jnp.float32) * rescale
+    stacked = jnp.concatenate([values[:, b * LANES : (b + 1) * LANES] for b in range(blocks)], axis=0)
+    stacked = jnp.dot(stacked.astype(jnp.bfloat16), order_ref[...], preferred_element_type=jnp.float32)
+    held = [stacked[b * inputs : (b + 1) * inputs] for b in range(blocks)]
+    lane = lax.broadcasted_iota(jnp.int32, (inputs, LANES), 1)
+    bit = 1
+    while bit < blocks:
+        shift = bit * part
+        left = (lane // shift) % 2 == 0
+        for b in range(blocks):
+            if not b & bit:
+                x, y = held[b], held[b | bit]
+                held[b] = jnp.where(left, x, pltpu.roll(y, shift, 1))
+                held[b | bit] = jnp.where(left, pltpu.roll(x, LANES - shift, 1), y)
+        bit *= 2
+    for k1 in range(blocks):
+        factor_ref[k1] = held[k1]
+    wide_taps_ref[...] = taps_ref[...].astype(jnp.float32)
+    same_twist_ref[...] = twist_ref[...]
+
+    sources = window_of(frames, near, far, (None, None, own_ref, None, None))
+    for plan, out_ref in zip(split_frames(frames, near, far), (middle_ref, outer_ref)):
+        filter_blocks(plan, given(sources[0]), sources, wide_taps_ref, keep_ref, out_ref)
 
 
 def middle_kernel(
-    frames, near, far, own_ref, before_ref, after_ref, taps_ref, keep_ref, twist_ref, table_ref, factor_ref,
-    out_ref, filt, rows,
+    frames, near, far, before_ref, after_ref, taps_ref, keep_ref, twist_ref, table_ref, factor_ref, begun_ref,
+    outer_begun_ref, out_ref, outer_ref, filt, rows,
 ):
-    window, first_later = window_of(own_ref, [(None, far[0]), (before_ref, near[0])], [(after_ref, near[1])], frames)
-    plan = middle_frames(near, far)
-    analyze(plan, (window, first_later), taps_ref, keep_ref, twist_ref, table_ref, factor_ref, filt, rows, out_ref)
-
-
-def middle_frames(near, far):
-    return list(range(far[0], far[0] + near[0] + near[1]))
+    sources = window_of(frames, near, far, (None, before_ref, None, after_ref, None))
+    middle, outer = split_frames(frames, near, far)
+    fresh = given(sources[0])
+    filter_blocks(middle, fresh, sources, taps_ref, keep_ref, filt, begun_ref)
+    transform(len(middle), twist_ref, table_ref, factor_ref, filt, rows, out_ref)
+    filter_blocks(outer, fresh, sources, taps_ref, keep_ref, outer_ref, outer_begun_ref)
 
 
 def outer_kernel(
-    frames, near, far, own_ref, before_ref, after_ref, farther_before_ref, farther_after_ref, taps_ref, keep_ref,
-    twist_ref, table_ref, factor_ref, middle_ref, out_ref, filt, rows, edge, words,
+    frames, near, far, before_ref, after_ref, taps_ref, keep_ref, twist_ref, table_ref, factor_ref, middle_ref,
+    begun_ref, out_ref, filt, rows, edge, words,
 ):
-    window, first_later = window_of(
-        own_ref,
-        [(farther_before_ref, far[0]), (before_ref, near[0])],
-        [(after_ref, near[1]), (farther_after_ref, far[1])],
-        frames,
-    )
-    middle = middle_frames(near, far)
-    plan = [f for f in range(frames) if f not in middle]
-    analyze(plan, (window, first_later), taps_ref, keep_ref, twist_ref, table_ref, factor_ref, filt, rows, edge)
+    sources = window_of(frames, near, far, (before_ref, None, None, None, after_ref))
+    _, plan = split_frames(frames, near, far)
+    filter_blocks(plan, given(sources[0]), sources, taps_ref, keep_ref, filt, begun_ref)
+    transform(len(plan), twist_ref, table_ref, factor_ref, filt, rows, edge)
     inputs = factor_ref.shape[1]
 
     def arrange(high, _):
@@ -194,21 +227,21 @@
             words[pl.ds(high * inputs + i, KEPT, stride=4 * inputs), :] = jnp.concatenate(parts, axis=0).T
         return 0
 
-    lax.fori_loop(0, RADIX // 4, arrange, 0)
+    lax.fori_loop(0, RADIX // 4, arrange, 0, unroll=True)
 
     def narrow(step, _):
         span = pl.ds(pl.multiple_of(step * 1024, 1024), 1024)
         out_ref[span, :] = words[span, :].astype(jnp.bfloat16)
         return 0
 
-    lax.fori_loop(0, words.shape[0] // 1024, narrow, 0)
-
-
-def tables():
+    lax.fori_loop(0, words.shape[0] // 1024, narrow, 0, unroll=True)
+
+
+def split_table():
     table = second_table()
     high = table.astype(jnp.bfloat16)
     low = (table - high.astype(np.float64)).astype(jnp.bfloat16)
-    return twist_table(), jnp.concatenate([high, low], axis=1)
+    return jnp.concatenate([high, low], axis=1)
 
 
 def scratch(inputs):
@@ -218,35 +251,90 @@
     ]
 
 
-def middle_frames_call(own, before, after, taps, keep, factor, frames, near, far):
+VMEM = pl.BlockSpec(memory_space=pltpu.VMEM)
+
+
+def sums_shape(count, chunks, inputs):
+    return jax.ShapeDtypeStruct((2, chunks, count, inputs, LANES), jnp.float32)
+
+
+def lane_order():
+    part = LANES // RADIX
+    order = np.zeros((LANES, LANES))
+    for m in range(part):
+        for k1 in range(RADIX):
+            order[m * RADIX + k1, k1 * part + m] = 1.0
+    return order.astype(jnp.bfloat16)
+
+
+def own_blocks_call(own, taps, keep, scales, rescale, frames, near, far):
     inputs = own.shape[1]
-    vmem = pl.BlockSpec(memory_space=pltpu.VMEM)
+    chunks = taps.shape[1] // LANES
+    twist = twist_table()
+    middle, outer = split_frames(frames, near, far)
+    return pl.pallas_call(
+        functools.partial(own_kernel, frames, near, far, rescale),
+        out_shape=(
+            sums_shape(len(middle), chunks, inputs),
+            sums_shape(len(outer), chunks, inputs),
+            jax.ShapeDtypeStruct((RADIX, inputs, KEPT), jnp.float32),
+            jax.ShapeDtypeStruct(taps.shape, jnp.float32),
+            jax.ShapeDtypeStruct(twist.shape, jnp.float32),
+        ),
+        in_specs=[VMEM] * 6,
+        out_specs=(VMEM,) * 5,
+        compiler_params=pltpu.CompilerParams(vmem_limit_bytes=VMEM_LIMIT),
+        cost_estimate=pl.CostEstimate(flops=3 * 10**9, bytes_accessed=6 * 2**20, transcendentals=0),
+        name="own_blocks",
+    )(own, taps, keep, scales, lane_order(), twist)
+
+
+def middle_frames_call(near_blocks, taps, keep, twist, table, factor, begun, outer_begun, frames, near, far):
+    inputs = near_blocks[0].shape[1]
     return pl.pallas_call(
         functools.partial(middle_kernel, frames, near, far),
-        out_shape=jax.ShapeDtypeStruct((2, RADIX * 8 * inputs, KEPT), jnp.float32),
-        in_specs=[vmem] * 8,
-        out_specs=vmem,
+        out_shape=(
+            jax.ShapeDtypeStruct((2, RADIX * 8 * inputs, KEPT), jnp.float32),
+            jax.ShapeDtypeStruct(outer_begun.shape, jnp.float32),
+        ),
+        in_specs=[VMEM] * 9,
+        out_specs=(VMEM, VMEM),
         scratch_shapes=scratch(inputs),
         compiler_params=pltpu.CompilerParams(vmem_limit_bytes=VMEM_LIMIT),
-        cost_estimate=pl.CostEstimate(flops=4 * 10**9, bytes_accessed=5 * 2**20, transcendentals=0),
+        cost_estimate=pl.CostEstimate(flops=3 * 10**9, bytes_accessed=5 * 2**20, transcendentals=0),
         name="middle_frames",
-    )(own, before, after, taps, keep, *tables(), factor)
-
-
-def outer_frames_call(own, near_blocks, far_blocks, taps, keep, factor, middle, frames, near, far):
-    inputs = own.shape[1]
-    vmem = pl.BlockSpec(memory_space=pltpu.VMEM)
+    )(*near_blocks, taps, keep, twist, table, factor, begun, outer_begun)
+
+
+def outer_frames_call(far_blocks, taps, keep, twist, table, factor, middle, begun, frames, near, far):
+    inputs = far_blocks[0].shape[1]
     messages = KEPT * 4 * inputs
     return pl.pallas_call(
         functools.partial(outer_kernel, frames, near, far),
         out_shape=jax.ShapeDtypeStruct((messages, LANES), jnp.bfloat16),
-        in_specs=[vmem] * 11,
-        out_specs=vmem,
+        in_specs=[VMEM] * 9,
+        out_specs=VMEM,
         scratch_shapes=scratch(inputs)
         + [pltpu.VMEM((2, RADIX * 8 * inputs, KEPT), jnp.float32), pltpu.VMEM((messages, LANES), jnp.float32)],
         compiler_params=pltpu.CompilerParams(vmem_limit_bytes=VMEM_LIMIT),
         name="outer_frames",
-    )(own, *near_blocks, *far_blocks, taps, keep, *tables(), factor, middle)
+    )(*far_blocks, taps, keep, twist, table, factor, middle, begun)
+
+
+def cut_kernel(spans, in_ref, *outs):
+    for (start, stop), out in zip(spans, outs):
+        out[...] = in_ref[:, :, start:stop]
+
+
+def cut_spans(samples, spans):
+    return pl.pallas_call(
+        functools.partial(cut_kernel, spans),
+        out_shape=[jax.ShapeDtypeStruct(samples.shape[:2] + (b - a,), samples.dtype) for a, b in spans],
+        in_specs=[VMEM],
+        out_specs=[VMEM] * len(spans),
+        compiler_params=pltpu.CompilerParams(vmem_limit_bytes=VMEM_LIMIT),
+        name="cut",
+    )(samples)
 
 
 def correlate_kernel(normalizer, words_ref, out_ref, joined, swapped):
@@ -257,7 +345,7 @@
 
     @pl.when(channel == 0)
     def _():
-        some = 8
+        some = stations
         lane = lax.broadcasted_iota(jnp.int32, (some * inputs, LANES), 1)
         sign = jnp.where(lane < LANES // 2, 1.0, -1.0)
 
@@ -322,11 +410,6 @@
     )(words)
 
 
-def band_factor(scales, rescale):
-    factor = (scales.astype(jnp.float32) * rescale).reshape(-1, KEPT, RADIX)
-    return jnp.transpose(factor, (2, 0, 1))
-
-
 def body(samples, taps, scales):
     length = taps.shape[1]
     inputs = samples.shape[1]
@@ -337,22 +420,29 @@
     onward = [(i, i + 1) for i in range(times - 1)]
     backward = [(i, (i - 1) % times) for i in range(times)]
 
-    def blocks(start, stop):
-        return samples[:, :, start * length : stop * length]
-
-    near_blocks = (
-        lax.ppermute(blocks(cut, frames), "tm", onward),
-        lax.ppermute(blocks(0, near[1]), "tm", backward),
-    )
-    far_blocks = (
-        lax.ppermute(blocks(cut - far[0], cut), "tm", onward),
-        lax.ppermute(blocks(near[1], near[1] + far[1]), "tm", backward),
-    )
+    spans = [
+        (cut, frames),
+        (0, near[1]),
+        (cut - far[0], cut),
+        (near[1], near[1] + far[1]),
+    ]
+    blocks = cut_spans(samples, [(a * length, b * length) for a, b in spans])
+    before, after, far_before, far_after = [
+        lax.ppermute(block, "tm", route) for block, route in zip(blocks, (onward, backward) * 2)
+    ]
     keep = jnp.where(lax.axis_index("tm") == times - 1, 0.0, 1.0)
     keep = jnp.broadcast_to(keep.astype(jnp.float32), (inputs, LANES))
-    factor = band_factor(scales, 16.0 / math.sqrt(length))
-    middle = middle_frames_call(samples, *near_blocks, taps, keep, factor, frames, near, far)
-    words = outer_frames_call(samples, near_blocks, far_blocks, taps, keep, factor, middle, frames, near, far)
+    table = split_table()
+    rescale = 16.0 / math.sqrt(length)
+    begun, outer_begun, factor, wide_taps, twist = own_blocks_call(
+        samples, taps, keep, scales, rescale, frames, near, far
+    )
+    middle, outer_begun = middle_frames_call(
+        (before, after), wide_taps, keep, twist, table, factor, begun, outer_begun, frames, near, far
+    )
+    words = outer_frames_call(
+        (far_before, far_after), wide_taps, keep, twist, table, factor, middle, outer_begun, frames, near, far
+    )
     words = words.reshape(stations * times, inputs, LANES)
     words = lax.all_to_all(words, ("stn", "tm"), split_axis=0, concat_axis=0, tiled=True)
     words = words.reshape(stations, times, inputs, LANES)

time: 130 us -> 122 us (0.938)
  local copies, waits for them, and re-layouts: 9.69 us -> 4.81 us
    pallas_call x0 -> x2, Pallas kernels: none -> 5.42 us  [the longest x1 4.24 us: own_blocks_call(): pl.pallas_call(functools.partial(own_kernel, frames, near, far, rescale),...]
    pallas_call x1, Pallas kernels: 7.76 us -> 3.54 us  [outer_frames_call(): pl.pallas_call(functools.partial(outer_kernel, frames, near, far), out_sh...]
    reshape x2 -> x0, local copies, waits for them, and re-layouts: 3.68 us -> none  [band_factor(): factor = (scales.astype(jnp.float32) * rescale).reshape(-1, KEPT, RADIX)]
    slice x2 -> x0, local copies, waits for them, and re-layouts: 3.5 us -> none  [blocks(): return samples[:, :, start * length:stop * length]]
    unnamed x12 -> x14, local copies, waits for them, and re-layouts: 2.5 us -> 4.81 us
  transfers between devices with their start and end apart: 4 -> 4, of which waited for: 0 -> 0; matrix products, arithmetic and copies ran while one was open for 4% -> 0% of each run, Pallas kernels for 4% -> 7%
where the time goes in v4:
time: 122 us; the launch traced here: 121 us
  blocking collectives  86.3 us (71%)
  Pallas kernels  17 us (14%)
  starting transfers between devices  13 us (11%)
  local copies, waits for them, and re-layouts  4.81 us (4%)
    all_to_all x1, blocking collectives, body(): lax.all_to_all(words, ('stn', 'tm'), split_axis=0, concat_axis=0, tiled=T...  86.3 us
    ppermute x4, starting transfers between devices, body(): lax.ppermute(block, 'tm', route)  13 us
    unnamed x14, local copies, waits for them, and re-layouts  4.81 us
    pallas_call x1, Pallas kernels, own_blocks_call(): pl.pallas_call(functools.partial(own_kernel, frames, near, far, rescale),...  4.24 us
    pallas_call x1, Pallas kernels, middle_frames_call(): pl.pallas_call(functools.partial(middle_kernel, frames, near, far), out_s...  4.16 us
    pallas_call x1, Pallas kernels, correlate(): pl.pallas_call(functools.partial(correlate_kernel, normalizer), grid=(4,)...  3.83 us
    pallas_call x1, Pallas kernels, outer_frames_call(): pl.pallas_call(functools.partial(outer_kernel, frames, near, far), out_sh...  3.54 us
  transfers between devices with their start and end apart: 4, of which 0 were waited for; matrix products, arithmetic and copies ran while one was open for 0% of the time, Pallas kernels for 7%

profile of v4, /device:TPU:1, one launch (start us, length us, event | category | flops | bytes accessed | tf_op | source)
XLA Modules:
  0.0 121.2 jit_solution(9816978484498174423)
XLA Ops:
  0.0 0.0 copy-start
  0.0 1.5 %copy-done = bf16[2,8,61440]{2,1,0:T(8,128)(2,1)S(1)} copy-done((bf16[2,8,61440]{2,1,0:T(8,128)(2,1)S(1)}, bf16[2,8,61440]{2,1,0:T(8,128)(2,1)}, u32[]{:S(2)}) %copy-start) | copy-done | bytes 1966104
  1.5 0.0 copy-start.1
  1.5 1.2 cut.1
  2.7 4.8 %collective-permute-start.2 = (bf16[2,8,16384]{2,1,0:T(8,128)(2,1)}, bf16[2,8,16384]{2,1,0:T(8,128)(2,1)}, u32[]{:S(2)}, u32[]{:S(2)}) collective-permute-start(bf16[2,8,16384]{2,1,0:T(8,128)(2,1)} %get-tuple-element.21), channel_id=1, source_target_pairs={{0,1},{1,2},{2,3},{3,4},{4,5},{5,6},{6,7},{8,9},{9,10},{10,11},{11... | collective-permute-start | bytes 1572872 | tf_op jit(solution)/shard_map/ppermute | solution.py:431
  7.5 2.9 %collective-permute-start.3 = (bf16[2,8,16384]{2,1,0:T(8,128)(2,1)}, bf16[2,8,16384]{2,1,0:T(8,128)(2,1)}, u32[]{:S(2)}, u32[]{:S(2)}) collective-permute-start(bf16[2,8,16384]{2,1,0:T(8,128)(2,1)} %get-tuple-element.22), channel_id=1, source_target_pairs={{0,7},{1,0},{2,1},{3,2},{4,3},{5,4},{6,5},{7,6},{8,15},{9,8},{10,9... | collective-permute-start | bytes 1572872 | tf_op jit(solution)/shard_map/ppermute | solution.py:431
  10.4 4.0 %collective-permute-start.1 = (bf16[2,8,12288]{2,1,0:T(8,128)(2,1)}, bf16[2,8,12288]{2,1,0:T(8,128)(2,1)S(1)}, u32[]{:S(2)}, u32[]{:S(2)}) collective-permute-start(bf16[2,8,12288]{2,1,0:T(8,128)(2,1)} %get-tuple-element.17), channel_id=1, source_target_pairs={{0,7},{1,0},{2,1},{3,2},{4,3},{5,4},{6,5},{7,6},{8,15},{9,8},{10,9... | collective-permute-start | bytes 1179656 | tf_op jit(solution)/shard_map/ppermute | solution.py:431
  14.4 1.3 %collective-permute-start = (bf16[2,8,16384]{2,1,0:T(8,128)(2,1)S(1)}, bf16[2,8,16384]{2,1,0:T(8,128)(2,1)S(1)}, u32[]{:S(2)}, u32[]{:S(2)}) collective-permute-start(bf16[2,8,16384]{2,1,0:T(8,128)(2,1)S(1)} %get-tuple-element.16), channel_id=1, source_target_pairs={{0,1},{1,2},{2,3},{3,4},{4,5},{5,6},{6,7},{8,9},{9,10},{10,11},{11... | collective-permute-start | bytes 1572872 | tf_op jit(solution)/shard_map/ppermute | solution.py:431
  15.8 0.0 copy-done.1
  15.8 0.0 copy-start.3
  15.8 0.9 copy-done.3
  16.7 0.0 copy-start.4
  16.7 0.8 copy-done.4
  17.5 0.0 copy-start.5
  17.5 0.8 copy-done.5
  18.3 0.0 copy-start.6
  18.3 0.8 copy-done.6
  19.0 0.0 copy-start.2
  19.0 4.2 %own_blocks.1 = (f32[2,32,8,8,128]{4,3,2,1,0:T(8,128)S(1)}, f32[2,32,7,8,128]{4,3,2,1,0:T(8,128)S(1)}, f32[16,8,128]{2,1,0:T(8,128)S(1)}, f32[16,4096]{1,0:T(8,128)S(1)}, f32[2,16,256]{2,1,0:T(8,128)S(1)}) custom-call(bf16[2,8,61440]{2,1,0:T(8,128)(2,1)S(1)} %copy-done.1, bf16[16,4096]{1,0:T(8,128)(2,1)S(1)} %copy-done.3, ...), custom_call_target="tpu_custom_call" | custom-call | flops 3000000000 | bytes 6291456 | tf_op jit(solution)/shard_map/own_blocks/pallas_call | solution.py:275
  23.3 0.0 collective-permute-done.2.before_ref
  23.3 0.0 collective-permute-done.3.after_ref
  23.3 0.0 copy-done.2
  23.3 4.2 %middle_frames.1 = (f32[2,1024,128]{2,1,0:T(8,128)S(1)}, f32[2,32,7,8,128]{4,3,2,1,0:T(8,128)S(1)}) custom-call(bf16[2,8,16384]{2,1,0:T(8,128)(2,1)} %collective-permute-done.2.before_ref, bf16[2,8,16384]{2,1,0:T(8,128)(2,1)} %collective-permute-done.3.after_ref, f32[16,4096]{1,0:T(8,128)S(1)} %get-tuple-element.18.taps_ref, ...), custom_call_target="tpu_custom_call" | custom-call | flops 3000000000 | bytes 5242880 | tf_op jit(solution)/shard_map/middle_frames/pallas_call | solution.py:294
  27.5 0.0 collective-permute-done.1.after_ref
  27.5 0.0 collective-permute-done.before_ref
  27.5 3.5 %outer_frames.1 = bf16[4096,128]{1,0:T(8,128)(2,1)S(1)} custom-call(bf16[2,8,16384]{2,1,0:T(8,128)(2,1)S(1)} %collective-permute-done.before_ref, bf16[2,8,12288]{2,1,0:T(8,128)(2,1)S(1)} %collective-permute-done.1.after_ref, f32[16,4096]{1,0:T(8,128)S(1)} %get-tuple-element.18.taps_ref, f32[8,128]{1,0:T(8,128)S(1)} %broadcast_in_dim.3.keep_ref, ...), custom_call_target="tpu_custom_call" | custom-call | tf_op jit(solution)/shard_map/outer_frames/pallas_call | solution.py:312
  31.1 86.3 %all_to_all.5 = bf16[512,8,128]{2,1,0:T(8,128)(2,1)S(1)} all-to-all(bf16[512,8,128]{2,1,0:T(8,128)(2,1)S(1)} %bitcast.2), channel_id=1, replica_groups=mesh['stn'=64,'tm'=8] {'stn','tm'}, dimensions={0} | all-to-all | bytes 2097152 | tf_op jit(solution)/shard_map/all_to_all | solution.py:447
  117.4 3.8 %correlate.1 = bf16[4,512,512]{2,1,0:T(8,128)(2,1)} custom-call(bf16[64,8,8,128]{3,2,1,0:T(8,128)(2,1)S(1)} %bitcast.3), custom_call_target="tpu_custom_call" | custom-call | tf_op jit(solution)/shard_map/correlate/pallas_call | solution.py:401
  (1 shorter events, 0.0 us)
Async XLA Ops:
  0.0 1.5 %copy-start = (bf16[2,8,61440]{2,1,0:T(8,128)(2,1)S(1)}, bf16[2,8,61440]{2,1,0:T(8,128)(2,1)}, u32[]{:S(2)}) copy-start(bf16[2,8,61440]{2,1,0:T(8,128)(2,1)} %own_ref.1) | copy-start | bytes 5898244
  1.5 14.2 %copy-start.1 = (bf16[2,8,61440]{2,1,0:T(8,128)(2,1)S(1)}, bf16[2,8,61440]{2,1,0:T(8,128)(2,1)}, u32[]{:S(2)}) copy-start(bf16[2,8,61440]{2,1,0:T(8,128)(2,1)} %own_ref.1) | copy-start | bytes 5898244
  2.7 20.6 %collective-permute-start.2 = (bf16[2,8,16384]{2,1,0:T(8,128)(2,1)}, bf16[2,8,16384]{2,1,0:T(8,128)(2,1)}, u32[]{:S(2)}, u32[]{:S(2)}) collective-permute-start(bf16[2,8,16384]{2,1,0:T(8,128)(2,1)} %get-tuple-element.21), channel_id=1, source_target_pairs={{0,1},{1,2},{2,3},{3,4},{4,5},{5,6},{6,7},{8,9},{9,10},{10,11},{11... | collective-permute-start | bytes 1572872 | tf_op jit(solution)/shard_map/ppermute | solution.py:431
  7.5 15.8 %collective-permute-start.3 = (bf16[2,8,16384]{2,1,0:T(8,128)(2,1)}, bf16[2,8,16384]{2,1,0:T(8,128)(2,1)}, u32[]{:S(2)}, u32[]{:S(2)}) collective-permute-start(bf16[2,8,16384]{2,1,0:T(8,128)(2,1)} %get-tuple-element.22), channel_id=1, source_target_pairs={{0,7},{1,0},{2,1},{3,2},{4,3},{5,4},{6,5},{7,6},{8,15},{9,8},{10,9... | collective-permute-start | bytes 1572872 | tf_op jit(solution)/shard_map/ppermute | solution.py:431
  10.4 17.1 %collective-permute-start.1 = (bf16[2,8,12288]{2,1,0:T(8,128)(2,1)}, bf16[2,8,12288]{2,1,0:T(8,128)(2,1)S(1)}, u32[]{:S(2)}, u32[]{:S(2)}) collective-permute-start(bf16[2,8,12288]{2,1,0:T(8,128)(2,1)} %get-tuple-element.17), channel_id=1, source_target_pairs={{0,7},{1,0},{2,1},{3,2},{4,3},{5,4},{6,5},{7,6},{8,15},{9,8},{10,9... | collective-permute-start | bytes 1179656 | tf_op jit(solution)/shard_map/ppermute | solution.py:431
  14.4 13.1 %collective-permute-start = (bf16[2,8,16384]{2,1,0:T(8,128)(2,1)S(1)}, bf16[2,8,16384]{2,1,0:T(8,128)(2,1)S(1)}, u32[]{:S(2)}, u32[]{:S(2)}) collective-permute-start(bf16[2,8,16384]{2,1,0:T(8,128)(2,1)S(1)} %get-tuple-element.16), channel_id=1, source_target_pairs={{0,1},{1,2},{2,3},{3,4},{4,5},{5,6},{6,7},{8,9},{9,10},{10,11},{11... | collective-permute-start | bytes 1572872 | tf_op jit(solution)/shard_map/ppermute | solution.py:431
  15.8 0.9 copy-start.3
  16.7 0.8 copy-start.4
  17.5 0.8 copy-start.5
  18.3 0.8 copy-start.6
  19.0 4.3 %copy-start.2 = (bf16[512,512]{1,0:T(8,128)(2,1)S(1)}, bf16[512,512]{1,0:T(8,128)(2,1)}, u32[]{:S(2)}) copy-start(bf16[512,512]{1,0:T(8,128)(2,1)} %constant.24.table_ref) | copy-start | bytes 1572868

commit v5 on v4

--- a/solution.py
+++ b/solution.py
@@ -15,6 +15,7 @@
 KEPT = 128
 SLOT = 16
 VMEM_LIMIT = 28 * 2**20
+WHOLE_VMEM = 62 * 2**20
 
 
 def second_table():
@@ -321,78 +322,88 @@
     )(*far_blocks, taps, keep, twist, table, factor, middle, begun)
 
 
-def cut_kernel(spans, in_ref, *outs):
-    for (start, stop), out in zip(spans, outs):
-        out[...] = in_ref[:, :, start:stop]
+def cut_kernel(spans, in_ref, *refs):
+    outs, sems = refs[:-1], refs[-1]
+    copies = [
+        pltpu.make_async_copy(in_ref.at[:, :, start:stop], out, sems.at[i])
+        for i, ((start, stop), out) in enumerate(zip(spans, outs))
+    ]
+    for copy in copies:
+        copy.start()
+    for copy in copies:
+        copy.wait()
 
 
 def cut_spans(samples, spans):
     return pl.pallas_call(
         functools.partial(cut_kernel, spans),
         out_shape=[jax.ShapeDtypeStruct(samples.shape[:2] + (b - a,), samples.dtype) for a, b in spans],
-        in_specs=[VMEM],
+        in_specs=[pl.BlockSpec(memory_space=pltpu.HBM)],
         out_specs=[VMEM] * len(spans),
-        compiler_params=pltpu.CompilerParams(vmem_limit_bytes=VMEM_LIMIT),
+        scratch_shapes=[pltpu.SemaphoreType.DMA((len(spans),))],
+        compiler_params=pltpu.CompilerParams(vmem_limit_bytes=WHOLE_VMEM),
         name="cut",
     )(samples)
 
 
-def correlate_kernel(normalizer, words_ref, out_ref, joined, swapped):
-    channel = pl.program_id(0)
+def correlate_kernel(normalizer, words_ref, out_ref, joined, swapped, result, sems):
     stations, times, inputs, _ = words_ref.shape
     size = stations * inputs
     half = size // 2
 
-    @pl.when(channel == 0)
-    def _():
-        some = stations
-        lane = lax.broadcasted_iota(jnp.int32, (some * inputs, LANES), 1)
-        sign = jnp.where(lane < LANES // 2, 1.0, -1.0)
-
-        def trade(block, _):
-            span = pl.ds(pl.multiple_of(block * some * inputs, some * inputs), some * inputs)
-            for q in range(times // 4):
-                held = [
-                    words_ref[pl.ds(block * some, some), 4 * q + r].astype(jnp.float32).reshape(some * inputs, LANES)
-                    for r in range(4)
-                ]
-                for bit in (1, 2):
-                    shift = bit * SLOT
-                    left = (lane // shift) % 2 == 0
-                    for r in range(4):
-                        if not r & bit:
-                            x, y = held[r], held[r | bit]
-                            held[r] = jnp.where(left, x, pltpu.roll(y, shift, 1))
-                            held[r | bit] = jnp.where(left, pltpu.roll(x, LANES - shift, 1), y)
-                for c in range(4):
-                    lanes = pl.ds(q * LANES, LANES)
-                    joined[c, span, lanes] = held[c].astype(jnp.bfloat16)
-                    other = pltpu.roll(held[c], LANES // 2, 1) * sign
-                    swapped[c, span, lanes] = other.astype(jnp.bfloat16)
-            return 0
-
-        lax.fori_loop(0, stations // some, trade, 0)
+    some = stations
+    lane = lax.broadcasted_iota(jnp.int32, (some * inputs, LANES), 1)
+    sign = jnp.where(lane < LANES // 2, 1.0, -1.0)
+
+    def trade(block, _):
+        span = pl.ds(pl.multiple_of(block * some * inputs, some * inputs), some * inputs)
+        for q in range(times // 4):
+            held = [
+                words_ref[pl.ds(block * some, some), 4 * q + r].astype(jnp.float32).reshape(some * inputs, LANES)
+                for r in range(4)
+            ]
+            for bit in (1, 2):
+                shift = bit * SLOT
+                left = (lane // shift) % 2 == 0
+                for r in range(4):
+                    if not r & bit:
+                        x, y = held[r], held[r | bit]
+                        held[r] = jnp.where(left, x, pltpu.roll(y, shift, 1))
+                        held[r | bit] = jnp.where(left, pltpu.roll(x, LANES - shift, 1), y)
+            for c in range(4):
+                lanes = pl.ds(q * LANES, LANES)
+                joined[c, span, lanes] = held[c].astype(jnp.bfloat16)
+                other = pltpu.roll(held[c], LANES // 2, 1) * sign
+                swapped[c, span, lanes] = other.astype(jnp.bfloat16)
+        return 0
+
+    lax.fori_loop(0, stations // some, trade, 0)
 
     def product(left, right):
         return lax.dot_general(
             left, right, (((1,), (1,)), ((), ())), preferred_element_type=jnp.float32
         )
 
-    first, second = joined[channel, :half], joined[channel, half:]
-    first_other, second_other = swapped[channel, :half], swapped[channel, half:]
+    def finish(values):
+        return (values * normalizer).astype(jnp.bfloat16)
+
     lower = lax.broadcasted_iota(jnp.int32, (half, half), 0) >= lax.broadcasted_iota(
         jnp.int32, (half, half), 1
     )
-
-    def finish(values):
-        return (values * normalizer).astype(jnp.bfloat16)
-
-    out_ref[0, :half, :half] = finish(jnp.where(lower, product(first, first), product(first_other, first)))
-    out_ref[0, half:, :half] = finish(product(second, first))
-    out_ref[0, :half, half:] = finish(product(first_other, second))
-    out_ref[0, half:, half:] = finish(
-        jnp.where(lower, product(second, second), product(second_other, second))
-    )
+    copies = []
+    for channel in range(4):
+        first, second = joined[channel, :half], joined[channel, half:]
+        first_other, second_other = swapped[channel, :half], swapped[channel, half:]
+        result[channel, :half, :half] = finish(jnp.where(lower, product(first, first), product(first_other, first)))
+        result[channel, half:, :half] = finish(product(second, first))
+        result[channel, :half, half:] = finish(product(first_other, second))
+        result[channel, half:, half:] = finish(
+            jnp.where(lower, product(second, second), product(second_other, second))
+        )
+        copies.append(pltpu.make_async_copy(result.at[channel], out_ref.at[channel], sems.at[channel]))
+        copies[-1].start()
+    for copy in copies:
+        copy.wait()
 
 
 def correlate(words, normalizer):
@@ -400,11 +411,11 @@
     size = stations * inputs
     return pl.pallas_call(
         functools.partial(correlate_kernel, normalizer),
-        grid=(4,),
         out_shape=jax.ShapeDtypeStruct((4, size, size), jnp.bfloat16),
-        in_specs=[pl.BlockSpec(words.shape, lambda c: (0, 0, 0, 0))],
-        out_specs=pl.BlockSpec((1, size, size), lambda c: (c, 0, 0)),
-        scratch_shapes=[pltpu.VMEM((4, size, times * 2 * SLOT), jnp.bfloat16)] * 2,
+        in_specs=[VMEM],
+        out_specs=pl.BlockSpec(memory_space=pltpu.HBM),
+        scratch_shapes=[pltpu.VMEM((4, size, times * 2 * SLOT), jnp.bfloat16)] * 2
+        + [pltpu.VMEM((4, size, size), jnp.bfloat16), pltpu.SemaphoreType.DMA((4,))],
         compiler_params=pltpu.CompilerParams(vmem_limit_bytes=VMEM_LIMIT),
         name="correlate",
     )(words)
@@ -426,7 +437,8 @@
         (cut - far[0], cut),
         (near[1], near[1] + far[1]),
     ]
-    blocks = cut_spans(samples, [(a * length, b * length) for a, b in spans])
+    spans = [(a * length, b * length) for a, b in spans]
+    blocks = cut_spans(samples, spans[:2]) + cut_spans(samples, spans[2:])
     before, after, far_before, far_after = [
         lax.ppermute(block, "tm", route) for block, route in zip(blocks, (onward, backward) * 2)
     ]

time: 122 us -> 120 us (0.984)
  local copies, waits for them, and re-layouts: 4.81 us -> 2.43 us
  Pallas kernels: 17 us -> 19 us
    pallas_call x1 -> x2, Pallas kernels: 1.18 us -> 4.43 us  [cut_spans(): pl.pallas_call(functools.partial(cut_kernel, spans), out_shape=[jax.Shape...]
    unnamed x14 -> x12, local copies, waits for them, and re-layouts: 4.81 us -> 2.43 us
    all_to_all x1, blocking collectives: 86.3 us -> 85.1 us  [body(): lax.all_to_all(words, ('stn', 'tm'), split_axis=0, concat_axis=0, tiled=T...]
  transfers between devices with their start and end apart: 4 -> 4, of which waited for: 0 -> 0; matrix products, arithmetic and copies ran while one was open for 0% -> 0% of each run, Pallas kernels for 7% -> 9%
where the time goes in v5:
time: 120 us
  blocking collectives  85.1 us (71%)
  Pallas kernels  19 us (16%)
  starting transfers between devices  13 us (11%)
  local copies, waits for them, and re-layouts  2.43 us (2%)
    all_to_all x1, blocking collectives, body(): lax.all_to_all(words, ('stn', 'tm'), split_axis=0, concat_axis=0, tiled=T...  85.1 us
    ppermute x4, starting transfers between devices, body(): lax.ppermute(block, 'tm', route)  13 us
    pallas_call x2, Pallas kernels, cut_spans(): pl.pallas_call(functools.partial(cut_kernel, spans), out_shape=[jax.Shape...  4.43 us
    pallas_call x1, Pallas kernels, own_blocks_call(): pl.pallas_call(functools.partial(own_kernel, frames, near, far, rescale),...  4.24 us
    pallas_call x1, Pallas kernels, middle_frames_call(): pl.pallas_call(functools.partial(middle_kernel, frames, near, far), out_s...  4.15 us
    pallas_call x1, Pallas kernels, outer_frames_call(): pl.pallas_call(functools.partial(outer_kernel, frames, near, far), out_sh...  3.53 us
    pallas_call x1, Pallas kernels, correlate(): pl.pallas_call(functools.partial(correlate_kernel, normalizer), out_shape...  2.63 us
    unnamed x12, local copies, waits for them, and re-layouts  2.43 us
  transfers between devices with their start and end apart: 4, of which 0 were waited for; matrix products, arithmetic and copies ran while one was open for 0% of the time, Pallas kernels for 9%

profile of v5, /device:TPU:1, one launch (start us, length us, event | category | flops | bytes accessed | tf_op | source)
XLA Modules:
  0.0 119.6 jit_solution(17253265727093825137)
XLA Ops:
  0.0 0.0 copy-start
  0.0 0.0 copy-start.3
  0.0 2.3 %cut.3 = (bf16[2,8,16384]{2,1,0:T(8,128)(2,1)}, bf16[2,8,16384]{2,1,0:T(8,128)(2,1)}) custom-call(bf16[2,8,61440]{2,1,0:T(8,128)(2,1)} %in_ref.3), custom_call_target="tpu_custom_call" | custom-call | tf_op jit(solution)/shard_map/cut/pallas_call | solution.py:338
  2.3 4.9 %collective-permute-start.2 = (bf16[2,8,16384]{2,1,0:T(8,128)(2,1)}, bf16[2,8,16384]{2,1,0:T(8,128)(2,1)}, u32[]{:S(2)}, u32[]{:S(2)}) collective-permute-start(bf16[2,8,16384]{2,1,0:T(8,128)(2,1)} %get-tuple-element.21), channel_id=1, source_target_pairs={{0,1},{1,2},{2,3},{3,4},{4,5},{5,6},{6,7},{8,9},{9,10},{10,11},{11... | collective-permute-start | bytes 1572872 | tf_op jit(solution)/shard_map/ppermute | solution.py:443
  7.2 2.8 %collective-permute-start.3 = (bf16[2,8,16384]{2,1,0:T(8,128)(2,1)}, bf16[2,8,16384]{2,1,0:T(8,128)(2,1)}, u32[]{:S(2)}, u32[]{:S(2)}) collective-permute-start(bf16[2,8,16384]{2,1,0:T(8,128)(2,1)} %get-tuple-element.22), channel_id=1, source_target_pairs={{0,7},{1,0},{2,1},{3,2},{4,3},{5,4},{6,5},{7,6},{8,15},{9,8},{10,9... | collective-permute-start | bytes 1572872 | tf_op jit(solution)/shard_map/ppermute | solution.py:443
  10.1 2.1 %cut.2 = (bf16[2,8,16384]{2,1,0:T(8,128)(2,1)}, bf16[2,8,12288]{2,1,0:T(8,128)(2,1)}) custom-call(bf16[2,8,61440]{2,1,0:T(8,128)(2,1)} %in_ref.3), custom_call_target="tpu_custom_call" | custom-call | tf_op jit(solution)/shard_map/cut/pallas_call | solution.py:338
  12.2 2.5 %collective-permute-start = (bf16[2,8,16384]{2,1,0:T(8,128)(2,1)}, bf16[2,8,16384]{2,1,0:T(8,128)(2,1)S(1)}, u32[]{:S(2)}, u32[]{:S(2)}) collective-permute-start(bf16[2,8,16384]{2,1,0:T(8,128)(2,1)} %get-tuple-element.16), channel_id=1, source_target_pairs={{0,1},{1,2},{2,3},{3,4},{4,5},{5,6},{6,7},{8,9},{9,10},{10,11},{11... | collective-permute-start | bytes 1572872 | tf_op jit(solution)/shard_map/ppermute | solution.py:443
  14.6 2.8 %collective-permute-start.1 = (bf16[2,8,12288]{2,1,0:T(8,128)(2,1)}, bf16[2,8,12288]{2,1,0:T(8,128)(2,1)S(1)}, u32[]{:S(2)}, u32[]{:S(2)}) collective-permute-start(bf16[2,8,12288]{2,1,0:T(8,128)(2,1)} %get-tuple-element.17), channel_id=1, source_target_pairs={{0,7},{1,0},{2,1},{3,2},{4,3},{5,4},{6,5},{7,6},{8,15},{9,8},{10,9... | collective-permute-start | bytes 1179656 | tf_op jit(solution)/shard_map/ppermute | solution.py:443
  17.5 0.0 copy-done
  17.5 0.0 copy-done.3
  17.5 0.0 copy-start.2
  17.5 0.9 copy-done.2
  18.4 0.0 copy-start.4
  18.4 0.8 copy-done.4
  19.2 0.0 copy-start.5
  19.2 0.8 copy-done.5
  19.9 0.0 copy-start.1
  19.9 4.2 %own_blocks.1 = (f32[2,32,8,8,128]{4,3,2,1,0:T(8,128)S(1)}, f32[2,32,7,8,128]{4,3,2,1,0:T(8,128)S(1)}, f32[16,8,128]{2,1,0:T(8,128)S(1)}, f32[16,4096]{1,0:T(8,128)S(1)}, f32[2,16,256]{2,1,0:T(8,128)S(1)}) custom-call(bf16[2,8,61440]{2,1,0:T(8,128)(2,1)S(1)} %copy-done, bf16[16,4096]{1,0:T(8,128)(2,1)S(1)} %copy-done.2, ...), custom_call_target="tpu_custom_call" | custom-call | flops 3000000000 | bytes 6291456 | tf_op jit(solution)/shard_map/own_blocks/pallas_call | solution.py:276
  24.2 0.0 collective-permute-done.2.before_ref
  24.2 0.0 collective-permute-done.3.after_ref
  24.2 0.0 copy-done.1
  24.2 4.2 %middle_frames.1 = (f32[2,1024,128]{2,1,0:T(8,128)S(1)}, f32[2,32,7,8,128]{4,3,2,1,0:T(8,128)S(1)}) custom-call(bf16[2,8,16384]{2,1,0:T(8,128)(2,1)} %collective-permute-done.2.before_ref, bf16[2,8,16384]{2,1,0:T(8,128)(2,1)} %collective-permute-done.3.after_ref, f32[16,4096]{1,0:T(8,128)S(1)} %get-tuple-element.18.taps_ref, ...), custom_call_target="tpu_custom_call" | custom-call | flops 3000000000 | bytes 5242880 | tf_op jit(solution)/shard_map/middle_frames/pallas_call | solution.py:295
  28.4 0.0 collective-permute-done.1.after_ref
  28.4 0.0 collective-permute-done.before_ref
  28.4 3.5 %outer_frames.1 = bf16[4096,128]{1,0:T(8,128)(2,1)S(1)} custom-call(bf16[2,8,16384]{2,1,0:T(8,128)(2,1)S(1)} %collective-permute-done.before_ref, bf16[2,8,12288]{2,1,0:T(8,128)(2,1)S(1)} %collective-permute-done.1.after_ref, f32[16,4096]{1,0:T(8,128)S(1)} %get-tuple-element.18.taps_ref, f32[8,128]{1,0:T(8,128)S(1)} %broadcast_in_dim.3.keep_ref, ...), custom_call_target="tpu_custom_call" | custom-call | tf_op jit(solution)/shard_map/outer_frames/pallas_call | solution.py:313
  31.9 85.1 %all_to_all.5 = bf16[512,8,128]{2,1,0:T(8,128)(2,1)S(1)} all-to-all(bf16[512,8,128]{2,1,0:T(8,128)(2,1)S(1)} %bitcast.2), channel_id=1, replica_groups=mesh['stn'=64,'tm'=8] {'stn','tm'}, dimensions={0} | all-to-all | bytes 2097152 | tf_op jit(solution)/shard_map/all_to_all | solution.py:459
  117.0 2.6 %correlate.1 = bf16[4,512,512]{2,1,0:T(8,128)(2,1)} custom-call(bf16[64,8,8,128]{3,2,1,0:T(8,128)(2,1)S(1)} %bitcast.3), custom_call_target="tpu_custom_call" | custom-call | tf_op jit(solution)/shard_map/correlate/pallas_call | solution.py:412
  (1 shorter events, 0.0 us)
Async XLA Ops:
  0.0 17.5 %copy-start = (bf16[2,8,61440]{2,1,0:T(8,128)(2,1)S(1)}, bf16[2,8,61440]{2,1,0:T(8,128)(2,1)}, u32[]{:S(2)}) copy-start(bf16[2,8,61440]{2,1,0:T(8,128)(2,1)} %in_ref.3) | copy-start | bytes 5898244
  0.0 17.5 %copy-start.3 = (s32[8,2048]{1,0:T(8,128)S(1)}, s32[8,2048]{1,0:T(8,128)}, u32[]{:S(2)}) copy-start(s32[8,2048]{1,0:T(8,128)} %scales_ref.1) | copy-start | bytes 196612
  2.3 21.8 %collective-permute-start.2 = (bf16[2,8,16384]{2,1,0:T(8,128)(2,1)}, bf16[2,8,16384]{2,1,0:T(8,128)(2,1)}, u32[]{:S(2)}, u32[]{:S(2)}) collective-permute-start(bf16[2,8,16384]{2,1,0:T(8,128)(2,1)} %get-tuple-element.21), channel_id=1, source_target_pairs={{0,1},{1,2},{2,3},{3,4},{4,5},{5,6},{6,7},{8,9},{9,10},{10,11},{11... | collective-permute-start | bytes 1572872 | tf_op jit(solution)/shard_map/ppermute | solution.py:443
  7.2 17.0 %collective-permute-start.3 = (bf16[2,8,16384]{2,1,0:T(8,128)(2,1)}, bf16[2,8,16384]{2,1,0:T(8,128)(2,1)}, u32[]{:S(2)}, u32[]{:S(2)}) collective-permute-start(bf16[2,8,16384]{2,1,0:T(8,128)(2,1)} %get-tuple-element.22), channel_id=1, source_target_pairs={{0,7},{1,0},{2,1},{3,2},{4,3},{5,4},{6,5},{7,6},{8,15},{9,8},{10,9... | collective-permute-start | bytes 1572872 | tf_op jit(solution)/shard_map/ppermute | solution.py:443
  12.2 16.2 %collective-permute-start = (bf16[2,8,16384]{2,1,0:T(8,128)(2,1)}, bf16[2,8,16384]{2,1,0:T(8,128)(2,1)S(1)}, u32[]{:S(2)}, u32[]{:S(2)}) collective-permute-start(bf16[2,8,16384]{2,1,0:T(8,128)(2,1)} %get-tuple-element.16), channel_id=1, source_target_pairs={{0,1},{1,2},{2,3},{3,4},{4,5},{5,6},{6,7},{8,9},{9,10},{10,11},{11... | collective-permute-start | bytes 1572872 | tf_op jit(solution)/shard_map/ppermute | solution.py:443
  14.6 13.7 %collective-permute-start.1 = (bf16[2,8,12288]{2,1,0:T(8,128)(2,1)}, bf16[2,8,12288]{2,1,0:T(8,128)(2,1)S(1)}, u32[]{:S(2)}, u32[]{:S(2)}) collective-permute-start(bf16[2,8,12288]{2,1,0:T(8,128)(2,1)} %get-tuple-element.17), channel_id=1, source_target_pairs={{0,7},{1,0},{2,1},{3,2},{4,3},{5,4},{6,5},{7,6},{8,15},{9,8},{10,9... | collective-permute-start | bytes 1179656 | tf_op jit(solution)/shard_map/ppermute | solution.py:443
  17.5 0.9 copy-start.2
  18.4 0.8 copy-start.4
  19.2 0.8 copy-start.5
  19.9 4.3 %copy-start.1 = (bf16[512,512]{1,0:T(8,128)(2,1)S(1)}, bf16[512,512]{1,0:T(8,128)(2,1)}, u32[]{:S(2)}) copy-start(bf16[512,512]{1,0:T(8,128)(2,1)} %constant.24.table_ref) | copy-start | bytes 1572868

commit v6 on v5

--- a/solution.py
+++ b/solution.py
@@ -15,7 +15,6 @@
 KEPT = 128
 SLOT = 16
 VMEM_LIMIT = 28 * 2**20
-WHOLE_VMEM = 62 * 2**20
 
 
 def second_table():
@@ -110,9 +109,8 @@
     lax.fori_loop(0, length // LANES, filter_chunk, 0)
 
 
-def transform(count_used, twist_ref, table_ref, factor_ref, filt, rows, store):
+def transform(used, slots, twist_ref, table_ref, factor_ref, filt, rows, store):
     inputs = factor_ref.shape[1]
-    slots = 8
 
     def first_transform(slot, _):
         for half in range(2):
@@ -129,23 +127,28 @@
                 rows[2 + half, at, :] = imag
         return 0
 
-    lax.fori_loop(0, count_used, first_transform, 0, unroll=True)
-    for slot in range(count_used, slots):
+    lax.fori_loop(0, used, first_transform, 0, unroll=True)
+    for slot in range(used, slots):
         for q in range(4):
             for k1 in range(RADIX):
                 at = (k1 * slots + slot) * inputs
                 rows[q, at : at + inputs, :] = jnp.zeros((inputs, LANES), jnp.float32)
 
-    block = jnp.concatenate([rows[q] for q in range(4)], axis=1)
-    high = block.astype(jnp.bfloat16)
-    low = (block - high.astype(jnp.float32)).astype(jnp.bfloat16)
-    both = jnp.dot(high, table_ref[...], preferred_element_type=jnp.float32)
-    rest = jnp.dot(low, table_ref[:, : 2 * KEPT], preferred_element_type=jnp.float32)
-    total = both[:, : 2 * KEPT] + both[:, 2 * KEPT :] + rest
-    scale = factor_ref[...][:, None]
-    for comp in range(2):
-        part = total[:, comp * KEPT : (comp + 1) * KEPT].reshape(RADIX, slots, inputs, KEPT)
-        store[comp] = jnp.clip(part * scale, -127.0, 127.0).reshape(-1, KEPT)
+    some = 8
+    count = some * slots * inputs
+    for first in range(0, RADIX, some):
+        span = slice(first * slots * inputs, first * slots * inputs + count)
+        block = jnp.concatenate([rows[q, span, :] for q in range(4)], axis=1)
+        high = block.astype(jnp.bfloat16)
+        low = (block - high.astype(jnp.float32)).astype(jnp.bfloat16)
+        both = jnp.dot(high, table_ref[...], preferred_element_type=jnp.float32)
+        rest = jnp.dot(low, table_ref[:, : 2 * KEPT], preferred_element_type=jnp.float32)
+        total = both[:, : 2 * KEPT] + both[:, 2 * KEPT :] + rest
+        scale = factor_ref[first : first + some][:, None]
+        for comp in range(2):
+            part = total[:, comp * KEPT : (comp + 1) * KEPT].reshape(some, slots, inputs, KEPT)
+            part = jnp.clip(part * scale, -127.0, 127.0)
+            store(comp, slice(first, first + some), part.reshape(some, slots * inputs, KEPT))
 
 
 def split_frames(frames, near, far):
@@ -154,8 +157,7 @@
 
 
 def window_of(frames, near, far, refs):
-    far_before, before, own, after, far_after = refs
-    counts = (far[0], near[0], frames, near[1], far[1])
+    counts = (far[0], near[0], near[1], frames - near[0] - near[1], near[0], near[1], far[1])
     window = [(ref, u) for ref, count in zip(refs, counts) for u in range(count)]
     return window, far[0] + near[0] + frames
 
@@ -165,8 +167,8 @@
 
 
 def own_kernel(
-    frames, near, far, rescale, own_ref, taps_ref, keep_ref, scales_ref, order_ref, twist_ref,
-    middle_ref, outer_ref, factor_ref, wide_taps_ref, same_twist_ref,
+    frames, near, far, rescale, early_ref, between_ref, late_ref, taps_ref, keep_ref, scales_ref, order_ref, twist_ref,
+    middle_ref, outer_ref, factor_ref, wide_taps_ref, same_twist_ref, early_far_ref, late_far_ref,
 ):
     inputs = scales_ref.shape[0]
     blocks = scales_ref.shape[1] // LANES
@@ -190,45 +192,58 @@
         factor_ref[k1] = held[k1]
     wide_taps_ref[...] = taps_ref[...].astype(jnp.float32)
     same_twist_ref[...] = twist_ref[...]
-
-    sources = window_of(frames, near, far, (None, None, own_ref, None, None))
+    cut = early_far_ref.shape[2]
+    early_far_ref[...] = between_ref[:, :, :cut]
+    late_far_ref[...] = between_ref[:, :, cut:]
+
+    own = (early_ref, between_ref, late_ref)
+    sources = window_of(frames, near, far, (None, None, *own, None, None))
     for plan, out_ref in zip(split_frames(frames, near, far), (middle_ref, outer_ref)):
         filter_blocks(plan, given(sources[0]), sources, wide_taps_ref, keep_ref, out_ref)
 
 
 def middle_kernel(
     frames, near, far, before_ref, after_ref, taps_ref, keep_ref, twist_ref, table_ref, factor_ref, begun_ref,
-    outer_begun_ref, out_ref, outer_ref, filt, rows,
+    outer_begun_ref, out_ref, edge_ref, outer_ref, filt, rows,
 ):
-    sources = window_of(frames, near, far, (None, before_ref, None, after_ref, None))
+    sources = window_of(frames, near, far, (None, before_ref) + (None,) * 3 + (after_ref, None))
     middle, outer = split_frames(frames, near, far)
     fresh = given(sources[0])
+    inputs = factor_ref.shape[1]
+
+    def store(comp, some, part):
+        out_ref[comp, some] = part[:, : 8 * inputs]
+        edge_ref[comp, some] = part[:, 8 * inputs :]
+
     filter_blocks(middle, fresh, sources, taps_ref, keep_ref, filt, begun_ref)
-    transform(len(middle), twist_ref, table_ref, factor_ref, filt, rows, out_ref)
+    transform(len(middle), len(middle), twist_ref, table_ref, factor_ref, filt, rows, store)
     filter_blocks(outer, fresh, sources, taps_ref, keep_ref, outer_ref, outer_begun_ref)
 
 
 def outer_kernel(
     frames, near, far, before_ref, after_ref, taps_ref, keep_ref, twist_ref, table_ref, factor_ref, middle_ref,
-    begun_ref, out_ref, filt, rows, edge, words,
+    edge_ref, begun_ref, out_ref, filt, rows, edge, words,
 ):
-    sources = window_of(frames, near, far, (before_ref, None, None, None, after_ref))
-    _, plan = split_frames(frames, near, far)
+    sources = window_of(frames, near, far, (before_ref,) + (None,) * 5 + (after_ref,))
+    middle, plan = split_frames(frames, near, far)
+    inputs = factor_ref.shape[1]
+    taken = (len(middle) - 8) * inputs
+    edge[:, :, :taken] = edge_ref[...]
+
+    def store(comp, some, part):
+        edge[comp, some, taken:] = part
+
     filter_blocks(plan, given(sources[0]), sources, taps_ref, keep_ref, filt, begun_ref)
-    transform(len(plan), twist_ref, table_ref, factor_ref, filt, rows, edge)
-    inputs = factor_ref.shape[1]
-
-    def arrange(high, _):
+    transform(len(plan), SLOT - len(middle), twist_ref, table_ref, factor_ref, filt, rows, store)
+
+    for high in range(RADIX // 4):
         for i in range(inputs):
             parts = []
             for comp in range(2):
                 for channel in range(4):
-                    at = pl.ds((high * 4 + channel) * 8 * inputs + i, 8, stride=inputs)
-                    parts += [middle_ref[comp, at, :], edge[comp, at, :]]
+                    for half in (middle_ref, edge):
+                        parts.append(half[comp, high * 4 + channel, pl.ds(i, 8, stride=inputs), :])
             words[pl.ds(high * inputs + i, KEPT, stride=4 * inputs), :] = jnp.concatenate(parts, axis=0).T
-        return 0
-
-    lax.fori_loop(0, RADIX // 4, arrange, 0, unroll=True)
 
     def narrow(step, _):
         span = pl.ds(pl.multiple_of(step * 1024, 1024), 1024)
@@ -245,10 +260,10 @@
     return jnp.concatenate([high, low], axis=1)
 
 
-def scratch(inputs):
+def scratch(inputs, slots):
     return [
-        pltpu.VMEM((2, RADIX * FINE // LANES, 8, inputs, LANES), jnp.float32),
-        pltpu.VMEM((4, RADIX * 8 * inputs, LANES), jnp.float32),
+        pltpu.VMEM((2, RADIX * FINE // LANES, slots, inputs, LANES), jnp.float32),
+        pltpu.VMEM((4, RADIX * slots * inputs, LANES), jnp.float32),
     ]
 
 
@@ -268,8 +283,8 @@
     return order.astype(jnp.bfloat16)
 
 
-def own_blocks_call(own, taps, keep, scales, rescale, frames, near, far):
-    inputs = own.shape[1]
+def own_blocks_call(pieces, taps, keep, scales, rescale, frames, near, far):
+    inputs = pieces[0].shape[1]
     chunks = taps.shape[1] // LANES
     twist = twist_table()
     middle, outer = split_frames(frames, near, far)
@@ -281,69 +296,49 @@
             jax.ShapeDtypeStruct((RADIX, inputs, KEPT), jnp.float32),
             jax.ShapeDtypeStruct(taps.shape, jnp.float32),
             jax.ShapeDtypeStruct(twist.shape, jnp.float32),
+            jax.ShapeDtypeStruct((2, inputs, far[1] * taps.shape[1]), pieces[0].dtype),
+            jax.ShapeDtypeStruct((2, inputs, far[0] * taps.shape[1]), pieces[0].dtype),
         ),
-        in_specs=[VMEM] * 6,
-        out_specs=(VMEM,) * 5,
+        in_specs=[VMEM] * 8,
+        out_specs=(VMEM,) * 7,
         compiler_params=pltpu.CompilerParams(vmem_limit_bytes=VMEM_LIMIT),
         cost_estimate=pl.CostEstimate(flops=3 * 10**9, bytes_accessed=6 * 2**20, transcendentals=0),
         name="own_blocks",
-    )(own, taps, keep, scales, lane_order(), twist)
+    )(*pieces, taps, keep, scales, lane_order(), twist)
 
 
 def middle_frames_call(near_blocks, taps, keep, twist, table, factor, begun, outer_begun, frames, near, far):
     inputs = near_blocks[0].shape[1]
+    count = near[0] + near[1]
     return pl.pallas_call(
         functools.partial(middle_kernel, frames, near, far),
         out_shape=(
-            jax.ShapeDtypeStruct((2, RADIX * 8 * inputs, KEPT), jnp.float32),
+            jax.ShapeDtypeStruct((2, RADIX, 8 * inputs, KEPT), jnp.float32),
+            jax.ShapeDtypeStruct((2, RADIX, (count - 8) * inputs, KEPT), jnp.float32),
             jax.ShapeDtypeStruct(outer_begun.shape, jnp.float32),
         ),
         in_specs=[VMEM] * 9,
-        out_specs=(VMEM, VMEM),
-        scratch_shapes=scratch(inputs),
+        out_specs=(VMEM,) * 3,
+        scratch_shapes=scratch(inputs, count),
         compiler_params=pltpu.CompilerParams(vmem_limit_bytes=VMEM_LIMIT),
         cost_estimate=pl.CostEstimate(flops=3 * 10**9, bytes_accessed=5 * 2**20, transcendentals=0),
         name="middle_frames",
     )(*near_blocks, taps, keep, twist, table, factor, begun, outer_begun)
 
 
-def outer_frames_call(far_blocks, taps, keep, twist, table, factor, middle, begun, frames, near, far):
+def outer_frames_call(far_blocks, taps, keep, twist, table, factor, middle, edge, begun, frames, near, far):
     inputs = far_blocks[0].shape[1]
     messages = KEPT * 4 * inputs
     return pl.pallas_call(
         functools.partial(outer_kernel, frames, near, far),
         out_shape=jax.ShapeDtypeStruct((messages, LANES), jnp.bfloat16),
-        in_specs=[VMEM] * 9,
+        in_specs=[VMEM] * 10,
         out_specs=VMEM,
-        scratch_shapes=scratch(inputs)
-        + [pltpu.VMEM((2, RADIX * 8 * inputs, KEPT), jnp.float32), pltpu.VMEM((messages, LANES), jnp.float32)],
+        scratch_shapes=scratch(inputs, SLOT - near[0] - near[1])
+        + [pltpu.VMEM((2, RADIX, 8 * inputs, KEPT), jnp.float32), pltpu.VMEM((messages, LANES), jnp.float32)],
         compiler_params=pltpu.CompilerParams(vmem_limit_bytes=VMEM_LIMIT),
         name="outer_frames",
-    )(*far_blocks, taps, keep, twist, table, factor, middle, begun)
-
-
-def cut_kernel(spans, in_ref, *refs):
-    outs, sems = refs[:-1], refs[-1]
-    copies = [
-        pltpu.make_async_copy(in_ref.at[:, :, start:stop], out, sems.at[i])
-        for i, ((start, stop), out) in enumerate(zip(spans, outs))
-    ]
-    for copy in copies:
-        copy.start()
-    for copy in copies:
-        copy.wait()
-
-
-def cut_spans(samples, spans):
-    return pl.pallas_call(
-        functools.partial(cut_kernel, spans),
-        out_shape=[jax.ShapeDtypeStruct(samples.shape[:2] + (b - a,), samples.dtype) for a, b in spans],
-        in_specs=[pl.BlockSpec(memory_space=pltpu.HBM)],
-        out_specs=[VMEM] * len(spans),
-        scratch_shapes=[pltpu.SemaphoreType.DMA((len(spans),))],
-        compiler_params=pltpu.CompilerParams(vmem_limit_bytes=WHOLE_VMEM),
-        name="cut",
-    )(samples)
+    )(*far_blocks, taps, keep, twist, table, factor, middle, edge, begun)
 
 
 def correlate_kernel(normalizer, words_ref, out_ref, joined, swapped, result, sems):
@@ -351,33 +346,23 @@
     size = stations * inputs
     half = size // 2
 
-    some = stations
-    lane = lax.broadcasted_iota(jnp.int32, (some * inputs, LANES), 1)
-    sign = jnp.where(lane < LANES // 2, 1.0, -1.0)
-
-    def trade(block, _):
-        span = pl.ds(pl.multiple_of(block * some * inputs, some * inputs), some * inputs)
-        for q in range(times // 4):
-            held = [
-                words_ref[pl.ds(block * some, some), 4 * q + r].astype(jnp.float32).reshape(some * inputs, LANES)
-                for r in range(4)
-            ]
-            for bit in (1, 2):
-                shift = bit * SLOT
-                left = (lane // shift) % 2 == 0
-                for r in range(4):
-                    if not r & bit:
-                        x, y = held[r], held[r | bit]
-                        held[r] = jnp.where(left, x, pltpu.roll(y, shift, 1))
-                        held[r | bit] = jnp.where(left, pltpu.roll(x, LANES - shift, 1), y)
-            for c in range(4):
-                lanes = pl.ds(q * LANES, LANES)
-                joined[c, span, lanes] = held[c].astype(jnp.bfloat16)
-                other = pltpu.roll(held[c], LANES // 2, 1) * sign
-                swapped[c, span, lanes] = other.astype(jnp.bfloat16)
-        return 0
-
-    lax.fori_loop(0, stations // some, trade, 0)
+    lane = lax.broadcasted_iota(jnp.int32, (size, LANES), 1)
+    sign = jnp.where(lane < LANES // 2, 1.0, -1.0).astype(jnp.bfloat16)
+
+    for q in range(times // 4):
+        held = [words_ref[:, 4 * q + r].astype(jnp.float32).reshape(size, LANES).astype(jnp.bfloat16) for r in range(4)]
+        for bit in (1, 2):
+            shift = bit * SLOT
+            left = (lane // shift) % 2 == 0
+            for r in range(4):
+                if not r & bit:
+                    x, y = held[r], held[r | bit]
+                    held[r] = jnp.where(left, x, pltpu.roll(y, shift, 1))
+                    held[r | bit] = jnp.where(left, pltpu.roll(x, LANES - shift, 1), y)
+        for c in range(4):
+            lanes = slice(q * LANES, (q + 1) * LANES)
+            joined[c, :, lanes] = held[c]
+            swapped[c, :, lanes] = pltpu.roll(held[c], LANES // 2, 1) * sign
 
     def product(left, right):
         return lax.dot_general(
@@ -426,34 +411,35 @@
     inputs = samples.shape[1]
     frames = samples.shape[2] // length
     stations, times = lax.axis_size("stn"), lax.axis_size("tm")
-    near, far = (4, 4), (4, 3)
-    cut = frames - near[0]
+    near, far = (5, 5), (2, 3)
     onward = [(i, i + 1) for i in range(times - 1)]
     backward = [(i, (i - 1) % times) for i in range(times)]
 
-    spans = [
-        (cut, frames),
-        (0, near[1]),
-        (cut - far[0], cut),
-        (near[1], near[1] + far[1]),
-    ]
-    spans = [(a * length, b * length) for a, b in spans]
-    blocks = cut_spans(samples, spans[:2]) + cut_spans(samples, spans[2:])
-    before, after, far_before, far_after = [
-        lax.ppermute(block, "tm", route) for block, route in zip(blocks, (onward, backward) * 2)
-    ]
+    def third(whole, which):
+        span = frames // 3 * length
+        return lax.slice_in_dim(whole, which * span, (which + 1) * span, axis=2)
+
+    late = third(samples, 2)
+    before = lax.ppermute(late, "tm", onward)
+    later, late = lax.optimization_barrier((samples, late))
+    early = third(later, 0)
+    after = lax.ppermute(early, "tm", backward)
+    latest, early = lax.optimization_barrier((later, early))
+    pieces = (early, third(latest, 1), late)
     keep = jnp.where(lax.axis_index("tm") == times - 1, 0.0, 1.0)
     keep = jnp.broadcast_to(keep.astype(jnp.float32), (inputs, LANES))
     table = split_table()
     rescale = 16.0 / math.sqrt(length)
-    begun, outer_begun, factor, wide_taps, twist = own_blocks_call(
-        samples, taps, keep, scales, rescale, frames, near, far
+    begun, outer_begun, factor, wide_taps, twist, early_far, late_far = own_blocks_call(
+        pieces, taps, keep, scales, rescale, frames, near, far
     )
-    middle, outer_begun = middle_frames_call(
+    far_after = lax.ppermute(early_far, "tm", backward)
+    far_before = lax.ppermute(late_far, "tm", onward)
+    middle, edge, outer_begun = middle_frames_call(
         (before, after), wide_taps, keep, twist, table, factor, begun, outer_begun, frames, near, far
     )
     words = outer_frames_call(
-        (far_before, far_after), wide_taps, keep, twist, table, factor, middle, outer_begun, frames, near, far
+        (far_before, far_after), wide_taps, keep, twist, table, factor, middle, edge, outer_begun, frames, near, far
     )
     words = words.reshape(stations * times, inputs, LANES)
     words = lax.all_to_all(words, ("stn", "tm"), split_axis=0, concat_axis=0, tiled=True)

time: 120 us -> 119 us (level)
  Pallas kernels: 19 us -> 13.4 us
  waiting for transfers between devices: 0.01 us -> 4.65 us
    ppermute x4, waiting for transfers between devices: 0.01 us -> 4.65 us  [the longest x1 2.57 us: body(): far_before = lax.ppermute(late_far, 'tm', onward)]
    pallas_call x2 -> x0, Pallas kernels: 4.43 us -> none  [cut_spans(): pl.pallas_call(functools.partial(cut_kernel, spans), out_shape=[jax.Shape...]
    slice x0 -> x3, local copies, waits for them, and re-layouts: none -> 3.44 us  [third(): return lax.slice_in_dim(whole, which * span, (which + 1) * span, axis=2)]
    unnamed x12 -> x10, local copies, waits for them, and re-layouts: 2.43 us -> 0.02 us
  transfers between devices with their start and end apart: 4 -> 4, of which waited for: 0 -> 2; matrix products, arithmetic and copies ran while one was open for 0% -> 1% of each run, Pallas kernels for 9% -> 7%
where the time goes in v6:
time: 119 us
  blocking collectives  84.5 us (71%)
  Pallas kernels  13.4 us (11%)
  starting transfers between devices  13 us (11%)
  waiting for transfers between devices  4.65 us (4%)
  local copies, waits for them, and re-layouts  3.46 us (3%)
    all_to_all x1, blocking collectives, body(): lax.all_to_all(words, ('stn', 'tm'), split_axis=0, concat_axis=0, tiled=T...  84.5 us
    ppermute x1, starting transfers between devices, body(): after = lax.ppermute(early, 'tm', backward)  6.4 us
    pallas_call x1, Pallas kernels, own_blocks_call(): pl.pallas_call(functools.partial(own_kernel, frames, near, far, rescale),...  4.23 us
    pallas_call x1, Pallas kernels, middle_frames_call(): pl.pallas_call(functools.partial(middle_kernel, frames, near, far), out_s...  3.54 us
    slice x3, local copies, waits for them, and re-layouts, third(): return lax.slice_in_dim(whole, which * span, (which + 1) * span, axis=2)  3.44 us
    pallas_call x1, Pallas kernels, outer_frames_call(): pl.pallas_call(functools.partial(outer_kernel, frames, near, far), out_sh...  3.29 us
    ppermute x1, starting transfers between devices, body(): far_before = lax.ppermute(late_far, 'tm', onward)  2.96 us
    ppermute x1, waiting for transfers between devices, body(): far_before = lax.ppermute(late_far, 'tm', onward)  2.57 us
  transfers between devices with their start and end apart: 4, of which 2 were waited for; matrix products, arithmetic and copies ran while one was open for 1% of the time, Pallas kernels for 7%

profile of v6, /device:TPU:1, one launch (start us, length us, event | category | flops | bytes accessed | tf_op | source)
XLA Modules:
  0.0 119.1 jit_solution(17438772972492785352)
XLA Ops:
  0.0 0.0 copy-start.3
  0.0 0.0 copy-start.4
  0.0 0.0 copy-start.2
  0.0 0.0 copy-start.1
  0.0 1.2 slice.9.late_ref
  1.2 1.1 slice.10.early_ref
  2.3 6.4 %collective-permute-start.3 = (bf16[2,8,20480]{2,1,0:T(8,128)(2,1)S(1)}, bf16[2,8,20480]{2,1,0:T(8,128)(2,1)S(1)}, u32[]{:S(2)}, u32[]{:S(2)}) collective-permute-start(bf16[2,8,20480]{2,1,0:T(8,128)(2,1)S(1)} %slice.10.early_ref), channel_id=1, source_target_pairs={{0,7},{1,0},{2,1},{3,2},{4,3},{5,4},{6,5},{7,6},{8,15},{9,8},{10,9... | collective-permute-start | bytes 1966088 | tf_op jit(solution)/shard_map/ppermute | solution.py:426
  8.7 1.3 %collective-permute-start.2 = (bf16[2,8,20480]{2,1,0:T(8,128)(2,1)S(1)}, bf16[2,8,20480]{2,1,0:T(8,128)(2,1)S(1)}, u32[]{:S(2)}, u32[]{:S(2)}) collective-permute-start(bf16[2,8,20480]{2,1,0:T(8,128)(2,1)S(1)} %slice.9.late_ref), channel_id=1, source_target_pairs={{0,1},{1,2},{2,3},{3,4},{4,5},{5,6},{6,7},{8,9},{9,10},{10,11},{11... | collective-permute-start | bytes 1966088 | tf_op jit(solution)/shard_map/ppermute | solution.py:423
  10.1 1.1 slice.11.between_ref
  11.2 0.0 copy-done.3
  11.2 0.0 copy-done.4
  11.3 0.0 copy-done.2
  11.3 0.0 copy-done.1
  11.3 0.0 copy-start
  11.3 4.2 %own_blocks.1 = (f32[2,32,10,8,128]{4,3,2,1,0:T(8,128)S(1)}, f32[2,32,5,8,128]{4,3,2,1,0:T(8,128)S(1)}, f32[16,8,128]{2,1,0:T(8,128)S(1)}, f32[16,4096]{1,0:T(8,...) custom-call(bf16[2,8,20480]{2,1,0:T(8,128)(2,1)S(1)} %slice.10.early_ref, ...), custom_call_target="tpu_custom_call" | custom-call | flops 3000000000 | bytes 6291456 | tf_op jit(solution)/shard_map/own_blocks/pallas_call | solution.py:291
  15.5 2.3 %collective-permute-start.1 = (bf16[2,8,12288]{2,1,0:T(8,128)(2,1)S(1)}, bf16[2,8,12288]{2,1,0:T(8,128)(2,1)S(1)}, u32[]{:S(2)}, u32[]{:S(2)}) collective-permute-start(bf16[2,8,12288]{2,1,0:T(8,128)(2,1)S(1)} %get-tuple-element.24), channel_id=1, source_target_pairs={{0,7},{1,0},{2,1},{3,2},{4,3},{5,4},{6,5},{7,6},{8,15},{9,8},{10,9... | collective-permute-start | bytes 1179656 | tf_op jit(solution)/shard_map/ppermute | solution.py:436
  17.9 3.0 %collective-permute-start = (bf16[2,8,8192]{2,1,0:T(8,128)(2,1)S(1)}, bf16[2,8,8192]{2,1,0:T(8,128)(2,1)S(1)}, u32[]{:S(2)}, u32[]{:S(2)}) collective-permute-start(bf16[2,8,8192]{2,1,0:T(8,128)(2,1)S(1)} %get-tuple-element.23), channel_id=1, source_target_pairs={{0,1},{1,2},{2,3},{3,4},{4,5},{5,6},{6,7},{8,9},{9,10},{10,11},{11... | collective-permute-start | bytes 786440 | tf_op jit(solution)/shard_map/ppermute | solution.py:437
  20.8 0.0 collective-permute-done.3.after_ref
  20.8 0.0 collective-permute-done.2.before_ref
  20.9 0.0 copy-done
  20.9 3.5 %middle_frames.1 = (f32[2,16,64,128]{3,2,1,0:T(8,128)S(1)}, f32[2,16,16,128]{3,2,1,0:T(8,128)S(1)}, f32[2,32,5,8,128]{4,3,2,1,0:T(8,128)S(1)}) custom-call(bf16[2,8,20480]{2,1,0:T(8,128)(2,1)S(1)} %collective-permute-done.2.before_ref, bf16[2,8,20480]{2,1,0:T(8,128)(2,1)S(1)} %collective-permute-done.3.after_ref, f32[16,4096]{1,0:T(8,128)S(1)} %get-tuple-element.25.taps_ref, ...), custom_call_target="tpu_custom_call" | custom-call | flops 3000000000 | bytes 5242880 | tf_op jit(solution)/shard_map/middle_frames/pallas_call | solution.py:313
  24.4 2.6 %collective-permute-done.before_ref = bf16[2,8,8192]{2,1,0:T(8,128)(2,1)S(1)} collective-permute-done((bf16[2,8,8192]{2,1,0:T(8,128)(2,1)S(1)}, bf16[2,8,8192]{2,1,0:T(8,128)(2,1)S(1)}, u32[]{:S(2)}, u32[]{:S(2)}) %collective-permute-start) | collective-permute-done | bytes 262176 | tf_op jit(solution)/shard_map/ppermute | solution.py:437
  27.0 2.1 %collective-permute-done.1.after_ref = bf16[2,8,12288]{2,1,0:T(8,128)(2,1)S(1)} collective-permute-done((bf16[2,8,12288]{2,1,0:T(8,128)(2,1)S(1)}, bf16[2,8,12288]{2,1,0:T(8,128)(2,1)S(1)}, u32[]{:S(2)}, u32[]{:S(2)}) %collective-permute-start.1) | collective-permute-done | bytes 393248 | tf_op jit(solution)/shard_map/ppermute | solution.py:436
  29.1 3.3 %outer_frames.1 = bf16[4096,128]{1,0:T(8,128)(2,1)S(1)} custom-call(bf16[2,8,8192]{2,1,0:T(8,128)(2,1)S(1)} %collective-permute-done.before_ref, bf16[2,8,12288]{2,1,0:T(8,128)(2,1)S(1)} %collective-permute-done.1.after_ref, f32[16,4096]{1,0:T(8,128)S(1)} %get-tuple-element.25.taps_ref, f32[8,128]{1,0:T(8,128)S(1)} %broadcast_in_dim.3.keep_ref, ...), custom_call_target="tpu_custom_call" | custom-call | tf_op jit(solution)/shard_map/outer_frames/pallas_call | solution.py:332
  32.4 84.5 %all_to_all.5 = bf16[512,8,128]{2,1,0:T(8,128)(2,1)S(1)} all-to-all(bf16[512,8,128]{2,1,0:T(8,128)(2,1)S(1)} %bitcast.3), channel_id=1, replica_groups=mesh['stn'=64,'tm'=8] {'stn','tm'}, dimensions={0} | all-to-all | bytes 2097152 | tf_op jit(solution)/shard_map/all_to_all | solution.py:445
  116.8 2.3 %correlate.1 = bf16[4,512,512]{2,1,0:T(8,128)(2,1)} custom-call(bf16[64,8,8,128]{3,2,1,0:T(8,128)(2,1)S(1)} %bitcast.2), custom_call_target="tpu_custom_call" | custom-call | tf_op jit(solution)/shard_map/correlate/pallas_call | solution.py:397
  (1 shorter events, 0.0 us)
Async XLA Ops:
  0.0 11.2 %copy-start.3 = (f32[2,16,256]{2,1,0:T(8,128)S(1)}, f32[2,16,256]{2,1,0:T(8,128)}, u32[]{:S(2)}) copy-start(f32[2,16,256]{2,1,0:T(8,128)} %constant.21.clone.twist_ref) | copy-start | bytes 98308
  0.0 11.2 %copy-start.4 = (bf16[128,128]{1,0:T(8,128)(2,1)S(1)}, bf16[128,128]{1,0:T(8,128)(2,1)}, u32[]{:S(2)}) copy-start(bf16[128,128]{1,0:T(8,128)(2,1)} %constant.20.clone.order_ref) | copy-start | bytes 98308
  0.0 11.3 %copy-start.2 = (s32[8,2048]{1,0:T(8,128)S(1)}, s32[8,2048]{1,0:T(8,128)}, u32[]{:S(2)}) copy-start(s32[8,2048]{1,0:T(8,128)} %scales_ref.1) | copy-start | bytes 196612
  0.0 11.3 %copy-start.1 = (bf16[16,4096]{1,0:T(8,128)(2,1)S(1)}, bf16[16,4096]{1,0:T(8,128)(2,1)}, u32[]{:S(2)}) copy-start(bf16[16,4096]{1,0:T(8,128)(2,1)} %taps_ref.1) | copy-start | bytes 393220
  2.3 18.5 %collective-permute-start.3 = (bf16[2,8,20480]{2,1,0:T(8,128)(2,1)S(1)}, bf16[2,8,20480]{2,1,0:T(8,128)(2,1)S(1)}, u32[]{:S(2)}, u32[]{:S(2)}) collective-permute-start(bf16[2,8,20480]{2,1,0:T(8,128)(2,1)S(1)} %slice.10.early_ref), channel_id=1, source_target_pairs={{0,7},{1,0},{2,1},{3,2},{4,3},{5,4},{6,5},{7,6},{8,15},{9,8},{10,9... | collective-permute-start | bytes 1966088 | tf_op jit(solution)/shard_map/ppermute | solution.py:426
  8.7 12.1 %collective-permute-start.2 = (bf16[2,8,20480]{2,1,0:T(8,128)(2,1)S(1)}, bf16[2,8,20480]{2,1,0:T(8,128)(2,1)S(1)}, u32[]{:S(2)}, u32[]{:S(2)}) collective-permute-start(bf16[2,8,20480]{2,1,0:T(8,128)(2,1)S(1)} %slice.9.late_ref), channel_id=1, source_target_pairs={{0,1},{1,2},{2,3},{3,4},{4,5},{5,6},{6,7},{8,9},{9,10},{10,11},{11... | collective-permute-start | bytes 1966088 | tf_op jit(solution)/shard_map/ppermute | solution.py:423
  11.3 9.6 %copy-start = (bf16[512,512]{1,0:T(8,128)(2,1)S(1)}, bf16[512,512]{1,0:T(8,128)(2,1)}, u32[]{:S(2)}) copy-start(bf16[512,512]{1,0:T(8,128)(2,1)} %constant.24.table_ref) | copy-start | bytes 1572868
  15.5 13.5 %collective-permute-start.1 = (bf16[2,8,12288]{2,1,0:T(8,128)(2,1)S(1)}, bf16[2,8,12288]{2,1,0:T(8,128)(2,1)S(1)}, u32[]{:S(2)}, u32[]{:S(2)}) collective-permute-start(bf16[2,8,12288]{2,1,0:T(8,128)(2,1)S(1)} %get-tuple-element.24), channel_id=1, source_target_pairs={{0,7},{1,0},{2,1},{3,2},{4,3},{5,4},{6,5},{7,6},{8,15},{9,8},{10,9... | collective-permute-start | bytes 1179656 | tf_op jit(solution)/shard_map/ppermute | solution.py:436
  17.9 9.1 %collective-permute-start = (bf16[2,8,8192]{2,1,0:T(8,128)(2,1)S(1)}, bf16[2,8,8192]{2,1,0:T(8,128)(2,1)S(1)}, u32[]{:S(2)}, u32[]{:S(2)}) collective-permute-start(bf16[2,8,8192]{2,1,0:T(8,128)(2,1)S(1)} %get-tuple-element.23), channel_id=1, source_target_pairs={{0,1},{1,2},{2,3},{3,4},{4,5},{5,6},{6,7},{8,9},{9,10},{10,11},{11... | collective-permute-start | bytes 786440 | tf_op jit(solution)/shard_map/ppermute | solution.py:437

commit v7 on v6

--- a/solution.py
+++ b/solution.py
@@ -106,7 +106,7 @@
                 out_ref[comp, chunk, slot] = late
         return 0
 
-    lax.fori_loop(0, length // LANES, filter_chunk, 0)
+    lax.fori_loop(0, length // LANES, filter_chunk, 0, unroll=4)
 
 
 def transform(used, slots, twist_ref, table_ref, factor_ref, filt, rows, store):
@@ -222,7 +222,7 @@
 
 def outer_kernel(
     frames, near, far, before_ref, after_ref, taps_ref, keep_ref, twist_ref, table_ref, factor_ref, middle_ref,
-    edge_ref, begun_ref, out_ref, filt, rows, edge, words,
+    edge_ref, begun_ref, out_ref, filt, rows, edge, first_words, second_words,
 ):
     sources = window_of(frames, near, far, (before_ref,) + (None,) * 5 + (after_ref,))
     middle, plan = split_frames(frames, near, far)
@@ -232,25 +232,25 @@
 
     def store(comp, some, part):
         edge[comp, some, taken:] = part
+        if comp == 1:
+            arrange(some.start // 8, (first_words, second_words)[some.start // 8])
+
+    def arrange(pair, words):
+        for high in range(2):
+            for i in range(inputs):
+                parts = []
+                for comp in range(2):
+                    for channel in range(4):
+                        k1 = (pair * 2 + high) * 4 + channel
+                        for half in (middle_ref, edge):
+                            parts.append(half[comp, k1, pl.ds(i, 8, stride=inputs), :])
+                turned = jnp.concatenate(parts, axis=0).T
+                words[pl.ds(high * inputs + i, KEPT, stride=2 * inputs), :] = turned
+        narrow = words[...].reshape(KEPT, 2 * inputs, LANES).astype(jnp.bfloat16)
+        out_ref[:, pair * 2 * inputs : (pair + 1) * 2 * inputs, :] = narrow
 
     filter_blocks(plan, given(sources[0]), sources, taps_ref, keep_ref, filt, begun_ref)
     transform(len(plan), SLOT - len(middle), twist_ref, table_ref, factor_ref, filt, rows, store)
-
-    for high in range(RADIX // 4):
-        for i in range(inputs):
-            parts = []
-            for comp in range(2):
-                for channel in range(4):
-                    for half in (middle_ref, edge):
-                        parts.append(half[comp, high * 4 + channel, pl.ds(i, 8, stride=inputs), :])
-            words[pl.ds(high * inputs + i, KEPT, stride=4 * inputs), :] = jnp.concatenate(parts, axis=0).T
-
-    def narrow(step, _):
-        span = pl.ds(pl.multiple_of(step * 1024, 1024), 1024)
-        out_ref[span, :] = words[span, :].astype(jnp.bfloat16)
-        return 0
-
-    lax.fori_loop(0, words.shape[0] // 1024, narrow, 0, unroll=True)
 
 
 def split_table():
@@ -328,14 +328,14 @@
 
 def outer_frames_call(far_blocks, taps, keep, twist, table, factor, middle, edge, begun, frames, near, far):
     inputs = far_blocks[0].shape[1]
-    messages = KEPT * 4 * inputs
     return pl.pallas_call(
         functools.partial(outer_kernel, frames, near, far),
-        out_shape=jax.ShapeDtypeStruct((messages, LANES), jnp.bfloat16),
+        out_shape=jax.ShapeDtypeStruct((KEPT, 4 * inputs, LANES), jnp.bfloat16),
         in_specs=[VMEM] * 10,
         out_specs=VMEM,
         scratch_shapes=scratch(inputs, SLOT - near[0] - near[1])
-        + [pltpu.VMEM((2, RADIX, 8 * inputs, KEPT), jnp.float32), pltpu.VMEM((messages, LANES), jnp.float32)],
+        + [pltpu.VMEM((2, RADIX, 8 * inputs, KEPT), jnp.float32)]
+        + [pltpu.VMEM((KEPT * 2 * inputs, LANES), jnp.float32)] * 2,
         compiler_params=pltpu.CompilerParams(vmem_limit_bytes=VMEM_LIMIT),
         name="outer_frames",
     )(*far_blocks, taps, keep, twist, table, factor, middle, edge, begun)

time: 119 us -> 119 us (level)
  Pallas kernels: 13.4 us -> 11.6 us
  transfers between devices with their start and end apart: 4 -> 4, of which waited for: 2 -> 3; matrix products, arithmetic and copies ran while one was open for 1% -> 1% of each run, Pallas kernels for 7% -> 6%
where the time goes in v7:
time: 119 us; the launch traced here: 118 us
  blocking collectives  84.5 us (71%)
  starting transfers between devices  13 us (11%)
  Pallas kernels  11.6 us (10%)
  waiting for transfers between devices  5.53 us (5%)
  local copies, waits for them, and re-layouts  3.46 us (3%)
    all_to_all x1, blocking collectives, body(): lax.all_to_all(words, ('stn', 'tm'), split_axis=0, concat_axis=0, tiled=T...  84.5 us
    ppermute x1, starting transfers between devices, body(): after = lax.ppermute(early, 'tm', backward)  6.4 us
    pallas_call x1, Pallas kernels, own_blocks_call(): pl.pallas_call(functools.partial(own_kernel, frames, near, far, rescale),...  3.77 us
    slice x3, local copies, waits for them, and re-layouts, third(): return lax.slice_in_dim(whole, which * span, (which + 1) * span, axis=2)  3.44 us
    pallas_call x1, Pallas kernels, middle_frames_call(): pl.pallas_call(functools.partial(middle_kernel, frames, near, far), out_s...  3.14 us
    ppermute x1, starting transfers between devices, body(): far_before = lax.ppermute(late_far, 'tm', onward)  2.96 us
    ppermute x1, waiting for transfers between devices, body(): far_before = lax.ppermute(late_far, 'tm', onward)  2.74 us
    ppermute x1, waiting for transfers between devices, body(): far_after = lax.ppermute(early_far, 'tm', backward)  2.53 us
  transfers between devices with their start and end apart: 4, of which 3 were waited for; matrix products, arithmetic and copies ran while one was open for 1% of the time, Pallas kernels for 6%

profile of v7, /device:TPU:1, one launch (start us, length us, event | category | flops | bytes accessed | tf_op | source)
XLA Modules:
  0.0 118.2 jit_solution(9227085560120474476)
XLA Ops:
  0.0 0.0 copy-start.3
  0.0 0.0 copy-start.4
  0.0 0.0 copy-start.2
  0.0 0.0 copy-start.1
  0.0 1.2 slice.9.late_ref
  1.2 1.1 slice.10.early_ref
  2.3 6.4 %collective-permute-start.3 = (bf16[2,8,20480]{2,1,0:T(8,128)(2,1)S(1)}, bf16[2,8,20480]{2,1,0:T(8,128)(2,1)S(1)}, u32[]{:S(2)}, u32[]{:S(2)}) collective-permute-start(bf16[2,8,20480]{2,1,0:T(8,128)(2,1)S(1)} %slice.10.early_ref), channel_id=1, source_target_pairs={{0,7},{1,0},{2,1},{3,2},{4,3},{5,4},{6,5},{7,6},{8,15},{9,8},{10,9... | collective-permute-start | bytes 1966088 | tf_op jit(solution)/shard_map/ppermute | solution.py:426
  8.7 1.3 %collective-permute-start.2 = (bf16[2,8,20480]{2,1,0:T(8,128)(2,1)S(1)}, bf16[2,8,20480]{2,1,0:T(8,128)(2,1)S(1)}, u32[]{:S(2)}, u32[]{:S(2)}) collective-permute-start(bf16[2,8,20480]{2,1,0:T(8,128)(2,1)S(1)} %slice.9.late_ref), channel_id=1, source_target_pairs={{0,1},{1,2},{2,3},{3,4},{4,5},{5,6},{6,7},{8,9},{9,10},{10,11},{11... | collective-permute-start | bytes 1966088 | tf_op jit(solution)/shard_map/ppermute | solution.py:423
  10.1 1.1 slice.11.between_ref
  11.2 0.0 copy-done.3
  11.2 0.0 copy-done.4
  11.3 0.0 copy-done.2
  11.3 0.0 copy-done.1
  11.3 0.0 copy-start
  11.3 3.8 %own_blocks.1 = (f32[2,32,10,8,128]{4,3,2,1,0:T(8,128)S(1)}, f32[2,32,5,8,128]{4,3,2,1,0:T(8,128)S(1)}, f32[16,8,128]{2,1,0:T(8,128)S(1)}, f32[16,4096]{1,0:T(8,...) custom-call(bf16[2,8,20480]{2,1,0:T(8,128)(2,1)S(1)} %slice.10.early_ref, ...), custom_call_target="tpu_custom_call" | custom-call | flops 3000000000 | bytes 6291456 | tf_op jit(solution)/shard_map/own_blocks/pallas_call | solution.py:291
  15.1 2.3 %collective-permute-start.1 = (bf16[2,8,12288]{2,1,0:T(8,128)(2,1)S(1)}, bf16[2,8,12288]{2,1,0:T(8,128)(2,1)S(1)}, u32[]{:S(2)}, u32[]{:S(2)}) collective-permute-start(bf16[2,8,12288]{2,1,0:T(8,128)(2,1)S(1)} %get-tuple-element.24), channel_id=1, source_target_pairs={{0,7},{1,0},{2,1},{3,2},{4,3},{5,4},{6,5},{7,6},{8,15},{9,8},{10,9... | collective-permute-start | bytes 1179656 | tf_op jit(solution)/shard_map/ppermute | solution.py:436
  17.4 3.0 %collective-permute-start = (bf16[2,8,8192]{2,1,0:T(8,128)(2,1)S(1)}, bf16[2,8,8192]{2,1,0:T(8,128)(2,1)S(1)}, u32[]{:S(2)}, u32[]{:S(2)}) collective-permute-start(bf16[2,8,8192]{2,1,0:T(8,128)(2,1)S(1)} %get-tuple-element.23), channel_id=1, source_target_pairs={{0,1},{1,2},{2,3},{3,4},{4,5},{5,6},{6,7},{8,9},{9,10},{10,11},{11... | collective-permute-start | bytes 786440 | tf_op jit(solution)/shard_map/ppermute | solution.py:437
  20.4 0.3 collective-permute-done.3.after_ref
  20.6 0.0 collective-permute-done.2.before_ref
  20.6 0.0 copy-done
  20.6 3.1 %middle_frames.1 = (f32[2,16,64,128]{3,2,1,0:T(8,128)S(1)}, f32[2,16,16,128]{3,2,1,0:T(8,128)S(1)}, f32[2,32,5,8,128]{4,3,2,1,0:T(8,128)S(1)}) custom-call(bf16[2,8,20480]{2,1,0:T(8,128)(2,1)S(1)} %collective-permute-done.2.before_ref, bf16[2,8,20480]{2,1,0:T(8,128)(2,1)S(1)} %collective-permute-done.3.after_ref, f32[16,4096]{1,0:T(8,128)S(1)} %get-tuple-element.25.taps_ref, ...), custom_call_target="tpu_custom_call" | custom-call | flops 3000000000 | bytes 5242880 | tf_op jit(solution)/shard_map/middle_frames/pallas_call | solution.py:313
  23.8 2.7 %collective-permute-done.before_ref = bf16[2,8,8192]{2,1,0:T(8,128)(2,1)S(1)} collective-permute-done((bf16[2,8,8192]{2,1,0:T(8,128)(2,1)S(1)}, bf16[2,8,8192]{2,1,0:T(8,128)(2,1)S(1)}, u32[]{:S(2)}, u32[]{:S(2)}) %collective-permute-start) | collective-permute-done | bytes 262176 | tf_op jit(solution)/shard_map/ppermute | solution.py:437
  26.5 2.5 %collective-permute-done.1.after_ref = bf16[2,8,12288]{2,1,0:T(8,128)(2,1)S(1)} collective-permute-done((bf16[2,8,12288]{2,1,0:T(8,128)(2,1)S(1)}, bf16[2,8,12288]{2,1,0:T(8,128)(2,1)S(1)}, u32[]{:S(2)}, u32[]{:S(2)}) %collective-permute-start.1) | collective-permute-done | bytes 393248 | tf_op jit(solution)/shard_map/ppermute | solution.py:436
  29.1 2.4 %outer_frames.1 = bf16[128,32,128]{2,1,0:T(8,128)(2,1)S(1)} custom-call(bf16[2,8,8192]{2,1,0:T(8,128)(2,1)S(1)} %collective-permute-done.before_ref, bf16[2,8,12288]{2,1,0:T(8,128)(2,1)S(1)} %collective-permute-done.1.after_ref, f32[16,4096]{1,0:T(8,128)S(1)} %get-tuple-element.25.taps_ref, f32[8,128]{1,0:T(8,128)S(1)} %broadcast_in_dim.3.keep_ref, ...), custom_call_target="tpu_custom_call" | custom-call | tf_op jit(solution)/shard_map/outer_frames/pallas_call | solution.py:331
  31.4 84.5 %all_to_all.5 = bf16[512,8,128]{2,1,0:T(8,128)(2,1)S(1)} all-to-all(bf16[512,8,128]{2,1,0:T(8,128)(2,1)S(1)} %bitcast.3), channel_id=1, replica_groups=mesh['stn'=64,'tm'=8] {'stn','tm'}, dimensions={0} | all-to-all | bytes 2097152 | tf_op jit(solution)/shard_map/all_to_all | solution.py:445
  115.9 2.3 %correlate.1 = bf16[4,512,512]{2,1,0:T(8,128)(2,1)} custom-call(bf16[64,8,8,128]{3,2,1,0:T(8,128)(2,1)S(1)} %bitcast.2), custom_call_target="tpu_custom_call" | custom-call | tf_op jit(solution)/shard_map/correlate/pallas_call | solution.py:397
  (1 shorter events, 0.0 us)
Async XLA Ops:
  0.0 11.2 %copy-start.3 = (f32[2,16,256]{2,1,0:T(8,128)S(1)}, f32[2,16,256]{2,1,0:T(8,128)}, u32[]{:S(2)}) copy-start(f32[2,16,256]{2,1,0:T(8,128)} %constant.21.clone.twist_ref) | copy-start | bytes 98308
  0.0 11.2 %copy-start.4 = (bf16[128,128]{1,0:T(8,128)(2,1)S(1)}, bf16[128,128]{1,0:T(8,128)(2,1)}, u32[]{:S(2)}) copy-start(bf16[128,128]{1,0:T(8,128)(2,1)} %constant.20.clone.order_ref) | copy-start | bytes 98308
  0.0 11.3 %copy-start.2 = (s32[8,2048]{1,0:T(8,128)S(1)}, s32[8,2048]{1,0:T(8,128)}, u32[]{:S(2)}) copy-start(s32[8,2048]{1,0:T(8,128)} %scales_ref.1) | copy-start | bytes 196612
  0.0 11.3 %copy-start.1 = (bf16[16,4096]{1,0:T(8,128)(2,1)S(1)}, bf16[16,4096]{1,0:T(8,128)(2,1)}, u32[]{:S(2)}) copy-start(bf16[16,4096]{1,0:T(8,128)(2,1)} %taps_ref.1) | copy-start | bytes 393220
  2.3 18.3 %collective-permute-start.3 = (bf16[2,8,20480]{2,1,0:T(8,128)(2,1)S(1)}, bf16[2,8,20480]{2,1,0:T(8,128)(2,1)S(1)}, u32[]{:S(2)}, u32[]{:S(2)}) collective-permute-start(bf16[2,8,20480]{2,1,0:T(8,128)(2,1)S(1)} %slice.10.early_ref), channel_id=1, source_target_pairs={{0,7},{1,0},{2,1},{3,2},{4,3},{5,4},{6,5},{7,6},{8,15},{9,8},{10,9... | collective-permute-start | bytes 1966088 | tf_op jit(solution)/shard_map/ppermute | solution.py:426
  8.7 11.9 %collective-permute-start.2 = (bf16[2,8,20480]{2,1,0:T(8,128)(2,1)S(1)}, bf16[2,8,20480]{2,1,0:T(8,128)(2,1)S(1)}, u32[]{:S(2)}, u32[]{:S(2)}) collective-permute-start(bf16[2,8,20480]{2,1,0:T(8,128)(2,1)S(1)} %slice.9.late_ref), channel_id=1, source_target_pairs={{0,1},{1,2},{2,3},{3,4},{4,5},{5,6},{6,7},{8,9},{9,10},{10,11},{11... | collective-permute-start | bytes 1966088 | tf_op jit(solution)/shard_map/ppermute | solution.py:423
  11.3 9.4 %copy-start = (bf16[512,512]{1,0:T(8,128)(2,1)S(1)}, bf16[512,512]{1,0:T(8,128)(2,1)}, u32[]{:S(2)}) copy-start(bf16[512,512]{1,0:T(8,128)(2,1)} %constant.24.table_ref) | copy-start | bytes 1572868
  15.1 14.0 %collective-permute-start.1 = (bf16[2,8,12288]{2,1,0:T(8,128)(2,1)S(1)}, bf16[2,8,12288]{2,1,0:T(8,128)(2,1)S(1)}, u32[]{:S(2)}, u32[]{:S(2)}) collective-permute-start(bf16[2,8,12288]{2,1,0:T(8,128)(2,1)S(1)} %get-tuple-element.24), channel_id=1, source_target_pairs={{0,7},{1,0},{2,1},{3,2},{4,3},{5,4},{6,5},{7,6},{8,15},{9,8},{10,9... | collective-permute-start | bytes 1179656 | tf_op jit(solution)/shard_map/ppermute | solution.py:436
  17.4 9.1 %collective-permute-start = (bf16[2,8,8192]{2,1,0:T(8,128)(2,1)S(1)}, bf16[2,8,8192]{2,1,0:T(8,128)(2,1)S(1)}, u32[]{:S(2)}, u32[]{:S(2)}) collective-permute-start(bf16[2,8,8192]{2,1,0:T(8,128)(2,1)S(1)} %get-tuple-element.23), channel_id=1, source_target_pairs={{0,1},{1,2},{2,3},{3,4},{4,5},{5,6},{6,7},{8,9},{9,10},{10,11},{11... | collective-permute-start | bytes 786440 | tf_op jit(solution)/shard_map/ppermute | solution.py:437

commit v8 on v7

--- a/solution.py
+++ b/solution.py
@@ -203,7 +203,7 @@
 
 
 def middle_kernel(
-    frames, near, far, before_ref, after_ref, taps_ref, keep_ref, twist_ref, table_ref, factor_ref, begun_ref,
+    frames, near, far, after_ref, before_ref, taps_ref, keep_ref, twist_ref, table_ref, factor_ref, begun_ref,
     outer_begun_ref, out_ref, edge_ref, outer_ref, filt, rows,
 ):
     sources = window_of(frames, near, far, (None, before_ref) + (None,) * 3 + (after_ref, None))
@@ -221,7 +221,7 @@
 
 
 def outer_kernel(
-    frames, near, far, before_ref, after_ref, taps_ref, keep_ref, twist_ref, table_ref, factor_ref, middle_ref,
+    frames, near, far, after_ref, before_ref, taps_ref, keep_ref, twist_ref, table_ref, factor_ref, middle_ref,
     edge_ref, begun_ref, out_ref, filt, rows, edge, first_words, second_words,
 ):
     sources = window_of(frames, near, far, (before_ref,) + (None,) * 5 + (after_ref,))
@@ -411,7 +411,7 @@
     inputs = samples.shape[1]
     frames = samples.shape[2] // length
     stations, times = lax.axis_size("stn"), lax.axis_size("tm")
-    near, far = (5, 5), (2, 3)
+    near, far = (5, 5), (3, 2)
     onward = [(i, i + 1) for i in range(times - 1)]
     backward = [(i, (i - 1) % times) for i in range(times)]
 
@@ -419,12 +419,12 @@
         span = frames // 3 * length
         return lax.slice_in_dim(whole, which * span, (which + 1) * span, axis=2)
 
-    late = third(samples, 2)
+    early = third(samples, 0)
+    after = lax.ppermute(early, "tm", backward)
+    later, early = lax.optimization_barrier((samples, early))
+    late = third(later, 2)
     before = lax.ppermute(late, "tm", onward)
-    later, late = lax.optimization_barrier((samples, late))
-    early = third(later, 0)
-    after = lax.ppermute(early, "tm", backward)
-    latest, early = lax.optimization_barrier((later, early))
+    latest, late = lax.optimization_barrier((later, late))
     pieces = (early, third(latest, 1), late)
     keep = jnp.where(lax.axis_index("tm") == times - 1, 0.0, 1.0)
     keep = jnp.broadcast_to(keep.astype(jnp.float32), (inputs, LANES))
@@ -436,10 +436,10 @@
     far_after = lax.ppermute(early_far, "tm", backward)
     far_before = lax.ppermute(late_far, "tm", onward)
     middle, edge, outer_begun = middle_frames_call(
-        (before, after), wide_taps, keep, twist, table, factor, begun, outer_begun, frames, near, far
+        (after, before), wide_taps, keep, twist, table, factor, begun, outer_begun, frames, near, far
     )
     words = outer_frames_call(
-        (far_before, far_after), wide_taps, keep, twist, table, factor, middle, edge, outer_begun, frames, near, far
+        (far_after, far_before), wide_taps, keep, twist, table, factor, middle, edge, outer_begun, frames, near, far
     )
     words = words.reshape(stations * times, inputs, LANES)
     words = lax.all_to_all(words, ("stn", "tm"), split_axis=0, concat_axis=0, tiled=True)

time: 119 us -> 118 us (level)
  waiting for transfers between devices: 5.53 us -> 4.03 us
  blocking collectives: 84.5 us -> 85.7 us
    ppermute x1, starting transfers between devices: 6.4 us -> 3.62 us  [body(): after = lax.ppermute(early, 'tm', backward)]
    ppermute x1, waiting for transfers between devices: 2.74 us -> 0.01 us  [body(): far_before = lax.ppermute(late_far, 'tm', onward)]
    ppermute x1, starting transfers between devices: 1.33 us -> 4.07 us  [body(): before = lax.ppermute(late, 'tm', onward)]
    ppermute x1, waiting for transfers between devices: 0.26 us -> 1.55 us  [body(): after = lax.ppermute(early, 'tm', backward)]
    ppermute x1, starting transfers between devices: 2.96 us -> 1.68 us  [body(): far_before = lax.ppermute(late_far, 'tm', onward)]
    ppermute x1, starting transfers between devices: 2.33 us -> 3.6 us  [body(): far_after = lax.ppermute(early_far, 'tm', backward)]
    all_to_all x1, blocking collectives: 84.5 us -> 85.7 us  [body(): lax.all_to_all(words, ('stn', 'tm'), split_axis=0, concat_axis=0, tiled=T...]
  transfers between devices with their start and end apart: 4 -> 4, of which waited for: 3 -> 2; matrix products, arithmetic and copies ran while one was open for 1% -> 1% of each run, Pallas kernels for 6% -> 6%
where the time goes in v8:
time: 118 us
  blocking collectives  85.7 us (73%)
  starting transfers between devices  13 us (11%)
  Pallas kernels  11.6 us (10%)
  waiting for transfers between devices  4.03 us (3%)
  local copies, waits for them, and re-layouts  3.46 us (3%)
    all_to_all x1, blocking collectives, body(): lax.all_to_all(words, ('stn', 'tm'), split_axis=0, concat_axis=0, tiled=T...  85.7 us
    ppermute x1, starting transfers between devices, body(): before = lax.ppermute(late, 'tm', onward)  4.07 us
    pallas_call x1, Pallas kernels, own_blocks_call(): pl.pallas_call(functools.partial(own_kernel, frames, near, far, rescale),...  3.78 us
    ppermute x1, starting transfers between devices, body(): after = lax.ppermute(early, 'tm', backward)  3.62 us
    ppermute x1, starting transfers between devices, body(): far_after = lax.ppermute(early_far, 'tm', backward)  3.6 us
    slice x3, local copies, waits for them, and re-layouts, third(): return lax.slice_in_dim(whole, which * span, (which + 1) * span, axis=2)  3.44 us
    pallas_call x1, Pallas kernels, middle_frames_call(): pl.pallas_call(functools.partial(middle_kernel, frames, near, far), out_s...  3.13 us
    ppermute x1, waiting for transfers between devices, body(): far_after = lax.ppermute(early_far, 'tm', backward)  2.48 us
  transfers between devices with their start and end apart: 4, of which 2 were waited for; matrix products, arithmetic and copies ran while one was open for 1% of the time, Pallas kernels for 6%

profile of v8, /device:TPU:1, one launch (start us, length us, event | category | flops | bytes accessed | tf_op | source)
XLA Modules:
  0.0 117.9 jit_solution(14406714601973988074)
XLA Ops:
  0.0 0.0 copy-start.3
  0.0 0.0 copy-start.4
  0.0 0.0 copy-start.2
  0.0 0.0 copy-start.1
  0.0 1.2 slice.9.early_ref
  1.2 1.1 slice.10.late_ref
  2.3 4.1 %collective-permute-start.3 = (bf16[2,8,20480]{2,1,0:T(8,128)(2,1)S(1)}, bf16[2,8,20480]{2,1,0:T(8,128)(2,1)S(1)}, u32[]{:S(2)}, u32[]{:S(2)}) collective-permute-start(bf16[2,8,20480]{2,1,0:T(8,128)(2,1)S(1)} %slice.10.late_ref), channel_id=1, source_target_pairs={{0,1},{1,2},{2,3},{3,4},{4,5},{5,6},{6,7},{8,9},{9,10},{10,11},{11... | collective-permute-start | bytes 1966088 | tf_op jit(solution)/shard_map/ppermute | solution.py:426
  6.4 3.6 %collective-permute-start.2 = (bf16[2,8,20480]{2,1,0:T(8,128)(2,1)S(1)}, bf16[2,8,20480]{2,1,0:T(8,128)(2,1)S(1)}, u32[]{:S(2)}, u32[]{:S(2)}) collective-permute-start(bf16[2,8,20480]{2,1,0:T(8,128)(2,1)S(1)} %slice.9.early_ref), channel_id=1, source_target_pairs={{0,7},{1,0},{2,1},{3,2},{4,3},{5,4},{6,5},{7,6},{8,15},{9,8},{10,9... | collective-permute-start | bytes 1966088 | tf_op jit(solution)/shard_map/ppermute | solution.py:423
  10.0 1.1 slice.11.between_ref
  11.2 0.0 copy-done.3
  11.2 0.0 copy-done.4
  11.2 0.0 copy-done.2
  11.2 0.0 copy-done.1
  11.2 0.0 copy-start
  11.3 3.8 %own_blocks.1 = (f32[2,32,10,8,128]{4,3,2,1,0:T(8,128)S(1)}, f32[2,32,5,8,128]{4,3,2,1,0:T(8,128)S(1)}, f32[16,8,128]{2,1,0:T(8,128)S(1)}, f32[16,4096]{1,0:T(8,...) custom-call(bf16[2,8,20480]{2,1,0:T(8,128)(2,1)S(1)} %slice.9.early_ref, ...), custom_call_target="tpu_custom_call" | custom-call | flops 3000000000 | bytes 6291456 | tf_op jit(solution)/shard_map/own_blocks/pallas_call | solution.py:291
  15.0 1.7 %collective-permute-start.1 = (bf16[2,8,12288]{2,1,0:T(8,128)(2,1)S(1)}, bf16[2,8,12288]{2,1,0:T(8,128)(2,1)S(1)}, u32[]{:S(2)}, u32[]{:S(2)}) collective-permute-start(bf16[2,8,12288]{2,1,0:T(8,128)(2,1)S(1)} %get-tuple-element.24), channel_id=1, source_target_pairs={{0,1},{1,2},{2,3},{3,4},{4,5},{5,6},{6,7},{8,9},{9,10},{10,11},{11... | collective-permute-start | bytes 1179656 | tf_op jit(solution)/shard_map/ppermute | solution.py:437
  16.7 3.6 %collective-permute-start = (bf16[2,8,8192]{2,1,0:T(8,128)(2,1)S(1)}, bf16[2,8,8192]{2,1,0:T(8,128)(2,1)S(1)}, u32[]{:S(2)}, u32[]{:S(2)}) collective-permute-start(bf16[2,8,8192]{2,1,0:T(8,128)(2,1)S(1)} %get-tuple-element.23), channel_id=1, source_target_pairs={{0,7},{1,0},{2,1},{3,2},{4,3},{5,4},{6,5},{7,6},{8,15},{9,8},{10,9... | collective-permute-start | bytes 786440 | tf_op jit(solution)/shard_map/ppermute | solution.py:436
  20.3 0.0 collective-permute-done.3.before_ref
  20.3 1.6 %collective-permute-done.2.after_ref = bf16[2,8,20480]{2,1,0:T(8,128)(2,1)S(1)} collective-permute-done((bf16[2,8,20480]{2,1,0:T(8,128)(2,1)S(1)}, bf16[2,8,20480]{2,1,0:T(8,128)(2,1)S(1)}, u32[]{:S(2)}, u32[]{:S(2)}) %collective-permute-start.2) | collective-permute-done | bytes 655392 | tf_op jit(solution)/shard_map/ppermute | solution.py:423
  21.9 0.0 copy-done
  21.9 3.1 %middle_frames.1 = (f32[2,16,64,128]{3,2,1,0:T(8,128)S(1)}, f32[2,16,16,128]{3,2,1,0:T(8,128)S(1)}, f32[2,32,5,8,128]{4,3,2,1,0:T(8,128)S(1)}) custom-call(bf16[2,8,20480]{2,1,0:T(8,128)(2,1)S(1)} %collective-permute-done.2.after_ref, bf16[2,8,20480]{2,1,0:T(8,128)(2,1)S(1)} %collective-permute-done.3.before_ref, f32[16,4096]{1,0:T(8,128)S(1)} %get-tuple-element.25.taps_ref, ...), custom_call_target="tpu_custom_call" | custom-call | flops 3000000000 | bytes 5242880 | tf_op jit(solution)/shard_map/middle_frames/pallas_call | solution.py:313
  25.0 2.5 %collective-permute-done.after_ref = bf16[2,8,8192]{2,1,0:T(8,128)(2,1)S(1)} collective-permute-done((bf16[2,8,8192]{2,1,0:T(8,128)(2,1)S(1)}, bf16[2,8,8192]{2,1,0:T(8,128)(2,1)S(1)}, u32[]{:S(2)}, u32[]{:S(2)}) %collective-permute-start) | collective-permute-done | bytes 262176 | tf_op jit(solution)/shard_map/ppermute | solution.py:436
  27.5 0.0 collective-permute-done.1.before_ref
  27.5 2.4 %outer_frames.1 = bf16[128,32,128]{2,1,0:T(8,128)(2,1)S(1)} custom-call(bf16[2,8,8192]{2,1,0:T(8,128)(2,1)S(1)} %collective-permute-done.after_ref, bf16[2,8,12288]{2,1,0:T(8,128)(2,1)S(1)} %collective-permute-done.1.before_ref, f32[16,4096]{1,0:T(8,128)S(1)} %get-tuple-element.25.taps_ref, f32[8,128]{1,0:T(8,128)S(1)} %broadcast_in_dim.3.keep_ref, ...), custom_call_target="tpu_custom_call" | custom-call | tf_op jit(solution)/shard_map/outer_frames/pallas_call | solution.py:331
  29.9 85.7 %all_to_all.5 = bf16[512,8,128]{2,1,0:T(8,128)(2,1)S(1)} all-to-all(bf16[512,8,128]{2,1,0:T(8,128)(2,1)S(1)} %bitcast.3), channel_id=1, replica_groups=mesh['stn'=64,'tm'=8] {'stn','tm'}, dimensions={0} | all-to-all | bytes 2097152 | tf_op jit(solution)/shard_map/all_to_all | solution.py:445
  115.6 2.3 %correlate.1 = bf16[4,512,512]{2,1,0:T(8,128)(2,1)} custom-call(bf16[64,8,8,128]{3,2,1,0:T(8,128)(2,1)S(1)} %bitcast.2), custom_call_target="tpu_custom_call" | custom-call | tf_op jit(solution)/shard_map/correlate/pallas_call | solution.py:397
  (1 shorter events, 0.0 us)
Async XLA Ops:
  0.0 11.2 %copy-start.3 = (f32[2,16,256]{2,1,0:T(8,128)S(1)}, f32[2,16,256]{2,1,0:T(8,128)}, u32[]{:S(2)}) copy-start(f32[2,16,256]{2,1,0:T(8,128)} %constant.21.clone.twist_ref) | copy-start | bytes 98308
  0.0 11.2 %copy-start.4 = (bf16[128,128]{1,0:T(8,128)(2,1)S(1)}, bf16[128,128]{1,0:T(8,128)(2,1)}, u32[]{:S(2)}) copy-start(bf16[128,128]{1,0:T(8,128)(2,1)} %constant.20.clone.order_ref) | copy-start | bytes 98308
  0.0 11.2 %copy-start.2 = (s32[8,2048]{1,0:T(8,128)S(1)}, s32[8,2048]{1,0:T(8,128)}, u32[]{:S(2)}) copy-start(s32[8,2048]{1,0:T(8,128)} %scales_ref.1) | copy-start | bytes 196612
  0.0 11.2 %copy-start.1 = (bf16[16,4096]{1,0:T(8,128)(2,1)S(1)}, bf16[16,4096]{1,0:T(8,128)(2,1)}, u32[]{:S(2)}) copy-start(bf16[16,4096]{1,0:T(8,128)(2,1)} %taps_ref.1) | copy-start | bytes 393220
  2.3 18.0 %collective-permute-start.3 = (bf16[2,8,20480]{2,1,0:T(8,128)(2,1)S(1)}, bf16[2,8,20480]{2,1,0:T(8,128)(2,1)S(1)}, u32[]{:S(2)}, u32[]{:S(2)}) collective-permute-start(bf16[2,8,20480]{2,1,0:T(8,128)(2,1)S(1)} %slice.10.late_ref), channel_id=1, source_target_pairs={{0,1},{1,2},{2,3},{3,4},{4,5},{5,6},{6,7},{8,9},{9,10},{10,11},{11... | collective-permute-start | bytes 1966088 | tf_op jit(solution)/shard_map/ppermute | solution.py:426
  6.4 15.5 %collective-permute-start.2 = (bf16[2,8,20480]{2,1,0:T(8,128)(2,1)S(1)}, bf16[2,8,20480]{2,1,0:T(8,128)(2,1)S(1)}, u32[]{:S(2)}, u32[]{:S(2)}) collective-permute-start(bf16[2,8,20480]{2,1,0:T(8,128)(2,1)S(1)} %slice.9.early_ref), channel_id=1, source_target_pairs={{0,7},{1,0},{2,1},{3,2},{4,3},{5,4},{6,5},{7,6},{8,15},{9,8},{10,9... | collective-permute-start | bytes 1966088 | tf_op jit(solution)/shard_map/ppermute | solution.py:423
  11.2 10.7 %copy-start = (bf16[512,512]{1,0:T(8,128)(2,1)S(1)}, bf16[512,512]{1,0:T(8,128)(2,1)}, u32[]{:S(2)}) copy-start(bf16[512,512]{1,0:T(8,128)(2,1)} %constant.24.table_ref) | copy-start | bytes 1572868
  15.0 12.5 %collective-permute-start.1 = (bf16[2,8,12288]{2,1,0:T(8,128)(2,1)S(1)}, bf16[2,8,12288]{2,1,0:T(8,128)(2,1)S(1)}, u32[]{:S(2)}, u32[]{:S(2)}) collective-permute-start(bf16[2,8,12288]{2,1,0:T(8,128)(2,1)S(1)} %get-tuple-element.24), channel_id=1, source_target_pairs={{0,1},{1,2},{2,3},{3,4},{4,5},{5,6},{6,7},{8,9},{9,10},{10,11},{11... | collective-permute-start | bytes 1179656 | tf_op jit(solution)/shard_map/ppermute | solution.py:437
  16.7 10.8 %collective-permute-start = (bf16[2,8,8192]{2,1,0:T(8,128)(2,1)S(1)}, bf16[2,8,8192]{2,1,0:T(8,128)(2,1)S(1)}, u32[]{:S(2)}, u32[]{:S(2)}) collective-permute-start(bf16[2,8,8192]{2,1,0:T(8,128)(2,1)S(1)} %get-tuple-element.23), channel_id=1, source_target_pairs={{0,7},{1,0},{2,1},{3,2},{4,3},{5,4},{6,5},{7,6},{8,15},{9,8},{10,9... | collective-permute-start | bytes 786440 | tf_op jit(solution)/shard_map/ppermute | solution.py:436

commit v9 on v8

--- a/solution.py
+++ b/solution.py
@@ -203,7 +203,7 @@
 
 
 def middle_kernel(
-    frames, near, far, after_ref, before_ref, taps_ref, keep_ref, twist_ref, table_ref, factor_ref, begun_ref,
+    frames, near, far, before_ref, after_ref, taps_ref, keep_ref, twist_ref, table_ref, factor_ref, begun_ref,
     outer_begun_ref, out_ref, edge_ref, outer_ref, filt, rows,
 ):
     sources = window_of(frames, near, far, (None, before_ref) + (None,) * 3 + (after_ref, None))
@@ -341,6 +341,32 @@
     )(*far_blocks, taps, keep, twist, table, factor, middle, edge, begun)
 
 
+def cut_kernel(spans, in_ref, *refs):
+    outs, sems = refs[:-1], refs[-1]
+    copies = [
+        pltpu.make_async_copy(in_ref.at[:, :, start:stop], out, sems.at[i])
+        for i, ((start, stop), out) in enumerate(zip(spans, outs))
+    ]
+    for copy in copies:
+        copy.start()
+    for copy in copies:
+        copy.wait()
+
+
+def cut_pieces(samples, near, frames, length):
+    spans = [(0, near[1] * length), ((frames - near[0]) * length, frames * length)]
+    early, late = pl.pallas_call(
+        functools.partial(cut_kernel, spans),
+        out_shape=[jax.ShapeDtypeStruct(samples.shape[:2] + (b - a,), samples.dtype) for a, b in spans],
+        in_specs=[pl.BlockSpec(memory_space=pltpu.HBM)],
+        out_specs=[VMEM] * 2,
+        scratch_shapes=[pltpu.SemaphoreType.DMA((2,))],
+        compiler_params=pltpu.CompilerParams(vmem_limit_bytes=VMEM_LIMIT),
+        name="cut",
+    )(pltpu.with_memory_space_constraint(samples, pltpu.HBM))
+    return late, early, lax.slice_in_dim(samples, spans[0][1], spans[1][0], axis=2)
+
+
 def correlate_kernel(normalizer, words_ref, out_ref, joined, swapped, result, sems):
     stations, times, inputs, _ = words_ref.shape
     size = stations * inputs
@@ -415,17 +441,10 @@
     onward = [(i, i + 1) for i in range(times - 1)]
     backward = [(i, (i - 1) % times) for i in range(times)]
 
-    def third(whole, which):
-        span = frames // 3 * length
-        return lax.slice_in_dim(whole, which * span, (which + 1) * span, axis=2)
-
-    early = third(samples, 0)
+    late, early, between = cut_pieces(samples, near, frames, length)
+    before = lax.ppermute(late, "tm", onward)
     after = lax.ppermute(early, "tm", backward)
-    later, early = lax.optimization_barrier((samples, early))
-    late = third(later, 2)
-    before = lax.ppermute(late, "tm", onward)
-    latest, late = lax.optimization_barrier((later, late))
-    pieces = (early, third(latest, 1), late)
+    pieces = (early, between, late)
     keep = jnp.where(lax.axis_index("tm") == times - 1, 0.0, 1.0)
     keep = jnp.broadcast_to(keep.astype(jnp.float32), (inputs, LANES))
     table = split_table()
@@ -436,7 +455,7 @@
     far_after = lax.ppermute(early_far, "tm", backward)
     far_before = lax.ppermute(late_far, "tm", onward)
     middle, edge, outer_begun = middle_frames_call(
-        (after, before), wide_taps, keep, twist, table, factor, begun, outer_begun, frames, near, far
+        (before, after), wide_taps, keep, twist, table, factor, begun, outer_begun, frames, near, far
     )
     words = outer_frames_call(
         (far_after, far_before), wide_taps, keep, twist, table, factor, middle, edge, outer_begun, frames, near, far

time: 118 us -> 120 us (1.017)
  local copies, waits for them, and re-layouts: 3.46 us -> 1.16 us
  blocking collectives: 85.7 us -> 88 us
  waiting for transfers between devices: 4.03 us -> 5.91 us
  starting transfers between devices: 13 us -> 11.4 us
  Pallas kernels: 11.6 us -> 12.9 us
    ppermute x1, starting transfers between devices: 3.62 us -> 6.4 us  [body(): after = lax.ppermute(early, 'tm', backward)]
    ppermute x1, starting transfers between devices: 4.07 us -> 1.33 us  [body(): before = lax.ppermute(late, 'tm', onward)]
    slice x3 -> x1, local copies, waits for them, and re-layouts: 3.44 us -> 1.13 us  [cut_pieces(): lax.slice_in_dim(samples, spans[0][1], spans[1][0], axis=2)]
    all_to_all x1, blocking collectives: 85.7 us -> 88 us  [body(): lax.all_to_all(words, ('stn', 'tm'), split_axis=0, concat_axis=0, tiled=T...]
    ppermute x1, starting transfers between devices: 3.6 us -> 2.02 us  [body(): far_after = lax.ppermute(early_far, 'tm', backward)]
    ppermute x1, waiting for transfers between devices: 0.01 us -> 1.48 us  [body(): far_before = lax.ppermute(late_far, 'tm', onward)]
    pallas_call x0 -> x1, Pallas kernels: none -> 1.35 us  [cut_pieces(): pl.pallas_call(functools.partial(cut_kernel, spans), out_shape=[jax.Shape...]
  transfers between devices with their start and end apart: 4 -> 4, of which waited for: 2 -> 3; matrix products, arithmetic and copies ran while one was open for 1% -> 1% of each run, Pallas kernels for 6% -> 6%
where the time goes in v9:
time: 120 us; the launch traced here: 119 us
  blocking collectives  88 us (73%)
  Pallas kernels  12.9 us (11%)
  starting transfers between devices  11.4 us (10%)
  waiting for transfers between devices  5.91 us (5%)
    all_to_all x1, blocking collectives, body(): lax.all_to_all(words, ('stn', 'tm'), split_axis=0, concat_axis=0, tiled=T...  88 us
    ppermute x1, starting transfers between devices, body(): after = lax.ppermute(early, 'tm', backward)  6.4 us
    pallas_call x1, Pallas kernels, own_blocks_call(): pl.pallas_call(functools.partial(own_kernel, frames, near, far, rescale),...  3.78 us
    pallas_call x1, Pallas kernels, middle_frames_call(): pl.pallas_call(functools.partial(middle_kernel, frames, near, far), out_s...  3.11 us
    ppermute x1, waiting for transfers between devices, body(): far_after = lax.ppermute(early_far, 'tm', backward)  2.5 us
  transfers between devices with their start and end apart: 4, of which 3 were waited for; matrix products, arithmetic and copies ran while one was open for 1% of the time, Pallas kernels for 6%

profile of v9, /device:TPU:1, one launch (start us, length us, event | category | flops | bytes accessed | tf_op | source)
XLA Modules:
  0.0 119.5 jit_solution(16831834803638156732)
XLA Ops:
  0.0 0.0 copy-start.3
  0.0 0.0 copy-start.4
  0.0 0.0 copy-start.2
  0.0 0.0 copy-start.1
  0.0 1.3 %cut.1 = (bf16[2,8,20480]{2,1,0:T(8,128)(2,1)S(1)}, bf16[2,8,20480]{2,1,0:T(8,128)(2,1)S(1)}) custom-call(bf16[2,8,61440]{2,1,0:T(8,128)(2,1)} %in_ref.1), custom_call_target="tpu_custom_call" | custom-call | tf_op jit(solution)/shard_map/cut/pallas_call | solution.py:358
  1.4 6.4 %collective-permute-start.3 = (bf16[2,8,20480]{2,1,0:T(8,128)(2,1)S(1)}, bf16[2,8,20480]{2,1,0:T(8,128)(2,1)S(1)}, u32[]{:S(2)}, u32[]{:S(2)}) collective-permute-start(bf16[2,8,20480]{2,1,0:T(8,128)(2,1)S(1)} %get-tuple-element.17.early_ref), channel_id=1, source_target_pairs={{0,7},{1,0},{2,1},{3,2},{4,3},{5,4},{6,5},{7,6},{8,15},{9,8},{10,9... | collective-permute-start | bytes 1966088 | tf_op jit(solution)/shard_map/ppermute | solution.py:446
  7.8 1.3 %collective-permute-start.2 = (bf16[2,8,20480]{2,1,0:T(8,128)(2,1)S(1)}, bf16[2,8,20480]{2,1,0:T(8,128)(2,1)S(1)}, u32[]{:S(2)}, u32[]{:S(2)}) collective-permute-start(bf16[2,8,20480]{2,1,0:T(8,128)(2,1)S(1)} %get-tuple-element.18.late_ref), channel_id=1, source_target_pairs={{0,1},{1,2},{2,3},{3,4},{4,5},{5,6},{6,7},{8,9},{9,10},{10,11},{11... | collective-permute-start | bytes 1966088 | tf_op jit(solution)/shard_map/ppermute | solution.py:445
  9.1 1.1 slice.3.between_ref
  10.3 0.0 copy-done.3
  10.3 0.0 copy-done.4
  10.3 0.0 copy-done.2
  10.3 0.0 copy-done.1
  10.3 0.0 copy-start
  10.3 3.8 %own_blocks.1 = (f32[2,32,10,8,128]{4,3,2,1,0:T(8,128)S(1)}, f32[2,32,5,8,128]{4,3,2,1,0:T(8,128)S(1)}, f32[16,8,128]{2,1,0:T(8,128)S(1)}, f32[16,4096]{1,0:T(8,...) custom-call(bf16[2,8,20480]{2,1,0:T(8,128)(2,1)S(1)} %get-tuple-element.17.ea, ...), custom_call_target="tpu_custom_call" | custom-call | flops 3000000000 | bytes 6291456 | tf_op jit(solution)/shard_map/own_blocks/pallas_call | solution.py:291
  14.1 1.6 %collective-permute-start.1 = (bf16[2,8,12288]{2,1,0:T(8,128)(2,1)S(1)}, bf16[2,8,12288]{2,1,0:T(8,128)(2,1)S(1)}, u32[]{:S(2)}, u32[]{:S(2)}) collective-permute-start(bf16[2,8,12288]{2,1,0:T(8,128)(2,1)S(1)} %get-tuple-element.20), channel_id=1, source_target_pairs={{0,1},{1,2},{2,3},{3,4},{4,5},{5,6},{6,7},{8,9},{9,10},{10,11},{11... | collective-permute-start | bytes 1179656 | tf_op jit(solution)/shard_map/ppermute | solution.py:456
  15.7 2.0 %collective-permute-start = (bf16[2,8,8192]{2,1,0:T(8,128)(2,1)S(1)}, bf16[2,8,8192]{2,1,0:T(8,128)(2,1)S(1)}, u32[]{:S(2)}, u32[]{:S(2)}) collective-permute-start(bf16[2,8,8192]{2,1,0:T(8,128)(2,1)S(1)} %get-tuple-element.19), channel_id=1, source_target_pairs={{0,7},{1,0},{2,1},{3,2},{4,3},{5,4},{6,5},{7,6},{8,15},{9,8},{10,9... | collective-permute-start | bytes 786440 | tf_op jit(solution)/shard_map/ppermute | solution.py:455
  17.8 1.9 %collective-permute-done.3.after_ref = bf16[2,8,20480]{2,1,0:T(8,128)(2,1)S(1)} collective-permute-done((bf16[2,8,20480]{2,1,0:T(8,128)(2,1)S(1)}, bf16[2,8,20480]{2,1,0:T(8,128)(2,1)S(1)}, u32[]{:S(2)}, u32[]{:S(2)}) %collective-permute-start.3) | collective-permute-done | bytes 655392 | tf_op jit(solution)/shard_map/ppermute | solution.py:446
  19.7 0.0 collective-permute-done.2.before_ref
  19.7 0.0 copy-done
  19.7 3.1 %middle_frames.1 = (f32[2,16,64,128]{3,2,1,0:T(8,128)S(1)}, f32[2,16,16,128]{3,2,1,0:T(8,128)S(1)}, f32[2,32,5,8,128]{4,3,2,1,0:T(8,128)S(1)}) custom-call(bf16[2,8,20480]{2,1,0:T(8,128)(2,1)S(1)} %collective-permute-done.2.before_ref, bf16[2,8,20480]{2,1,0:T(8,128)(2,1)S(1)} %collective-permute-done.3.after_ref, f32[16,4096]{1,0:T(8,128)S(1)} %get-tuple-element.21.taps_ref, ...), custom_call_target="tpu_custom_call" | custom-call | flops 3000000000 | bytes 5242880 | tf_op jit(solution)/shard_map/middle_frames/pallas_call | solution.py:313
  22.8 2.5 %collective-permute-done.after_ref = bf16[2,8,8192]{2,1,0:T(8,128)(2,1)S(1)} collective-permute-done((bf16[2,8,8192]{2,1,0:T(8,128)(2,1)S(1)}, bf16[2,8,8192]{2,1,0:T(8,128)(2,1)S(1)}, u32[]{:S(2)}, u32[]{:S(2)}) %collective-permute-start) | collective-permute-done | bytes 262176 | tf_op jit(solution)/shard_map/ppermute | solution.py:455
  25.3 1.5 %collective-permute-done.1.before_ref = bf16[2,8,12288]{2,1,0:T(8,128)(2,1)S(1)} collective-permute-done((bf16[2,8,12288]{2,1,0:T(8,128)(2,1)S(1)}, bf16[2,8,12288]{2,1,0:T(8,128)(2,1)S(1)}, u32[]{:S(2)}, u32[]{:S(2)}) %collective-permute-start.1) | collective-permute-done | bytes 393248 | tf_op jit(solution)/shard_map/ppermute | solution.py:456
  26.8 2.4 %outer_frames.1 = bf16[128,32,128]{2,1,0:T(8,128)(2,1)S(1)} custom-call(bf16[2,8,8192]{2,1,0:T(8,128)(2,1)S(1)} %collective-permute-done.after_ref, bf16[2,8,12288]{2,1,0:T(8,128)(2,1)S(1)} %collective-permute-done.1.before_ref, f32[16,4096]{1,0:T(8,128)S(1)} %get-tuple-element.21.taps_ref, f32[8,128]{1,0:T(8,128)S(1)} %broadcast_in_dim.3.keep_ref, ...), custom_call_target="tpu_custom_call" | custom-call | tf_op jit(solution)/shard_map/outer_frames/pallas_call | solution.py:331
  29.2 88.0 %all_to_all.5 = bf16[512,8,128]{2,1,0:T(8,128)(2,1)S(1)} all-to-all(bf16[512,8,128]{2,1,0:T(8,128)(2,1)S(1)} %bitcast.3), channel_id=1, replica_groups=mesh['stn'=64,'tm'=8] {'stn','tm'}, dimensions={0} | all-to-all | bytes 2097152 | tf_op jit(solution)/shard_map/all_to_all | solution.py:464
  117.2 2.3 %correlate.1 = bf16[4,512,512]{2,1,0:T(8,128)(2,1)} custom-call(bf16[64,8,8,128]{3,2,1,0:T(8,128)(2,1)S(1)} %bitcast.2), custom_call_target="tpu_custom_call" | custom-call | tf_op jit(solution)/shard_map/correlate/pallas_call | solution.py:423
  (1 shorter events, 0.0 us)
Async XLA Ops:
  0.0 10.3 %copy-start.3 = (f32[2,16,256]{2,1,0:T(8,128)S(1)}, f32[2,16,256]{2,1,0:T(8,128)}, u32[]{:S(2)}) copy-start(f32[2,16,256]{2,1,0:T(8,128)} %constant.21.clone.twist_ref) | copy-start | bytes 98308
  0.0 10.3 %copy-start.4 = (bf16[128,128]{1,0:T(8,128)(2,1)S(1)}, bf16[128,128]{1,0:T(8,128)(2,1)}, u32[]{:S(2)}) copy-start(bf16[128,128]{1,0:T(8,128)(2,1)} %constant.20.clone.order_ref) | copy-start | bytes 98308
  0.0 10.3 %copy-start.2 = (s32[8,2048]{1,0:T(8,128)S(1)}, s32[8,2048]{1,0:T(8,128)}, u32[]{:S(2)}) copy-start(s32[8,2048]{1,0:T(8,128)} %scales_ref.1) | copy-start | bytes 196612
  0.0 10.3 %copy-start.1 = (bf16[16,4096]{1,0:T(8,128)(2,1)S(1)}, bf16[16,4096]{1,0:T(8,128)(2,1)}, u32[]{:S(2)}) copy-start(bf16[16,4096]{1,0:T(8,128)(2,1)} %taps_ref.1) | copy-start | bytes 393220
  1.4 18.3 %collective-permute-start.3 = (bf16[2,8,20480]{2,1,0:T(8,128)(2,1)S(1)}, bf16[2,8,20480]{2,1,0:T(8,128)(2,1)S(1)}, u32[]{:S(2)}, u32[]{:S(2)}) collective-permute-start(bf16[2,8,20480]{2,1,0:T(8,128)(2,1)S(1)} %get-tuple-element.17.early_ref), channel_id=1, source_target_pairs={{0,7},{1,0},{2,1},{3,2},{4,3},{5,4},{6,5},{7,6},{8,15},{9,8},{10,9... | collective-permute-start | bytes 1966088 | tf_op jit(solution)/shard_map/ppermute | solution.py:446
  7.8 11.9 %collective-permute-start.2 = (bf16[2,8,20480]{2,1,0:T(8,128)(2,1)S(1)}, bf16[2,8,20480]{2,1,0:T(8,128)(2,1)S(1)}, u32[]{:S(2)}, u32[]{:S(2)}) collective-permute-start(bf16[2,8,20480]{2,1,0:T(8,128)(2,1)S(1)} %get-tuple-element.18.late_ref), channel_id=1, source_target_pairs={{0,1},{1,2},{2,3},{3,4},{4,5},{5,6},{6,7},{8,9},{9,10},{10,11},{11... | collective-permute-start | bytes 1966088 | tf_op jit(solution)/shard_map/ppermute | solution.py:445
  10.3 9.4 %copy-start = (bf16[512,512]{1,0:T(8,128)(2,1)S(1)}, bf16[512,512]{1,0:T(8,128)(2,1)}, u32[]{:S(2)}) copy-start(bf16[512,512]{1,0:T(8,128)(2,1)} %constant.24.table_ref) | copy-start | bytes 1572868
  14.1 12.7 %collective-permute-start.1 = (bf16[2,8,12288]{2,1,0:T(8,128)(2,1)S(1)}, bf16[2,8,12288]{2,1,0:T(8,128)(2,1)S(1)}, u32[]{:S(2)}, u32[]{:S(2)}) collective-permute-start(bf16[2,8,12288]{2,1,0:T(8,128)(2,1)S(1)} %get-tuple-element.20), channel_id=1, source_target_pairs={{0,1},{1,2},{2,3},{3,4},{4,5},{5,6},{6,7},{8,9},{9,10},{10,11},{11... | collective-permute-start | bytes 1179656 | tf_op jit(solution)/shard_map/ppermute | solution.py:456
  15.7 9.6 %collective-permute-start = (bf16[2,8,8192]{2,1,0:T(8,128)(2,1)S(1)}, bf16[2,8,8192]{2,1,0:T(8,128)(2,1)S(1)}, u32[]{:S(2)}, u32[]{:S(2)}) collective-permute-start(bf16[2,8,8192]{2,1,0:T(8,128)(2,1)S(1)} %get-tuple-element.19), channel_id=1, source_target_pairs={{0,7},{1,0},{2,1},{3,2},{4,3},{5,4},{6,5},{7,6},{8,15},{9,8},{10,9... | collective-permute-start | bytes 786440 | tf_op jit(solution)/shard_map/ppermute | solution.py:455

commit v10 on v9

--- a/solution.py
+++ b/solution.py
@@ -167,7 +167,7 @@
 
 
 def own_kernel(
-    frames, near, far, rescale, early_ref, between_ref, late_ref, taps_ref, keep_ref, scales_ref, order_ref, twist_ref,
+    frames, near, far, rescale, late_ref, between_ref, early_ref, taps_ref, keep_ref, scales_ref, order_ref, twist_ref,
     middle_ref, outer_ref, factor_ref, wide_taps_ref, same_twist_ref, early_far_ref, late_far_ref,
 ):
     inputs = scales_ref.shape[0]
@@ -354,8 +354,8 @@
 
 
 def cut_pieces(samples, near, frames, length):
-    spans = [(0, near[1] * length), ((frames - near[0]) * length, frames * length)]
-    early, late = pl.pallas_call(
+    spans = [((frames - near[0]) * length, frames * length), (0, near[1] * length)]
+    late, early = pl.pallas_call(
         functools.partial(cut_kernel, spans),
         out_shape=[jax.ShapeDtypeStruct(samples.shape[:2] + (b - a,), samples.dtype) for a, b in spans],
         in_specs=[pl.BlockSpec(memory_space=pltpu.HBM)],
@@ -364,7 +364,7 @@
         compiler_params=pltpu.CompilerParams(vmem_limit_bytes=VMEM_LIMIT),
         name="cut",
     )(pltpu.with_memory_space_constraint(samples, pltpu.HBM))
-    return late, early, lax.slice_in_dim(samples, spans[0][1], spans[1][0], axis=2)
+    return late, early, lax.slice_in_dim(samples, spans[1][1], spans[0][0], axis=2)
 
 
 def correlate_kernel(normalizer, words_ref, out_ref, joined, swapped, result, sems):
@@ -444,7 +444,7 @@
     late, early, between = cut_pieces(samples, near, frames, length)
     before = lax.ppermute(late, "tm", onward)
     after = lax.ppermute(early, "tm", backward)
-    pieces = (early, between, late)
+    pieces = (late, between, early)
     keep = jnp.where(lax.axis_index("tm") == times - 1, 0.0, 1.0)
     keep = jnp.broadcast_to(keep.astype(jnp.float32), (inputs, LANES))
     table = split_table()

time: 120 us -> 117 us (0.975)
  blocking collectives: 88 us -> 85.7 us
  waiting for transfers between devices: 5.91 us -> 4.06 us
  starting transfers between devices: 11.4 us -> 13 us
    ppermute x1, starting transfers between devices: 6.4 us -> 3.62 us  [body(): after = lax.ppermute(early, 'tm', backward)]
    ppermute x1, starting transfers between devices: 1.33 us -> 4.07 us  [body(): before = lax.ppermute(late, 'tm', onward)]
    all_to_all x1, blocking collectives: 88 us -> 85.7 us  [body(): lax.all_to_all(words, ('stn', 'tm'), split_axis=0, concat_axis=0, tiled=T...]
    ppermute x1, starting transfers between devices: 2.02 us -> 3.6 us  [body(): far_after = lax.ppermute(early_far, 'tm', backward)]
    ppermute x1, waiting for transfers between devices: 1.48 us -> 0.01 us  [body(): far_before = lax.ppermute(late_far, 'tm', onward)]
  transfers between devices with their start and end apart: 4 -> 4, of which waited for: 3 -> 2; matrix products, arithmetic and copies ran while one was open for 1% -> 1% of each run, Pallas kernels for 6% -> 6%
where the time goes in v10:
time: 117 us
  blocking collectives  85.7 us (73%)
  starting transfers between devices  13 us (11%)
  Pallas kernels  12.9 us (11%)
  waiting for transfers between devices  4.06 us (3%)
    all_to_all x1, blocking collectives, body(): lax.all_to_all(words, ('stn', 'tm'), split_axis=0, concat_axis=0, tiled=T...  85.7 us
    ppermute x1, starting transfers between devices, body(): before = lax.ppermute(late, 'tm', onward)  4.07 us
    pallas_call x1, Pallas kernels, own_blocks_call(): pl.pallas_call(functools.partial(own_kernel, frames, near, far, rescale),...  3.78 us
    ppermute x1, starting transfers between devices, body(): after = lax.ppermute(early, 'tm', backward)  3.62 us
    ppermute x1, starting transfers between devices, body(): far_after = lax.ppermute(early_far, 'tm', backward)  3.6 us
    pallas_call x1, Pallas kernels, middle_frames_call(): pl.pallas_call(functools.partial(middle_kernel, frames, near, far), out_s...  3.11 us
    ppermute x1, waiting for transfers between devices, body(): far_after = lax.ppermute(early_far, 'tm', backward)  2.5 us
    pallas_call x1, Pallas kernels, outer_frames_call(): pl.pallas_call(functools.partial(outer_kernel, frames, near, far), out_sh...  2.37 us
  transfers between devices with their start and end apart: 4, of which 2 were waited for; matrix products, arithmetic and copies ran while one was open for 1% of the time, Pallas kernels for 6%

profile of v10, /device:TPU:1, one launch (start us, length us, event | category | flops | bytes accessed | tf_op | source)
XLA Modules:
  0.0 117.0 jit_solution(10138699889054143552)
XLA Ops:
  0.0 0.0 copy-start.3
  0.0 0.0 copy-start.4
  0.0 0.0 copy-start.2
  0.0 0.0 copy-start.1
  0.0 1.3 %cut.1 = (bf16[2,8,20480]{2,1,0:T(8,128)(2,1)S(1)}, bf16[2,8,20480]{2,1,0:T(8,128)(2,1)S(1)}) custom-call(bf16[2,8,61440]{2,1,0:T(8,128)(2,1)} %in_ref.1), custom_call_target="tpu_custom_call" | custom-call | tf_op jit(solution)/shard_map/cut/pallas_call | solution.py:358
  1.4 4.1 %collective-permute-start.2 = (bf16[2,8,20480]{2,1,0:T(8,128)(2,1)S(1)}, bf16[2,8,20480]{2,1,0:T(8,128)(2,1)S(1)}, u32[]{:S(2)}, u32[]{:S(2)}) collective-permute-start(bf16[2,8,20480]{2,1,0:T(8,128)(2,1)S(1)} %get-tuple-element.17.late_ref), channel_id=1, source_target_pairs={{0,1},{1,2},{2,3},{3,4},{4,5},{5,6},{6,7},{8,9},{9,10},{10,11},{11... | collective-permute-start | bytes 1966088 | tf_op jit(solution)/shard_map/ppermute | solution.py:445
  5.5 3.6 %collective-permute-start.3 = (bf16[2,8,20480]{2,1,0:T(8,128)(2,1)S(1)}, bf16[2,8,20480]{2,1,0:T(8,128)(2,1)S(1)}, u32[]{:S(2)}, u32[]{:S(2)}) collective-permute-start(bf16[2,8,20480]{2,1,0:T(8,128)(2,1)S(1)} %get-tuple-element.18.early_ref), channel_id=1, source_target_pairs={{0,7},{1,0},{2,1},{3,2},{4,3},{5,4},{6,5},{7,6},{8,15},{9,8},{10,9... | collective-permute-start | bytes 1966088 | tf_op jit(solution)/shard_map/ppermute | solution.py:446
  9.1 1.1 slice.3.between_ref
  10.2 0.0 copy-done.3
  10.2 0.0 copy-done.4
  10.3 0.0 copy-done.2
  10.3 0.0 copy-done.1
  10.3 0.0 copy-start
  10.3 3.8 %own_blocks.1 = (f32[2,32,10,8,128]{4,3,2,1,0:T(8,128)S(1)}, f32[2,32,5,8,128]{4,3,2,1,0:T(8,128)S(1)}, f32[16,8,128]{2,1,0:T(8,128)S(1)}, f32[16,4096]{1,0:T(8,...) custom-call(bf16[2,8,20480]{2,1,0:T(8,128)(2,1)S(1)} %get-tuple-element.17.la, ...), custom_call_target="tpu_custom_call" | custom-call | flops 3000000000 | bytes 6291456 | tf_op jit(solution)/shard_map/own_blocks/pallas_call | solution.py:291
  14.1 1.7 %collective-permute-start.1 = (bf16[2,8,12288]{2,1,0:T(8,128)(2,1)S(1)}, bf16[2,8,12288]{2,1,0:T(8,128)(2,1)S(1)}, u32[]{:S(2)}, u32[]{:S(2)}) collective-permute-start(bf16[2,8,12288]{2,1,0:T(8,128)(2,1)S(1)} %get-tuple-element.20), channel_id=1, source_target_pairs={{0,1},{1,2},{2,3},{3,4},{4,5},{5,6},{6,7},{8,9},{9,10},{10,11},{11... | collective-permute-start | bytes 1179656 | tf_op jit(solution)/shard_map/ppermute | solution.py:456
  15.8 3.6 %collective-permute-start = (bf16[2,8,8192]{2,1,0:T(8,128)(2,1)S(1)}, bf16[2,8,8192]{2,1,0:T(8,128)(2,1)S(1)}, u32[]{:S(2)}, u32[]{:S(2)}) collective-permute-start(bf16[2,8,8192]{2,1,0:T(8,128)(2,1)S(1)} %get-tuple-element.19), channel_id=1, source_target_pairs={{0,7},{1,0},{2,1},{3,2},{4,3},{5,4},{6,5},{7,6},{8,15},{9,8},{10,9... | collective-permute-start | bytes 786440 | tf_op jit(solution)/shard_map/ppermute | solution.py:455
  19.4 0.0 collective-permute-done.2.before_ref
  19.4 1.6 %collective-permute-done.3.after_ref = bf16[2,8,20480]{2,1,0:T(8,128)(2,1)S(1)} collective-permute-done((bf16[2,8,20480]{2,1,0:T(8,128)(2,1)S(1)}, bf16[2,8,20480]{2,1,0:T(8,128)(2,1)S(1)}, u32[]{:S(2)}, u32[]{:S(2)}) %collective-permute-start.3) | collective-permute-done | bytes 655392 | tf_op jit(solution)/shard_map/ppermute | solution.py:446
  20.9 0.0 copy-done
  20.9 3.1 %middle_frames.1 = (f32[2,16,64,128]{3,2,1,0:T(8,128)S(1)}, f32[2,16,16,128]{3,2,1,0:T(8,128)S(1)}, f32[2,32,5,8,128]{4,3,2,1,0:T(8,128)S(1)}) custom-call(bf16[2,8,20480]{2,1,0:T(8,128)(2,1)S(1)} %collective-permute-done.2.before_ref, bf16[2,8,20480]{2,1,0:T(8,128)(2,1)S(1)} %collective-permute-done.3.after_ref, f32[16,4096]{1,0:T(8,128)S(1)} %get-tuple-element.21.taps_ref, ...), custom_call_target="tpu_custom_call" | custom-call | flops 3000000000 | bytes 5242880 | tf_op jit(solution)/shard_map/middle_frames/pallas_call | solution.py:313
  24.1 2.5 %collective-permute-done.after_ref = bf16[2,8,8192]{2,1,0:T(8,128)(2,1)S(1)} collective-permute-done((bf16[2,8,8192]{2,1,0:T(8,128)(2,1)S(1)}, bf16[2,8,8192]{2,1,0:T(8,128)(2,1)S(1)}, u32[]{:S(2)}, u32[]{:S(2)}) %collective-permute-start) | collective-permute-done | bytes 262176 | tf_op jit(solution)/shard_map/ppermute | solution.py:455
  26.6 0.0 collective-permute-done.1.before_ref
  26.6 2.4 %outer_frames.1 = bf16[128,32,128]{2,1,0:T(8,128)(2,1)S(1)} custom-call(bf16[2,8,8192]{2,1,0:T(8,128)(2,1)S(1)} %collective-permute-done.after_ref, bf16[2,8,12288]{2,1,0:T(8,128)(2,1)S(1)} %collective-permute-done.1.before_ref, f32[16,4096]{1,0:T(8,128)S(1)} %get-tuple-element.21.taps_ref, f32[8,128]{1,0:T(8,128)S(1)} %broadcast_in_dim.3.keep_ref, ...), custom_call_target="tpu_custom_call" | custom-call | tf_op jit(solution)/shard_map/outer_frames/pallas_call | solution.py:331
  28.9 85.7 %all_to_all.5 = bf16[512,8,128]{2,1,0:T(8,128)(2,1)S(1)} all-to-all(bf16[512,8,128]{2,1,0:T(8,128)(2,1)S(1)} %bitcast.3), channel_id=1, replica_groups=mesh['stn'=64,'tm'=8] {'stn','tm'}, dimensions={0} | all-to-all | bytes 2097152 | tf_op jit(solution)/shard_map/all_to_all | solution.py:464
  114.7 2.3 %correlate.1 = bf16[4,512,512]{2,1,0:T(8,128)(2,1)} custom-call(bf16[64,8,8,128]{3,2,1,0:T(8,128)(2,1)S(1)} %bitcast.2), custom_call_target="tpu_custom_call" | custom-call | tf_op jit(solution)/shard_map/correlate/pallas_call | solution.py:423
  (1 shorter events, 0.0 us)
Async XLA Ops:
  0.0 10.2 %copy-start.3 = (f32[2,16,256]{2,1,0:T(8,128)S(1)}, f32[2,16,256]{2,1,0:T(8,128)}, u32[]{:S(2)}) copy-start(f32[2,16,256]{2,1,0:T(8,128)} %constant.21.clone.twist_ref) | copy-start | bytes 98308
  0.0 10.2 %copy-start.4 = (bf16[128,128]{1,0:T(8,128)(2,1)S(1)}, bf16[128,128]{1,0:T(8,128)(2,1)}, u32[]{:S(2)}) copy-start(bf16[128,128]{1,0:T(8,128)(2,1)} %constant.20.clone.order_ref) | copy-start | bytes 98308
  0.0 10.3 %copy-start.2 = (s32[8,2048]{1,0:T(8,128)S(1)}, s32[8,2048]{1,0:T(8,128)}, u32[]{:S(2)}) copy-start(s32[8,2048]{1,0:T(8,128)} %scales_ref.1) | copy-start | bytes 196612
  0.0 10.3 %copy-start.1 = (bf16[16,4096]{1,0:T(8,128)(2,1)S(1)}, bf16[16,4096]{1,0:T(8,128)(2,1)}, u32[]{:S(2)}) copy-start(bf16[16,4096]{1,0:T(8,128)(2,1)} %taps_ref.1) | copy-start | bytes 393220
  1.4 18.0 %collective-permute-start.2 = (bf16[2,8,20480]{2,1,0:T(8,128)(2,1)S(1)}, bf16[2,8,20480]{2,1,0:T(8,128)(2,1)S(1)}, u32[]{:S(2)}, u32[]{:S(2)}) collective-permute-start(bf16[2,8,20480]{2,1,0:T(8,128)(2,1)S(1)} %get-tuple-element.17.late_ref), channel_id=1, source_target_pairs={{0,1},{1,2},{2,3},{3,4},{4,5},{5,6},{6,7},{8,9},{9,10},{10,11},{11... | collective-permute-start | bytes 1966088 | tf_op jit(solution)/shard_map/ppermute | solution.py:445
  5.5 15.5 %collective-permute-start.3 = (bf16[2,8,20480]{2,1,0:T(8,128)(2,1)S(1)}, bf16[2,8,20480]{2,1,0:T(8,128)(2,1)S(1)}, u32[]{:S(2)}, u32[]{:S(2)}) collective-permute-start(bf16[2,8,20480]{2,1,0:T(8,128)(2,1)S(1)} %get-tuple-element.18.early_ref), channel_id=1, source_target_pairs={{0,7},{1,0},{2,1},{3,2},{4,3},{5,4},{6,5},{7,6},{8,15},{9,8},{10,9... | collective-permute-start | bytes 1966088 | tf_op jit(solution)/shard_map/ppermute | solution.py:446
  10.3 10.7 %copy-start = (bf16[512,512]{1,0:T(8,128)(2,1)S(1)}, bf16[512,512]{1,0:T(8,128)(2,1)}, u32[]{:S(2)}) copy-start(bf16[512,512]{1,0:T(8,128)(2,1)} %constant.24.table_ref) | copy-start | bytes 1572868
  14.1 12.5 %collective-permute-start.1 = (bf16[2,8,12288]{2,1,0:T(8,128)(2,1)S(1)}, bf16[2,8,12288]{2,1,0:T(8,128)(2,1)S(1)}, u32[]{:S(2)}, u32[]{:S(2)}) collective-permute-start(bf16[2,8,12288]{2,1,0:T(8,128)(2,1)S(1)} %get-tuple-element.20), channel_id=1, source_target_pairs={{0,1},{1,2},{2,3},{3,4},{4,5},{5,6},{6,7},{8,9},{9,10},{10,11},{11... | collective-permute-start | bytes 1179656 | tf_op jit(solution)/shard_map/ppermute | solution.py:456
  15.8 10.8 %collective-permute-start = (bf16[2,8,8192]{2,1,0:T(8,128)(2,1)S(1)}, bf16[2,8,8192]{2,1,0:T(8,128)(2,1)S(1)}, u32[]{:S(2)}, u32[]{:S(2)}) collective-permute-start(bf16[2,8,8192]{2,1,0:T(8,128)(2,1)S(1)} %get-tuple-element.19), channel_id=1, source_target_pairs={{0,7},{1,0},{2,1},{3,2},{4,3},{5,4},{6,5},{7,6},{8,15},{9,8},{10,9... | collective-permute-start | bytes 786440 | tf_op jit(solution)/shard_map/ppermute | solution.py:455

commit v11 on v10

--- a/solution.py
+++ b/solution.py
@@ -437,7 +437,7 @@
     inputs = samples.shape[1]
     frames = samples.shape[2] // length
     stations, times = lax.axis_size("stn"), lax.axis_size("tm")
-    near, far = (5, 5), (3, 2)
+    near, far = (6, 5), (2, 2)
     onward = [(i, i + 1) for i in range(times - 1)]
     backward = [(i, (i - 1) % times) for i in range(times)]
 

time: 117 us -> 117 us (level)
  waiting for transfers between devices: 4.06 us -> 1.6 us
  local copies, waits for them, and re-layouts: 1.16 us -> 3.44 us
    unnamed x10, local copies, waits for them, and re-layouts: 0.02 us -> 2.36 us
    ppermute x1, waiting for transfers between devices: 1.55 us -> 0.01 us  [body(): after = lax.ppermute(early, 'tm', backward)]
  transfers between devices with their start and end apart: 4 -> 4, of which waited for: 2 -> 1; matrix products, arithmetic and copies ran while one was open for 1% -> 1% of each run, Pallas kernels for 6% -> 6%
where the time goes in v11:
time: 117 us
  blocking collectives  85.7 us (73%)
  starting transfers between devices  13 us (11%)
  Pallas kernels  12.9 us (11%)
  local copies, waits for them, and re-layouts  3.44 us (3%)
  waiting for transfers between devices  1.6 us (1%)
    all_to_all x1, blocking collectives, body(): lax.all_to_all(words, ('stn', 'tm'), split_axis=0, concat_axis=0, tiled=T...  85.7 us
    ppermute x1, starting transfers between devices, body(): before = lax.ppermute(late, 'tm', onward)  4.08 us
    ppermute x1, starting transfers between devices, body(): far_after = lax.ppermute(early_far, 'tm', backward)  3.99 us
    pallas_call x1, Pallas kernels, own_blocks_call(): pl.pallas_call(functools.partial(own_kernel, frames, near, far, rescale),...  3.78 us
    ppermute x1, starting transfers between devices, body(): after = lax.ppermute(early, 'tm', backward)  3.61 us
    pallas_call x1, Pallas kernels, middle_frames_call(): pl.pallas_call(functools.partial(middle_kernel, frames, near, far), out_s...  3.34 us
    unnamed x10, local copies, waits for them, and re-layouts  2.36 us
  transfers between devices with their start and end apart: 4, of which 1 were waited for; matrix products, arithmetic and copies ran while one was open for 1% of the time, Pallas kernels for 6%

profile of v11, /device:TPU:1, one launch (start us, length us, event | category | flops | bytes accessed | tf_op | source)
XLA Modules:
  0.0 116.7 jit_solution(14068871127878234778)
XLA Ops:
  0.0 0.0 copy-start.1
  0.0 1.4 %cut.1 = (bf16[2,8,24576]{2,1,0:T(8,128)(2,1)S(1)}, bf16[2,8,20480]{2,1,0:T(8,128)(2,1)S(1)}) custom-call(bf16[2,8,61440]{2,1,0:T(8,128)(2,1)} %in_ref.1), custom_call_target="tpu_custom_call" | custom-call | tf_op jit(solution)/shard_map/cut/pallas_call | solution.py:358
  1.4 4.1 %collective-permute-start.2 = (bf16[2,8,24576]{2,1,0:T(8,128)(2,1)S(1)}, bf16[2,8,24576]{2,1,0:T(8,128)(2,1)S(1)}, u32[]{:S(2)}, u32[]{:S(2)}) collective-permute-start(bf16[2,8,24576]{2,1,0:T(8,128)(2,1)S(1)} %get-tuple-element.17.late_ref), channel_id=1, source_target_pairs={{0,1},{1,2},{2,3},{3,4},{4,5},{5,6},{6,7},{8,9},{9,10},{10,11},{11... | collective-permute-start | bytes 2359304 | tf_op jit(solution)/shard_map/ppermute | solution.py:445
  5.5 3.6 %collective-permute-start.3 = (bf16[2,8,20480]{2,1,0:T(8,128)(2,1)S(1)}, bf16[2,8,20480]{2,1,0:T(8,128)(2,1)S(1)}, u32[]{:S(2)}, u32[]{:S(2)}) collective-permute-start(bf16[2,8,20480]{2,1,0:T(8,128)(2,1)S(1)} %get-tuple-element.18.early_ref), channel_id=1, source_target_pairs={{0,7},{1,0},{2,1},{3,2},{4,3},{5,4},{6,5},{7,6},{8,15},{9,8},{10,9... | collective-permute-start | bytes 1966088 | tf_op jit(solution)/shard_map/ppermute | solution.py:446
  9.1 1.1 slice.3.between_ref
  10.2 0.0 copy-done.1
  10.2 0.0 copy-start.2
  10.2 0.8 copy-done.2
  11.1 0.0 copy-start.3
  11.1 0.8 copy-done.3
  11.8 0.0 copy-start.4
  11.8 0.8 copy-done.4
  12.6 0.0 copy-start
  12.6 3.8 %own_blocks.1 = (f32[2,32,11,8,128]{4,3,2,1,0:T(8,128)S(1)}, f32[2,32,4,8,128]{4,3,2,1,0:T(8,128)S(1)}, f32[16,8,128]{2,1,0:T(8,128)S(1)}, f32[16,4096]{1,0:T(8,...) custom-call(bf16[2,8,24576]{2,1,0:T(8,128)(2,1)S(1)} %get-tuple-element.17.lat, ...), custom_call_target="tpu_custom_call" | custom-call | flops 3000000000 | bytes 6291456 | tf_op jit(solution)/shard_map/own_blocks/pallas_call | solution.py:291
  16.4 4.0 %collective-permute-start = (bf16[2,8,8192]{2,1,0:T(8,128)(2,1)S(1)}, bf16[2,8,8192]{2,1,0:T(8,128)(2,1)S(1)}, u32[]{:S(2)}, u32[]{:S(2)}) collective-permute-start(bf16[2,8,8192]{2,1,0:T(8,128)(2,1)S(1)} %get-tuple-element.19), channel_id=1, source_target_pairs={{0,7},{1,0},{2,1},{3,2},{4,3},{5,4},{6,5},{7,6},{8,15},{9,8},{10,9... | collective-permute-start | bytes 786440 | tf_op jit(solution)/shard_map/ppermute | solution.py:455
  20.4 1.3 %collective-permute-start.1 = (bf16[2,8,8192]{2,1,0:T(8,128)(2,1)S(1)}, bf16[2,8,8192]{2,1,0:T(8,128)(2,1)S(1)}, u32[]{:S(2)}, u32[]{:S(2)}) collective-permute-start(bf16[2,8,8192]{2,1,0:T(8,128)(2,1)S(1)} %get-tuple-element.20), channel_id=1, source_target_pairs={{0,1},{1,2},{2,3},{3,4},{4,5},{5,6},{6,7},{8,9},{9,10},{10,11},{11... | collective-permute-start | bytes 786440 | tf_op jit(solution)/shard_map/ppermute | solution.py:456
  21.7 0.0 collective-permute-done.3.after_ref
  21.7 0.0 collective-permute-done.2.before_ref
  21.7 0.0 copy-done
  21.7 3.3 %middle_frames.1 = (f32[2,16,64,128]{3,2,1,0:T(8,128)S(1)}, f32[2,16,24,128]{3,2,1,0:T(8,128)S(1)}, f32[2,32,4,8,128]{4,3,2,1,0:T(8,128)S(1)}) custom-call(bf16[2,8,24576]{2,1,0:T(8,128)(2,1)S(1)} %collective-permute-done.2.before_ref, bf16[2,8,20480]{2,1,0:T(8,128)(2,1)S(1)} %collective-permute-done.3.after_ref, f32[16,4096]{1,0:T(8,128)S(1)} %get-tuple-element.21.taps_ref, ...), custom_call_target="tpu_custom_call" | custom-call | flops 3000000000 | bytes 5242880 | tf_op jit(solution)/shard_map/middle_frames/pallas_call | solution.py:313
  25.0 1.6 %collective-permute-done.after_ref = bf16[2,8,8192]{2,1,0:T(8,128)(2,1)S(1)} collective-permute-done((bf16[2,8,8192]{2,1,0:T(8,128)(2,1)S(1)}, bf16[2,8,8192]{2,1,0:T(8,128)(2,1)S(1)}, u32[]{:S(2)}, u32[]{:S(2)}) %collective-permute-start) | collective-permute-done | bytes 262176 | tf_op jit(solution)/shard_map/ppermute | solution.py:455
  26.6 0.0 collective-permute-done.1.before_ref
  26.6 2.1 %outer_frames.1 = bf16[128,32,128]{2,1,0:T(8,128)(2,1)S(1)} custom-call(bf16[2,8,8192]{2,1,0:T(8,128)(2,1)S(1)} %collective-permute-done.after_ref, bf16[2,8,8192]{2,1,0:T(8,128)(2,1)S(1)} %collective-permute-done.1.before_ref, f32[16,4096]{1,0:T(8,128)S(1)} %get-tuple-element.21.taps_ref, f32[8,128]{1,0:T(8,128)S(1)} %broadcast_in_dim.3.keep_ref, ...), custom_call_target="tpu_custom_call" | custom-call | tf_op jit(solution)/shard_map/outer_frames/pallas_call | solution.py:331
  28.7 85.7 %all_to_all.5 = bf16[512,8,128]{2,1,0:T(8,128)(2,1)S(1)} all-to-all(bf16[512,8,128]{2,1,0:T(8,128)(2,1)S(1)} %bitcast.3), channel_id=1, replica_groups=mesh['stn'=64,'tm'=8] {'stn','tm'}, dimensions={0} | all-to-all | bytes 2097152 | tf_op jit(solution)/shard_map/all_to_all | solution.py:464
  114.4 2.3 %correlate.1 = bf16[4,512,512]{2,1,0:T(8,128)(2,1)} custom-call(bf16[64,8,8,128]{3,2,1,0:T(8,128)(2,1)S(1)} %bitcast.2), custom_call_target="tpu_custom_call" | custom-call | tf_op jit(solution)/shard_map/correlate/pallas_call | solution.py:423
  (1 shorter events, 0.0 us)
Async XLA Ops:
  0.0 10.2 %copy-start.1 = (bf16[16,4096]{1,0:T(8,128)(2,1)S(1)}, bf16[16,4096]{1,0:T(8,128)(2,1)}, u32[]{:S(2)}) copy-start(bf16[16,4096]{1,0:T(8,128)(2,1)} %taps_ref.1) | copy-start | bytes 393220
  1.4 20.3 %collective-permute-start.2 = (bf16[2,8,24576]{2,1,0:T(8,128)(2,1)S(1)}, bf16[2,8,24576]{2,1,0:T(8,128)(2,1)S(1)}, u32[]{:S(2)}, u32[]{:S(2)}) collective-permute-start(bf16[2,8,24576]{2,1,0:T(8,128)(2,1)S(1)} %get-tuple-element.17.late_ref), channel_id=1, source_target_pairs={{0,1},{1,2},{2,3},{3,4},{4,5},{5,6},{6,7},{8,9},{9,10},{10,11},{11... | collective-permute-start | bytes 2359304 | tf_op jit(solution)/shard_map/ppermute | solution.py:445
  5.5 16.2 %collective-permute-start.3 = (bf16[2,8,20480]{2,1,0:T(8,128)(2,1)S(1)}, bf16[2,8,20480]{2,1,0:T(8,128)(2,1)S(1)}, u32[]{:S(2)}, u32[]{:S(2)}) collective-permute-start(bf16[2,8,20480]{2,1,0:T(8,128)(2,1)S(1)} %get-tuple-element.18.early_ref), channel_id=1, source_target_pairs={{0,7},{1,0},{2,1},{3,2},{4,3},{5,4},{6,5},{7,6},{8,15},{9,8},{10,9... | collective-permute-start | bytes 1966088 | tf_op jit(solution)/shard_map/ppermute | solution.py:446
  10.2 0.8 copy-start.2
  11.1 0.8 copy-start.3
  11.8 0.8 copy-start.4
  12.6 9.1 %copy-start = (bf16[512,512]{1,0:T(8,128)(2,1)S(1)}, bf16[512,512]{1,0:T(8,128)(2,1)}, u32[]{:S(2)}) copy-start(bf16[512,512]{1,0:T(8,128)(2,1)} %constant.24.table_ref) | copy-start | bytes 1572868
  16.4 10.3 %collective-permute-start = (bf16[2,8,8192]{2,1,0:T(8,128)(2,1)S(1)}, bf16[2,8,8192]{2,1,0:T(8,128)(2,1)S(1)}, u32[]{:S(2)}, u32[]{:S(2)}) collective-permute-start(bf16[2,8,8192]{2,1,0:T(8,128)(2,1)S(1)} %get-tuple-element.19), channel_id=1, source_target_pairs={{0,7},{1,0},{2,1},{3,2},{4,3},{5,4},{6,5},{7,6},{8,15},{9,8},{10,9... | collective-permute-start | bytes 786440 | tf_op jit(solution)/shard_map/ppermute | solution.py:455
  20.4 6.3 %collective-permute-start.1 = (bf16[2,8,8192]{2,1,0:T(8,128)(2,1)S(1)}, bf16[2,8,8192]{2,1,0:T(8,128)(2,1)S(1)}, u32[]{:S(2)}, u32[]{:S(2)}) collective-permute-start(bf16[2,8,8192]{2,1,0:T(8,128)(2,1)S(1)} %get-tuple-element.20), channel_id=1, source_target_pairs={{0,1},{1,2},{2,3},{3,4},{4,5},{5,6},{6,7},{8,9},{9,10},{10,11},{11... | collective-permute-start | bytes 786440 | tf_op jit(solution)/shard_map/ppermute | solution.py:456
